TPU v7x, 32 devices: a whole 2x2x4 slice. The times are simulated.
32 devices in a mesh: dp: 16 (over z, y, core), tensor: 2 (over x).
Axes of the slice: x: 2, y: 2, z: 4, core: 2. Of those that a mesh axis runs over, the one named last changes fastest.
Arguments:
- block_input: bfloat16 [4096, 2560], P(('dp', 'tensor')), may hold values from -6 to 6
- starts: int32 [4096], P('dp'), may hold values from 0 to 1, as said below
- cotangent: bfloat16 [4096, 2560], P(('dp', 'tensor')), may hold values from -6 to 6
- gain_mixer: bfloat16 [2560], P('dp'), may hold values from 0.5 to 1.5
- w_branch: bfloat16 [2560, 2560], P(None, ('tensor', 'dp')), may hold values from -0.125 to 0.125
- w_signal: bfloat16 [2560, 2560], P(None, ('tensor', 'dp')), may hold values from -0.125 to 0.125
- w_input_gate: bfloat16 [10, 256, 256], P('tensor', 'dp'), may hold values from -0.375 to 0.375
- w_decay_gate: bfloat16 [10, 256, 256], P('tensor', 'dp'), may hold values from -0.375 to 0.375
- conv_taps: bfloat16 [2560, 4], P(('tensor', 'dp')), may hold values from -3 to 3
- decay_param: bfloat16 [2560], P(('tensor', 'dp')), may hold values from -9 to -2
- w_mixout: bfloat16 [2560, 2560], P(('tensor', 'dp')), may hold values from -0.5 to 0.5
- gain_dense: bfloat16 [2560], P('dp'), may hold values from 0.5 to 1.5
- w_gate: bfloat16 [2560, 7680], P(None, ('tensor', 'dp')), may hold values from -0.125 to 0.125
- w_up: bfloat16 [2560, 7680], P(None, ('tensor', 'dp')), may hold values from -0.125 to 0.125
- w_down: bfloat16 [7680, 2560], P(('tensor', 'dp')), may hold values from -0.125 to 0.125
Outputs:
- block_output: bfloat16 [4096, 2560], P(('dp', 'tensor'))
- grad_input: float32 [4096, 2560], P(('dp', 'tensor'))
- grad_gain_mixer: float32 [2560], P('dp')
- grad_w_branch: float32 [2560, 2560], P(None, ('tensor', 'dp'))
- grad_w_signal: float32 [2560, 2560], P(None, ('tensor', 'dp'))
- grad_input_gate: float32 [10, 256, 256], P('tensor', 'dp')
- grad_decay_gate: float32 [10, 256, 256], P('tensor', 'dp')
- grad_conv_taps: float32 [2560, 4], P(('tensor', 'dp'))
- grad_decay_param: float32 [2560], P(('tensor', 'dp'))
- grad_w_mixout: float32 [2560, 2560], P(('tensor', 'dp'))
- grad_gain_dense: float32 [2560], P('dp')
- grad_w_gate: float32 [2560, 7680], P(None, ('tensor', 'dp'))
- grad_w_up: float32 [2560, 7680], P(None, ('tensor', 'dp'))
- grad_w_down: float32 [7680, 2560], P(('tensor', 'dp'))
Inputs may be any that keep to these rules, and one draw needn't show every extreme that they name: starts[0] is 1; the distance between consecutive ones, and from the last one to the end, is at most 1024, and one distance equals 1024 exactly.
All inputs are finite; a program needn't handle non-finite values.
Results may differ from a plain program's by a relative error of at most 0.02.
Values may be sent and summed in bfloat16 or wider, within the bound.
No kernel may reach another device: no remote copies, remote signals or barrier semaphores. Data moves between devices by JAX's collectives and lax.ppermute only.
A program may use at most 320 MiB of HBM per device.

v0:
```python
import jax
import jax.numpy as jnp
from jax import lax
from jax.sharding import PartitionSpec as P

BLOCK = 256
CONV = 4


EPS = 1e-06


def from_behind(block, axis, distance):
    devices = range(lax.axis_size(axis))
    route = [(i - distance, i) for i in devices if i - distance in devices]
    return lax.ppermute(block, axis, route)


def entering(part, axis, combine, identity, reverse):
    count = lax.axis_size(axis)
    place = lax.axis_index(axis)
    ahead = count - 1 - place if reverse else place
    gathered = jax.tree.map(lambda a: lax.all_gather(a, axis), part)
    state = jax.tree.map(lambda a, e: jnp.zeros_like(a) + jnp.asarray(e, a.dtype), part, identity)

    def one(hop, state):
        source = count - 1 - hop if reverse else hop
        return combine(
            state, jax.tree.map(lambda a: lax.dynamic_index_in_dim(a, source, 0, False), gathered)
        )

    return lax.fori_loop(0, ahead, one, state)


def normed(value, gain):
    return value * lax.rsqrt(jnp.mean(value * value, axis=-1, keepdims=True) + EPS) * gain


def gelu_tanh(value):
    return jax.nn.gelu(value, approximate=True)


def affine(first, second):
    return (first[0] * second[0], second[0] * first[1] + second[1])


def lru_coeffs(ga_pre, gx_pre, conv_out, param, reset):
    gate_a = jax.nn.sigmoid(ga_pre)
    gate_x = jax.nn.sigmoid(gx_pre)
    log_a = -8.0 * gate_a * jax.nn.softplus(param)
    keep = 1.0 - reset
    decay = jnp.exp(log_a) * keep
    multiplier = jnp.sqrt(-jnp.expm1(2.0 * log_a)) * keep + reset
    return (decay, gate_x * conv_out * multiplier)


def conv_mix(padded, taps, masks):
    lag = CONV - 1
    count = masks.shape[0]
    total = taps[:, 0] * padded[lag : lag + count] * masks[:, 0:1]
    for shift_k in range(1, CONV):
        total = (
            total
            + taps[:, shift_k]
            * padded[lag - shift_k : lag - shift_k + count]
            * masks[:, shift_k : shift_k + 1]
        )
    return total


def rows_inner(left, right):
    return lax.dot_general(
        left, right, (((0,), (0,)), ((), ())), preferred_element_type=jnp.float32
    )


def cols_inner(left, right):
    return lax.dot_general(
        left, right, (((1,), (1,)), ((), ())), preferred_element_type=jnp.float32
    )


def gather_rows(value):
    return lax.all_gather(value, "tensor", axis=0, tiled=True)


def reduce_rows(value):
    return lax.psum_scatter(
        value.astype(jnp.bfloat16), "tensor", scatter_dimension=0, tiled=True
    ).astype(jnp.float32)


def tensor_total(value):
    return lax.psum(value, "tensor")


def fetch_mixer(
    gain_mixer, w_branch, w_signal, w_input_gate, w_decay_gate, conv_taps, decay_param, w_mixout
):
    return (
        lax.all_gather(gain_mixer, "dp", axis=0, tiled=True),
        lax.all_gather(w_branch, "dp", axis=1, tiled=True),
        lax.all_gather(w_signal, "dp", axis=1, tiled=True),
        lax.all_gather(w_input_gate, "dp", axis=1, tiled=True),
        lax.all_gather(w_decay_gate, "dp", axis=1, tiled=True),
        lax.all_gather(conv_taps, "dp", axis=0, tiled=True),
        lax.all_gather(decay_param, "dp", axis=0, tiled=True),
        lax.all_gather(w_mixout, "dp", axis=0, tiled=True),
    )


def fetch_dense(gain_dense, w_gate, w_up, w_down):
    return (
        lax.all_gather(gain_dense, "dp", axis=0, tiled=True),
        lax.all_gather(w_gate, "dp", axis=1, tiled=True),
        lax.all_gather(w_up, "dp", axis=1, tiled=True),
        lax.all_gather(w_down, "dp", axis=0, tiled=True),
    )


def per_device(
    block_input,
    starts,
    cotangent,
    gain_mixer,
    w_branch,
    w_signal,
    w_input_gate,
    w_decay_gate,
    conv_taps,
    decay_param,
    w_mixout,
    gain_dense,
    w_gate,
    w_up,
    w_down,
):
    group = starts.shape[0]
    lag = CONV - 1
    mixer_args = (
        gain_mixer,
        w_branch,
        w_signal,
        w_input_gate,
        w_decay_gate,
        conv_taps,
        decay_param,
        w_mixout,
    )
    dense_args = (gain_dense, w_gate, w_up, w_down)
    gain_one, wide_b, wide_s, wide_ig, wide_dg, taps, param, wide_o = fetch_mixer(*mixer_args)
    gain_two, wide_g, wide_u, wide_d = fetch_dense(*dense_args)
    x_val = block_input.astype(jnp.float32)
    n_one, norm_one_back = jax.vjp(normed, x_val, gain_one.astype(jnp.float32))
    h_one = gather_rows(n_one.astype(jnp.bfloat16))
    branch_pre = jnp.dot(h_one, wide_b, preferred_element_type=jnp.float32)
    branch, branch_back = jax.vjp(gelu_tanh, branch_pre)
    signal = jnp.dot(h_one, wide_s, preferred_element_type=jnp.float32).astype(jnp.bfloat16)
    channels = signal.shape[1]
    reset = starts.astype(jnp.float32)[:, None]
    cumulative = jnp.cumsum(starts)
    padded_cum = jnp.concatenate([jnp.zeros((lag,), jnp.int32), cumulative])
    masks = jnp.stack(
        [
            (cumulative - padded_cum[lag - k : lag - k + group] == 0).astype(jnp.float32)
            for k in range(CONV)
        ],
        axis=1,
    )
    tail_keep = (cumulative[group - 1] - cumulative[group - lag :] == 0)[:, None]
    rim = from_behind(signal[group - lag :] * tail_keep.astype(jnp.bfloat16), "dp", 1)
    padded = jnp.concatenate([rim, signal]).astype(jnp.float32)

    def conv_local(padded_in, taps_in):
        return conv_mix(padded_in, taps_in, masks)

    mixed_full, conv_back = jax.vjp(conv_local, padded, taps.astype(jnp.float32))
    mixed = mixed_full.astype(jnp.bfloat16)
    heads_here = wide_ig.shape[0]
    grouped = mixed.reshape(group, heads_here, BLOCK)
    gx_pre = jnp.einsum(
        "ghb,hbc->ghc", grouped, wide_ig, preferred_element_type=jnp.float32
    ).reshape(group, channels)
    ga_pre = jnp.einsum(
        "ghb,hbc->ghc", grouped, wide_dg, preferred_element_type=jnp.float32
    ).reshape(group, channels)

    def coeff_local(ga_in, gx_in, conv_in, param_in):
        return lru_coeffs(ga_in, gx_in, conv_in, param_in, reset)

    (decay, drive), coeff_back = jax.vjp(
        coeff_local, ga_pre, gx_pre, mixed.astype(jnp.float32), param.astype(jnp.float32)
    )
    prods, local_state = lax.associative_scan(affine, (decay, drive), axis=0)
    ones_row = jnp.ones((channels,), jnp.float32)
    zeros_row = jnp.zeros((channels,), jnp.float32)
    incoming = entering(
        (prods[group - 1], local_state[group - 1]), "dp", affine, (ones_row, zeros_row), False
    )
    state = local_state + prods * incoming[1][None, :]
    merged = (state * branch).astype(jnp.bfloat16)
    x_one = x_val + reduce_rows(jnp.dot(merged, wide_o, preferred_element_type=jnp.float32))
    n_two, norm_two_back = jax.vjp(normed, x_one, gain_two.astype(jnp.float32))
    h_two = gather_rows(n_two.astype(jnp.bfloat16))
    gate_pre = jnp.dot(h_two, wide_g, preferred_element_type=jnp.float32)
    up_val = jnp.dot(h_two, wide_u, preferred_element_type=jnp.float32)
    gate_act, gate_back = jax.vjp(gelu_tanh, gate_pre)
    act = (gate_act * up_val).astype(jnp.bfloat16)
    block_output = (
        x_one + reduce_rows(jnp.dot(act, wide_d, preferred_element_type=jnp.float32))
    ).astype(jnp.bfloat16)
    gain_two, wide_g, wide_u, wide_d = fetch_dense(*dense_args)
    d_out = gather_rows(cotangent)
    d_act = cols_inner(d_out, wide_d)
    d_gate = gate_back(d_act * up_val)[0].astype(jnp.bfloat16)
    d_up = (d_act * gate_act).astype(jnp.bfloat16)
    d_h_two = reduce_rows(cols_inner(d_gate, wide_g) + cols_inner(d_up, wide_u))
    d_x_norm_two, g_gain_two = norm_two_back(d_h_two)
    d_x_one = cotangent.astype(jnp.float32) + d_x_norm_two
    g_gain_two = tensor_total(g_gain_two)
    g_down = rows_inner(act, d_out)
    g_gate_rows = rows_inner(d_gate, h_two)
    g_up_rows = rows_inner(d_up, h_two)
    s_gain_two, s_gate_rows, s_up_rows, s_down = (
        lax.psum_scatter(g_gain_two, "dp", scatter_dimension=0, tiled=True),
        lax.psum_scatter(g_gate_rows, "dp", scatter_dimension=0, tiled=True),
        lax.psum_scatter(g_up_rows, "dp", scatter_dimension=0, tiled=True),
        lax.psum_scatter(g_down, "dp", scatter_dimension=0, tiled=True),
    )
    s_gate = s_gate_rows.T
    s_up = s_up_rows.T
    gain_one, wide_b, wide_s, wide_ig, wide_dg, taps, param, wide_o = fetch_mixer(*mixer_args)
    d_mix = gather_rows(d_x_one.astype(jnp.bfloat16))
    g_mixout = rows_inner(merged, d_mix)
    d_merged = cols_inner(d_mix, wide_o)
    d_state = d_merged * branch
    d_branch = branch_back(d_merged * state)[0].astype(jnp.bfloat16)
    shifted = jnp.concatenate([decay[1:], jnp.ones((1, channels), jnp.float32)])
    rev_prods, rev_state = lax.associative_scan(affine, (shifted[::-1], d_state[::-1]), axis=0)
    rev_prods = rev_prods[::-1]
    rev_state = rev_state[::-1]
    later = entering(
        (decay[0] * rev_prods[0], decay[0] * rev_state[0]),
        "dp",
        affine,
        (ones_row, zeros_row),
        True,
    )
    d_total = rev_state + rev_prods * later[1][None, :]
    previous = jnp.concatenate([incoming[1][None, :], state[:-1]])
    d_ga, d_gx, d_mixed_direct, g_param = coeff_back((d_total * previous, d_total))
    d_ga_low = d_ga.astype(jnp.bfloat16).reshape(group, heads_here, BLOCK)
    d_gx_low = d_gx.astype(jnp.bfloat16).reshape(group, heads_here, BLOCK)
    g_input_rows = jnp.einsum("ghb,ghc->bhc", grouped, d_gx_low, preferred_element_type=jnp.float32)
    g_decay_rows = jnp.einsum("ghb,ghc->bhc", grouped, d_ga_low, preferred_element_type=jnp.float32)
    d_back_gates = jnp.einsum(
        "ghc,hbc->ghb", d_gx_low, wide_ig, preferred_element_type=jnp.float32
    ) + jnp.einsum("ghc,hbc->ghb", d_ga_low, wide_dg, preferred_element_type=jnp.float32)
    d_mixed = d_mixed_direct + d_back_gates.reshape(group, channels)
    d_padded, g_taps = conv_back(d_mixed)
    back_rim = from_behind(d_padded[:lag], "dp", -1)
    d_sig_full = d_padded[lag:]
    d_sig_full = jnp.concatenate(
        [
            d_sig_full[: group - lag],
            d_sig_full[group - lag :] + back_rim * tail_keep.astype(jnp.float32),
        ]
    )
    d_signal = d_sig_full.astype(jnp.bfloat16)
    g_branch_rows = rows_inner(d_branch, h_one)
    g_signal_rows = rows_inner(d_signal, h_one)
    d_h_one = reduce_rows(cols_inner(d_branch, wide_b) + cols_inner(d_signal, wide_s))
    d_x_norm_one, g_gain_one = norm_one_back(d_h_one)
    grad_input = d_x_one + d_x_norm_one
    g_gain_one = tensor_total(g_gain_one)
    (
        s_gain_one,
        s_branch_rows,
        s_signal_rows,
        s_input_rows,
        s_decay_rows,
        s_taps,
        s_param,
        s_mixout,
    ) = (
        lax.psum_scatter(g_gain_one, "dp", scatter_dimension=0, tiled=True),
        lax.psum_scatter(g_branch_rows, "dp", scatter_dimension=0, tiled=True),
        lax.psum_scatter(g_signal_rows, "dp", scatter_dimension=0, tiled=True),
        lax.psum_scatter(g_input_rows, "dp", scatter_dimension=0, tiled=True),
        lax.psum_scatter(g_decay_rows, "dp", scatter_dimension=0, tiled=True),
        lax.psum_scatter(g_taps, "dp", scatter_dimension=0, tiled=True),
        lax.psum_scatter(g_param, "dp", scatter_dimension=0, tiled=True),
        lax.psum_scatter(g_mixout, "dp", scatter_dimension=0, tiled=True),
    )
    s_branch = s_branch_rows.T
    s_signal = s_signal_rows.T
    s_input_gate = jnp.transpose(s_input_rows, (1, 0, 2))
    s_decay_gate = jnp.transpose(s_decay_rows, (1, 0, 2))
    return (
        block_output,
        grad_input,
        s_gain_one,
        s_branch,
        s_signal,
        s_input_gate,
        s_decay_gate,
        s_taps,
        s_param,
        s_mixout,
        s_gain_two,
        s_gate,
        s_up,
        s_down,
    )


def solution(mesh):
    placed = (
        P(("dp", "tensor"), None),
        P("dp"),
        P(("dp", "tensor"), None),
        P("dp"),
        P(None, ("tensor", "dp")),
        P(None, ("tensor", "dp")),
        P("tensor", "dp", None),
        P("tensor", "dp", None),
        P(("tensor", "dp"), None),
        P(("tensor", "dp")),
        P(("tensor", "dp"), None),
        P("dp"),
        P(None, ("tensor", "dp")),
        P(None, ("tensor", "dp")),
        P(("tensor", "dp"), None),
    )
    return jax.shard_map(
        per_device,
        mesh=mesh,
        in_specs=placed,
        out_specs=(
            P(("dp", "tensor"), None),
            P(("dp", "tensor"), None),
            P("dp"),
            P(None, ("tensor", "dp")),
            P(None, ("tensor", "dp")),
            P("tensor", "dp", None),
            P("tensor", "dp", None),
            P(("tensor", "dp"), None),
            P(("tensor", "dp")),
            P(("tensor", "dp"), None),
            P("dp"),
            P(None, ("tensor", "dp")),
            P(None, ("tensor", "dp")),
            P(("tensor", "dp"), None),
        ),
        check_vma=False,
    )
```

profile of v0, /device:TPU:0, one launch (start us, length us, event | category | flops | bytes accessed | tf_op | source)
XLA Modules:
  0.0 2973.9 jit_solution(11796489775713776362)
XLA Ops:
  12.5 62.9 %all-reduce.83 = (bf16[2560]{0:T(1024)(128)(2,1)S(1)}, bf16[1280]{0:T(1024)(128)(2,1)S(1)}, bf16[2560]{0:T(1024)(128)(2,1)}) all-reduce(bf16[2560]{0:T(1024)(128)(2,1)S(1)} %dynamic-update-slice, bf16[1280]{0:T(1024)(128)(2,1)S(1)} %dynamic-update-slice.1, ...), channel_id=1, replica_groups=mesh['dp'=16,'tensor'=2] {'dp'}, use_global_device_ids=true, to_apply=%add.75 | all-reduce | flops 6400 | bytes 25600
  83.8 17.1 all-gather
  101.0 22.5 all_gather.74
  123.5 23.1 all_gather.75
  146.7 22.7 all-gather.18.cloned.1.call-done
  343.2 21.5 all-gather.1
  376.1 17.7 all-gather.2
  394.2 8.3 multiply_convert_fusion.3
  403.4 5.8 convolution_convert_fusion
  409.8 22.2 reduce-scatter.16.cloned.1.call-done
  437.5 21.6 all-gather.24.cloned.1.call-done
  459.1 104.4 %all-gather.26.cloned.1.call-done = bf16[2560,3840]{0,1:T(8,128)(2,1)} async-done(((bf16[2560,240]{0,1:T(8,128)(2,1)}), bf16[2560,3840]{0,1:T(8,128)(2,1)}) %all-gather.26.cloned.1.call-update) | async-done | bytes 19660816 | tf_op jit(solution)/shard_map/all_gather | solution.py:115
  563.4 11.2 fusion.96
  574.7 93.1 %all-gather.28.cloned.1.call-done = bf16[2560,3840]{0,1:T(8,128)(2,1)} async-done(((bf16[2560,240]{0,1:T(8,128)(2,1)}), bf16[2560,3840]{0,1:T(8,128)(2,1)}) %all-gather.28.cloned.1.call-update) | async-done | bytes 19660816 | tf_op jit(solution)/shard_map/all_gather | solution.py:116
  667.8 11.2 fusion.97
  679.0 14.7 all-gather.32.cloned.1.call-done
  693.7 104.2 %all-gather.30.cloned.1.call-done = bf16[3840,2560]{1,0:T(8,128)(2,1)} async-done(((bf16[240,2560]{1,0:T(8,128)(2,1)}), bf16[3840,2560]{1,0:T(8,128)(2,1)}) %all-gather.30.cloned.1.call-update) | async-done | bytes 19660816 | tf_op jit(solution)/shard_map/all_gather | solution.py:117
  797.9 15.4 multiply_convert_fusion
  813.3 10.0 fusion.98
  823.3 11.0 fusion.8
  834.6 23.1 reduce-scatter.20.cloned.1.call-done
  876.7 5.9 slice.657
  882.6 5.9 slice.666
  891.7 7.7 fusion.45
  906.8 5.9 slice.663
  996.9 6.0 slice.719
  1068.7 10.8 rev.8
  1079.5 10.7 rev.9
  1090.2 21.5 all-gather.3
  1111.8 17.6 all-gather.4
  1130.9 5.9 multiply_reduce_fusion
  1172.3 5.9 fusion.7
  1178.3 11.0 convolution_convert_fusion.1
  1190.6 6.6 fusion.100
  1198.3 8.0 fusion.101
  1206.4 6.5 fusion.46
  1214.2 17.7 fusion.102
  1232.0 17.1 fusion.103
  1250.7 16.8 fusion.104
  1274.8 62.6 %reduce-scatter.30.cloned.1.call-done = f32[16,5,256]{2,1,0:T(8,128)} async-done(((f32[256,5,256]{2,1,0:T(8,128)}), f32[16,5,256]{2,1,0:T(8,128)}) %reduce-scatter.30.cloned.1.call-update) | async-done | bytes 81936 | tf_op jit(solution)/shard_map/reduce_scatter | solution.py:290
  1338.9 23.4 reduce-scatter.22.cloned.1.call-done
  1364.1 61.2 %all-reduce.81 = (f32[2560]{0:T(1024)S(1)}, f32[1280]{0:T(1024)S(1)}, f32[2560]{0:T(1024)S(1)}) all-reduce(f32[2560]{0:T(1024)S(1)} %get-tuple-element.206, f32[1280]{0:T(1024)S(1)} %get-tuple-element.336, f32[2560]{0:T(1024)S(1)} %copy-done.63), channel_id=6, replica_groups=mesh['dp'=16,'tensor'=2] {'dp'}, use_global_device_ids=true, to_apply=%region_16.17.clone | all-reduce | flops 6400 | bytes 51200
  1435.2 95.9 %reduce-scatter.24.cloned.1.call-done = f32[80,2560]{1,0:T(8,128)} async-done(((f32[1280,2560]{1,0:T(8,128)}), f32[80,2560]{1,0:T(8,128)}) %reduce-scatter.24.cloned.1.call-update) | async-done | bytes 819216 | tf_op jit(solution)/shard_map/reduce_scatter | solution.py:287
  1531.1 142.2 %reduce-scatter.32.cloned.1.call-done = f32[80,2560]{1,0:T(8,128)} async-done(((f32[1280,2560]{1,0:T(8,128)}), f32[80,2560]{1,0:T(8,128)}) %reduce-scatter.32.cloned.1.call-update) | async-done | bytes 819216 | tf_op jit(solution)/shard_map/reduce_scatter | solution.py:293
  1673.3 142.6 %reduce-scatter.26.cloned.1.call-done = f32[80,2560]{1,0:T(8,128)} async-done(((f32[1280,2560]{1,0:T(8,128)}), f32[80,2560]{1,0:T(8,128)}) %reduce-scatter.26.cloned.1.call-update) | async-done | bytes 819216 | tf_op jit(solution)/shard_map/reduce_scatter | solution.py:288
  1815.9 383.7 %reduce-scatter.34.cloned.1.call-done = f32[240,2560]{1,0:T(8,128)} async-done(((f32[3840,2560]{1,0:T(8,128)}), f32[240,2560]{1,0:T(8,128)}) %reduce-scatter.34.cloned.1.call-update) | async-done | bytes 2457616 | tf_op jit(solution)/shard_map/reduce_scatter | solution.py:226
  2199.6 383.8 %reduce-scatter.36.cloned.1.call-done = f32[240,2560]{1,0:T(8,128)} async-done(((f32[3840,2560]{1,0:T(8,128)}), f32[240,2560]{1,0:T(8,128)}) %reduce-scatter.36.cloned.1.call-update) | async-done | bytes 2457616 | tf_op jit(solution)/shard_map/reduce_scatter | solution.py:227
  2583.4 383.8 %reduce-scatter.38.cloned.1.call-done = f32[240,2560]{1,0:T(8,128)} async-done(((f32[3840,2560]{1,0:T(8,128)}), f32[240,2560]{1,0:T(8,128)}) %reduce-scatter.38.cloned.1.call-update) | async-done | bytes 2457616 | tf_op jit(solution)/shard_map/reduce_scatter | solution.py:228
  (654 shorter events, 445.3 us)
Async XLA Ops:
  7.2 139.5 %all-gather.16.cloned.1.call-start = ((), (), s32[]{:S(2)}) async-start(), calls=%async_computation.13 | async-start | bytes 1966080 | tf_op jit(solution)/shard_map/all_gather | solution.py:84
  75.4 71.2 %copy-start.97 = (bf16[1280]{0:T(1024)(128)(2,1)}, bf16[1280]{0:T(1024)(128)(2,1)S(1)}, u32[]{:S(2)}) copy-start(bf16[1280]{0:T(1024)(128)(2,1)S(1)} %get-tuple-element.238) | copy-start | bytes 7684
  79.0 90.3 %all-gather.18.cloned.1.call-start = ((), (), s32[]{:S(2)}) async-start(), calls=%async_computation.14 | async-start | bytes 6963200 | tf_op jit(solution)/shard_map/all_gather | solution.py:103
  79.8 314.4 %all-gather.20.cloned.1.call-start = ((), (), s32[]{:S(2)}) async-start(), calls=%async_computation.15 | async-start | bytes 6963200 | tf_op jit(solution)/shard_map/all_gather | solution.py:102
  80.5 322.0 %all-gather.22.cloned.1.call-start = ((), (), s32[]{:S(2)}) async-start(), calls=%async_computation.16 | async-start | bytes 6963200 | tf_op jit(solution)/shard_map/all_gather | solution.py:108
  81.1 351.0 %reduce-scatter.16.cloned.1.call-start = ((), (), s32[]{:S(2)}) async-start(), calls=%async_computation.17 | async-start | bytes 1966080 | tf_op jit(solution)/shard_map/reduce_scatter | solution.py:88
  82.4 105.1 %copy-start.71 = (f32[256]{0:T(256)}, f32[256]{0:T(256)S(1)}, u32[]{:S(2)}) copy-start(f32[256]{0:T(256)S(1)} %get-tuple-element.340) | copy-start | bytes 3076
  82.4 105.1 %copy-start.73 = (f32[256]{0:T(256)}, f32[256]{0:T(256)S(1)}, u32[]{:S(2)}) copy-start(f32[256]{0:T(256)S(1)} %get-tuple-element.341) | copy-start | bytes 3076
  82.4 105.1 %copy-start.75 = (f32[256]{0:T(256)}, f32[256]{0:T(256)S(1)}, u32[]{:S(2)}) copy-start(f32[256]{0:T(256)S(1)} %get-tuple-element.342) | copy-start | bytes 3076
  82.4 105.1 %copy-start.99 = (f32[256]{0:T(256)}, f32[256]{0:T(256)S(1)}, u32[]{:S(2)}) copy-start(f32[256]{0:T(256)S(1)} %broadcast_subtract_fusion) | copy-start | bytes 3076
  123.5 55.2 %copy-start.33 = (bf16[5,256,256]{2,1,0:T(8,128)(2,1)}, bf16[5,256,256]{2,1,0:T(8,128)(2,1)S(1)}, u32[]{:S(2)}) copy-start(bf16[5,256,256]{2,1,0:T(8,128)(2,1)S(1)} %all_gather.74) | copy-start | bytes 1966084
  174.6 3.0 collective-permute-start
  409.2 49.9 %all-gather.24.cloned.1.call-start = ((), (), s32[]{:S(2)}) async-start(), calls=%async_computation.18 | async-start | bytes 1966080 | tf_op jit(solution)/shard_map/all_gather | solution.py:84
  409.8 450.6 %copy-start.48 = (f32[2560]{0:T(1024)}, f32[2560]{0:T(1024)S(1)}, u32[]{:S(2)}) copy-start(f32[2560]{0:T(1024)S(1)} %convert_element_type.125) | copy-start | bytes 30724
  433.5 426.9 %copy-start.104 = (f32[128]{0:T(128)}, f32[128]{0:T(128)S(1)}, u32[]{:S(2)}) copy-start(f32[128]{0:T(128)S(1)} %fusion.79) | copy-start | bytes 1540
  434.6 128.8 %all-gather.26.cloned.1.call-start = ((), (), s32[]{:S(2)}) async-start(), calls=%async_computation.19 | async-start | bytes 20889600 | tf_op jit(solution)/shard_map/all_gather | solution.py:115
  435.4 232.4 %all-gather.28.cloned.1.call-start = ((), (), s32[]{:S(2)}) async-start(), calls=%async_computation.20 | async-start | bytes 20889600 | tf_op jit(solution)/shard_map/all_gather | solution.py:116
  436.1 257.6 %all-gather.32.cloned.1.call-start = ((), (), s32[]{:S(2)}) async-start(), calls=%async_computation.23 | async-start | bytes 1966080 | tf_op jit(solution)/shard_map/all_gather | solution.py:84
  436.9 361.1 %all-gather.30.cloned.1.call-start = ((), (), s32[]{:S(2)}) async-start(), calls=%async_computation.21 | async-start | bytes 20889600 | tf_op jit(solution)/shard_map/all_gather | solution.py:117
  437.5 420.2 %reduce-scatter.20.cloned.1.call-start = ((), (), s32[]{:S(2)}) async-start(), calls=%async_computation.24 | async-start | bytes 1966080 | tf_op jit(solution)/shard_map/reduce_scatter | solution.py:88
  834.4 57.4 %all-gather.34.cloned.1.call-start = ((), (), s32[]{:S(2)}) async-start(), calls=%async_computation.25 | async-start | bytes 1966080 | tf_op jit(solution)/shard_map/all_gather | solution.py:84
  861.8 407.3 %reduce-scatter.40.cloned.1.call-start = ((), (), s32[]{:S(2)}) async-start(), calls=%async_computation.35 | async-start | bytes 696320
  1079.4 51.5 %copy-start.76 = (f32[256]{0:T(256)S(1)}, f32[256]{0:T(256)}, u32[]{:S(2)}) copy-start(f32[256]{0:T(256)} %copy-done.75) | copy-start | bytes 3076
  1079.5 51.5 %copy-start.96 = (f32[1,1280]{1,0:T(1,128)S(1)}, f32[1,1280]{1,0:T(1,128)}, u32[]{:S(2)}) copy-start(f32[1,1280]{1,0:T(1,128)} %broadcast_in_dim.15) | copy-start | bytes 15364
  1079.5 51.5 %copy-start.100 = (f32[256]{0:T(256)S(1)}, f32[256]{0:T(256)}, u32[]{:S(2)}) copy-start(f32[256]{0:T(256)} %copy-done.99) | copy-start | bytes 3076
  1079.5 51.5 %copy-start.102 = (f32[256]{0:T(256)S(1)}, f32[256]{0:T(256)}, u32[]{:S(2)}) copy-start(f32[256]{0:T(256)} %copy-done.101) | copy-start | bytes 3076
  1154.9 118.3 %reduce-scatter.28.cloned.1.call-start = ((), (), s32[]{:S(2)}) async-start(), calls=%async_computation.29 | async-start | bytes 2228224 | tf_op jit(solution)/shard_map/reduce_scatter | solution.py:289
  1157.3 180.1 %reduce-scatter.30.cloned.1.call-start = ((), (), s32[]{:S(2)}) async-start(), calls=%async_computation.30 | async-start | bytes 2228224 | tf_op jit(solution)/shard_map/reduce_scatter | solution.py:290
  1163.9 198.5 %reduce-scatter.22.cloned.1.call-start = ((), (), s32[]{:S(2)}) async-start(), calls=%async_computation.26 | async-start | bytes 1966080 | tf_op jit(solution)/shard_map/reduce_scatter | solution.py:88
  1164.8 6.9 collective-permute-start.1
  1178.3 253.3 %reduce-scatter.18.cloned.1.call-start = ((), (), s32[]{:S(2)}) async-start(), calls=%async_computation.22 | async-start | bytes 1966080 | tf_op jit(solution)/shard_map/reduce_scatter | solution.py:88
  1189.3 341.8 %reduce-scatter.24.cloned.1.call-start = ((), (), s32[]{:S(2)}) async-start(), calls=%async_computation.27 | async-start | bytes 13926400 | tf_op jit(solution)/shard_map/reduce_scatter | solution.py:287
  1197.3 476.1 %reduce-scatter.32.cloned.1.call-start = ((), (), s32[]{:S(2)}) async-start(), calls=%async_computation.31 | async-start | bytes 13926400 | tf_op jit(solution)/shard_map/reduce_scatter | solution.py:293
  1206.3 609.6 %reduce-scatter.26.cloned.1.call-start = ((), (), s32[]{:S(2)}) async-start(), calls=%async_computation.28 | async-start | bytes 13926400 | tf_op jit(solution)/shard_map/reduce_scatter | solution.py:288
  1212.9 986.7 %reduce-scatter.34.cloned.1.call-start = ((), (), s32[]{:S(2)}) async-start(), calls=%async_computation.32 | async-start | bytes 41779200 | tf_op jit(solution)/shard_map/reduce_scatter | solution.py:226
  1232.0 1351.4 %reduce-scatter.36.cloned.1.call-start = ((), (), s32[]{:S(2)}) async-start(), calls=%async_computation.33 | async-start | bytes 41779200 | tf_op jit(solution)/shard_map/reduce_scatter | solution.py:227
  1249.2 1718.0 %reduce-scatter.38.cloned.1.call-start = ((), (), s32[]{:S(2)}) async-start(), calls=%async_computation.34 | async-start | bytes 41779200 | tf_op jit(solution)/shard_map/reduce_scatter | solution.py:228
  1267.5 94.8 %copy-start.1 = (bf16[128,2560]{1,0:T(8,128)(2,1)S(1)}, bf16[128,2560]{1,0:T(8,128)(2,1)}, u32[]{:S(2)}) copy-start(bf16[128,2560]{1,0:T(8,128)(2,1)} %param.19) | copy-start | bytes 1966084
  1267.5 94.8 %copy-start.51 = (f32[2560]{0:T(1024)S(1)}, f32[2560]{0:T(1024)}, u32[]{:S(2)}) copy-start(f32[2560]{0:T(1024)} %copy-done.50) | copy-start | bytes 30724
  1267.5 94.8 %copy-start.108 = (f32[128]{0:T(128)S(1)}, f32[128]{0:T(128)}, u32[]{:S(2)}) copy-start(f32[128]{0:T(128)} %copy-done.107) | copy-start | bytes 1540
  1267.5 164.1 %copy-start.21 = (bf16[128,2560]{1,0:T(8,128)(2,1)S(1)}, bf16[128,2560]{1,0:T(8,128)(2,1)}, u32[]{:S(2)}) copy-start(bf16[128,2560]{1,0:T(8,128)(2,1)} %param.21) | copy-start | bytes 1966084
  1267.5 96.6 %copy-start.63 = (f32[2560]{0:T(1024)S(1)}, f32[2560]{0:T(1024)}, u32[]{:S(2)}) copy-start(f32[2560]{0:T(1024)} %get-tuple-element.204) | copy-start | bytes 30724
  1267.6 164.0 %copy-start.114 = (f32[128]{0:T(128)S(1)}, f32[128]{0:T(128)}, u32[]{:S(2)}) copy-start(f32[128]{0:T(128)} %copy-done.113) | copy-start | bytes 1540
  1267.6 164.0 %copy-start.7 = (bf16[128,2560]{1,0:T(8,128)(2,1)S(1)}, bf16[128,2560]{1,0:T(8,128)(2,1)}, u32[]{:S(2)}) copy-start(bf16[128,2560]{1,0:T(8,128)(2,1)} %reduce-scatter.16.cloned.1.call-done) | copy-start | bytes 1966084
  1267.6 164.0 %copy-start.19 = (bf16[128,2560]{1,0:T(8,128)(2,1)S(1)}, bf16[128,2560]{1,0:T(8,128)(2,1)}, u32[]{:S(2)}) copy-start(bf16[128,2560]{1,0:T(8,128)(2,1)} %reduce-scatter.20.cloned.1.call-done) | copy-start | bytes 1966084
  1267.6 164.0 %copy-start.49 = (f32[2560]{0:T(1024)S(1)}, f32[2560]{0:T(1024)}, u32[]{:S(2)}) copy-start(f32[2560]{0:T(1024)} %copy-done.48) | copy-start | bytes 30724
  1267.6 164.0 %copy-start.105 = (f32[128]{0:T(128)S(1)}, f32[128]{0:T(128)}, u32[]{:S(2)}) copy-start(f32[128]{0:T(128)} %copy-done.104) | copy-start | bytes 1540
  1267.6 164.0 %copy-start.111 = (f32[128]{0:T(128)S(1)}, f32[128]{0:T(128)}, u32[]{:S(2)}) copy-start(f32[128]{0:T(128)} %copy-done.110) | copy-start | bytes 1540
  (92 other events, 779.8 us)
Sparse Core Ops, SparseCore 0:
  79.1 21.5 all-gather.15
  102.9 66.3 all-gather.17
  171.6 62.3 all-gather.19
  236.2 61.9 all-gather.21
  409.3 22.7 reduce-scatter.15
  434.8 24.2 all-gather.23
  460.7 102.6 all-gather.25
  565.1 102.6 all-gather.27
  669.4 24.2 all-gather.31
  695.2 102.6 all-gather.29
  834.5 23.1 reduce-scatter.19
  862.0 24.2 all-gather.33
  1155.0 53.5 reduce-scatter.39
  1212.6 60.5 reduce-scatter.27
  1276.8 60.5 reduce-scatter.29
  1340.1 22.1 reduce-scatter.21
  1364.4 23.1 reduce-scatter.17
  1392.7 138.3 reduce-scatter.23
  1535.8 137.4 reduce-scatter.31
  1678.4 137.5 reduce-scatter.25
  1820.8 378.7 reduce-scatter.33
  2204.5 378.8 reduce-scatter.35
  2588.3 378.8 reduce-scatter.37
where the time goes:
time: 2990 us; the launch traced here: 2970 us
  waiting for transfers between devices  2030 us (68%)
  local copies, waits for them, and re-layouts  337 us (11%)
  blocking collectives  271 us (9%)
  matrix products  191 us (6%)
  other arithmetic  118 us (4%)
    reduce_scatter x1, waiting for transfers between devices, per_device(): lax.psum_scatter(g_down, 'dp', scatter_dimension=0, tiled=True)  384 us
    reduce_scatter x1, waiting for transfers between devices, per_device(): lax.psum_scatter(g_up_rows, 'dp', scatter_dimension=0, tiled=True)  384 us
    reduce_scatter x1, waiting for transfers between devices, per_device(): lax.psum_scatter(g_gate_rows, 'dp', scatter_dimension=0, tiled=True)  384 us
    reduce_scatter x1, waiting for transfers between devices, per_device(): lax.psum_scatter(g_signal_rows, 'dp', scatter_dimension=0, tiled=True)  143 us
    reduce_scatter x1, waiting for transfers between devices, per_device(): lax.psum_scatter(g_mixout, 'dp', scatter_dimension=0, tiled=True)  142 us
    unnamed x2, blocking collectives  124 us
    slice x57, local copies, waits for them, and re-layouts, per_device(): lax.associative_scan(affine, (shifted[::-1], d_state[::-1]), axis=0)  115 us
    all_gather x1, waiting for transfers between devices, fetch_dense(): lax.all_gather(w_gate, 'dp', axis=1, tiled=True)  104 us
  transfers between devices with their start and end apart: 25, of which 18 were waited for; matrix products, arithmetic and copies ran while one was open for 12% of the time, Pallas kernels for 0%

commit v1 on v0

v1 whole, which is shorter than its diff:
```python
import functools

import jax
import jax.numpy as jnp
from jax import lax
from jax.experimental import pallas as pl
from jax.experimental.pallas import tpu as pltpu
from jax.sharding import PartitionSpec as P

BLOCK = 256
CONV = 4
MAXLEN = 1024
EPS = 1e-06
BF16 = jnp.bfloat16
F32 = jnp.float32


def ring_order(chips):
    return list(range(0, chips, 2)) + list(range(chips - 1, 0, -2))


class Ring:
    def __init__(self):
        count = lax.axis_size("dp")
        self.chips = count // 2
        self.reach = self.chips // 2
        order = ring_order(self.chips)
        self.up_route = [
            (order[p] * 2 + c, order[(p + 1) % self.chips] * 2 + c)
            for p in range(self.chips)
            for c in range(2)
        ]
        self.down_route = [(b, a) for a, b in self.up_route]
        place = [0] * self.chips
        for p, chip in enumerate(order):
            place[chip] = p
        me = lax.axis_index("dp")
        self.core = lax.rem(me, 2)
        self.order = jnp.array(order, jnp.int32)
        self.place = jnp.array(place, jnp.int32)[me // 2]

    def chip_at(self, distance):
        return self.order[lax.rem(self.place - distance + self.chips, self.chips)]

    def up(self, value):
        return lax.ppermute(value, "dp", self.up_route)

    def down(self, value):
        return lax.ppermute(value, "dp", self.down_route)

    def gather(self, value):
        half = value.shape[0] // 2
        u = d = value
        pairs = []
        for _ in range(self.reach - 1):
            u, d = self.up(u), self.down(d)
            pairs.append((u, d))
        far = jnp.concatenate([self.up(u[:half]), self.down(d[half:])])
        return pairs, far

    def scatter(self, own, pairs, far):
        half = far.shape[0] // 2
        to_down = self.down(far[:half])
        to_up = self.up(far[half:])
        first = True
        for u, d in reversed(pairs):
            if first:
                u = jnp.concatenate([plus(u[:half], to_down), u[half:].astype(BF16)])
                d = jnp.concatenate([d[:half].astype(BF16), plus(d[half:], to_up)])
                first = False
            else:
                u, d = plus(u, to_down), plus(d, to_up)
            to_down, to_up = self.down(u), self.up(d)
        return own.astype(F32) + to_down.astype(F32) + to_up.astype(F32)


def plus(a, b):
    return (a.astype(F32) + b.astype(F32)).astype(BF16)


def core_swap(value):
    count = lax.axis_size("dp")
    return lax.ppermute(value, "dp", [(i, i ^ 1) for i in range(count)])


def tensor_swap(value):
    return lax.ppermute(value, "tensor", [(0, 1), (1, 0)])


def after(value, other):
    return lax.optimization_barrier((value, other))[0]


def from_behind(block, distance):
    devices = range(lax.axis_size("dp"))
    route = [(i - distance, i) for i in devices if i - distance in devices]
    return lax.ppermute(block, "dp", route)


def entering(prods, state, hops, reverse):
    part = jnp.stack([prods, state])
    total = jnp.zeros_like(state)
    sign = -1 if reverse else 1
    got = [from_behind(part, sign * hop) for hop in range(1, hops + 1)]
    for value in reversed(got):
        total = value[0] * total + value[1]
    return total


def normed(value, gain):
    return value * lax.rsqrt(jnp.mean(value * value, axis=-1, keepdims=True) + EPS) * gain


def gelu_tanh(value):
    return jax.nn.gelu(value, approximate=True)


def lru_coeffs(ga_pre, gx_pre, conv_out, param, reset):
    gate_a = jax.nn.sigmoid(ga_pre)
    gate_x = jax.nn.sigmoid(gx_pre)
    log_a = -8.0 * gate_a * jax.nn.softplus(param)
    keep = 1.0 - reset
    decay = jnp.exp(log_a) * keep
    multiplier = jnp.sqrt(-jnp.expm1(2.0 * log_a)) * keep + reset
    return (decay, gate_x * conv_out * multiplier)


def conv_mix(padded, taps, masks):
    lag = CONV - 1
    count = masks.shape[0]
    total = taps[:, 0] * padded[lag : lag + count] * masks[:, 0:1]
    for shift_k in range(1, CONV):
        total = (
            total
            + taps[:, shift_k]
            * padded[lag - shift_k : lag - shift_k + count]
            * masks[:, shift_k : shift_k + 1]
        )
    return total


def rows_inner(left, right):
    return lax.dot_general(
        left, right, (((0,), (0,)), ((), ())), preferred_element_type=F32
    )


def cols_inner(left, right):
    return lax.dot_general(
        left, right, (((1,), (1,)), ((), ())), preferred_element_type=F32
    )


def scan_body(reverse, a_ref, b_ref, p_ref, s_ref):
    rows, width = a_ref.shape
    blocks = rows // 8
    row = lax.broadcasted_iota(jnp.int32, (8, width), 0)

    def step(i, carry):
        p_in, s_in = carry
        at = (blocks - 1 - i) if reverse else i
        here = pl.ds(pl.multiple_of(at * 8, 8), 8)
        a = a_ref[here, :]
        b = b_ref[here, :]
        for shift in (1, 2, 4):
            turn = 8 - shift if reverse else shift
            inside = (row < 8 - shift) if reverse else (row >= shift)
            a_prev = jnp.where(inside, pltpu.roll(a, turn, 0), 1.0)
            b_prev = jnp.where(inside, pltpu.roll(b, turn, 0), 0.0)
            b = a * b_prev + b
            a = a * a_prev
        b = b + a * s_in
        a = a * p_in
        p_ref[here, :] = a
        s_ref[here, :] = b
        last = 0 if reverse else 7
        return (a[last : last + 1], b[last : last + 1])

    lax.fori_loop(
        0, blocks, step, (jnp.ones((1, width), F32), jnp.zeros((1, width), F32))
    )


def local_scan(coeff, value, reverse):
    shape = jax.ShapeDtypeStruct(value.shape, F32)
    return pl.pallas_call(
        functools.partial(scan_body, reverse),
        out_shape=(shape, shape),
        in_specs=[pl.BlockSpec(memory_space=pltpu.VMEM)] * 2,
        out_specs=(pl.BlockSpec(memory_space=pltpu.VMEM),) * 2,
        cost_estimate=pl.CostEstimate(
            flops=20 * value.size, bytes_accessed=16 * value.size, transcendentals=0
        ),
        compiler_params=pltpu.CompilerParams(vmem_limit_bytes=32 << 20),
    )(coeff, value)


def gather_absolute(ring, shard, sizes, wait=None):
    count = 2 * ring.chips
    width = shard.shape[1]
    if wait is not None:
        shard = after(shard, wait)
    pairs, far = ring.gather(shard)
    chunks = [(0, shard)]
    for k, (u, d) in enumerate(pairs, 1):
        chunks += [(k, u), (-k, d)]
    chunks.append((ring.reach, far))
    outs = [jnp.zeros((count, size, width), shard.dtype) for size in sizes]
    for distance, chunk in chunks:
        other = core_swap(chunk)
        first = jnp.where(ring.core == 0, chunk, other)
        second = jnp.where(ring.core == 0, other, chunk)
        both = jnp.stack([first, second])
        at = ring.chip_at(distance) * 2
        start = 0
        for i, size in enumerate(sizes):
            outs[i] = lax.dynamic_update_slice(
                outs[i], both[:, start : start + size], (at, 0, 0)
            )
            start += size
    return outs, pairs[-1]


def scatter_absolute(ring, parts):
    count = 2 * ring.chips
    split = [p.astype(BF16).reshape(ring.chips, 2, p.shape[1], p.shape[2]) for p in parts]
    split = jnp.concatenate(split, axis=2)
    theirs = core_swap(lax.dynamic_index_in_dim(split, 1 - ring.core, 1, False))
    mine = plus(lax.dynamic_index_in_dim(split, ring.core, 1, False), theirs)

    def part(distance):
        return lax.dynamic_index_in_dim(mine, ring.chip_at(distance), 0, False)

    pairs = [(part(k), part(-k)) for k in range(1, ring.reach)]
    return ring.scatter(part(0), pairs, part(ring.reach))


def fetch_hidden(shard):
    mine = jnp.concatenate([shard, tensor_swap(shard)])
    return jnp.concatenate([mine, core_swap(mine)])


def reduce_hidden(grad):
    size = grad.shape[0] // 4
    mine = grad[: 2 * size] + core_swap(grad[2 * size :].astype(BF16)).astype(F32)
    return mine[:size] + tensor_swap(mine[size:].astype(BF16)).astype(F32)


def ordered(ring_tensor, own, other):
    first = jnp.where(ring_tensor == 0, own, other)
    second = jnp.where(ring_tensor == 0, other, own)
    return jnp.concatenate([first, second])


def per_device(
    block_input,
    starts,
    cotangent,
    gain_mixer,
    w_branch,
    w_signal,
    w_input_gate,
    w_decay_gate,
    conv_taps,
    decay_param,
    w_mixout,
    gain_dense,
    w_gate,
    w_up,
    w_down,
):
    ring = Ring()
    side = lax.axis_index("tensor")
    count = lax.axis_size("dp")
    group = starts.shape[0]
    rows, width = block_input.shape
    shard = w_branch.shape[1]
    channels = shard * count
    lag = CONV - 1
    hops = -(-MAXLEN // group)
    heads_here = w_input_gate.shape[0]

    small = jnp.concatenate(
        [gain_mixer, gain_dense, conv_taps.reshape(-1), decay_param]
    )
    n_small = small.shape[0]
    small = jnp.pad(small, (0, width - n_small)).reshape(1, width)
    gates = jnp.concatenate(
        [w_input_gate.reshape(-1, width), w_decay_gate.reshape(-1, width)]
    )
    n_gate = gates.shape[0]
    pack = jnp.concatenate([w_signal.T, gates, small])
    pad = -pack.shape[0] % 16
    pack = jnp.pad(pack, ((0, pad), (0, 0)))
    (wide_s, wide_gates, wide_small), done = gather_absolute(
        ring, pack, (shard, n_gate, 1)
    )
    (wide_b,), done = gather_absolute(ring, w_branch.T, (shard,), done)
    (wide_o,), done = gather_absolute(ring, w_mixout, (shard,), done)
    wide_s = wide_s.reshape(channels, width)
    wide_b = wide_b.reshape(channels, width)
    wide_o = wide_o.reshape(channels, width)
    wide_gates = wide_gates.reshape(count, 2, heads_here, BLOCK // count, BLOCK)
    wide_ig = jnp.swapaxes(wide_gates[:, 0], 0, 1).reshape(heads_here, BLOCK, BLOCK)
    wide_dg = jnp.swapaxes(wide_gates[:, 1], 0, 1).reshape(heads_here, BLOCK, BLOCK)
    wide_small = wide_small[:, 0]
    n_gain = gain_mixer.shape[0]
    gain_one = wide_small[:, :n_gain].reshape(width).astype(F32)
    gain_two = wide_small[:, n_gain : 2 * n_gain].reshape(width).astype(F32)
    taps = wide_small[:, 2 * n_gain : 2 * n_gain + shard * CONV]
    taps = taps.reshape(channels, CONV).astype(F32)
    param = wide_small[:, 2 * n_gain + shard * CONV : n_small].reshape(channels).astype(F32)

    x_other = tensor_swap(block_input)
    dy_pairs, dy_far = ring.gather(after(cotangent, done))
    hid_g = fetch_hidden(after(w_gate.T, x_other))
    hid_u = fetch_hidden(after(w_up.T, hid_g))
    hid_d = fetch_hidden(after(w_down, hid_u))

    x_val = block_input.astype(F32)
    x_both = ordered(side, block_input, x_other).astype(F32)
    h_one = normed(x_both, gain_one).astype(BF16)
    signal = cols_inner(h_one, wide_s).astype(BF16)
    branch_pre = cols_inner(h_one, wide_b)
    branch, branch_back = jax.vjp(gelu_tanh, branch_pre)
    reset = starts.astype(F32)[:, None]
    cumulative = jnp.cumsum(starts)
    padded_cum = jnp.concatenate([jnp.zeros((lag,), jnp.int32), cumulative])
    masks = jnp.stack(
        [
            (cumulative - padded_cum[lag - k : lag - k + group] == 0).astype(F32)
            for k in range(CONV)
        ],
        axis=1,
    )
    tail_keep = (cumulative[group - 1] - cumulative[group - lag :] == 0)[:, None]
    rim = from_behind(signal[group - lag :] * tail_keep.astype(BF16), 1)
    padded = jnp.concatenate([rim, signal]).astype(F32)

    def conv_local(padded_in, taps_in):
        return conv_mix(padded_in, taps_in, masks)

    mixed_full, conv_back = jax.vjp(conv_local, padded, taps)
    mixed = mixed_full.astype(BF16)
    grouped = mixed.reshape(group, heads_here, BLOCK)
    gx_pre = jnp.einsum(
        "ghb,hbc->ghc", grouped, wide_ig, preferred_element_type=F32
    ).reshape(group, channels)
    ga_pre = jnp.einsum(
        "ghb,hbc->ghc", grouped, wide_dg, preferred_element_type=F32
    ).reshape(group, channels)

    def coeff_local(ga_in, gx_in, conv_in, param_in):
        return lru_coeffs(ga_in, gx_in, conv_in, param_in, reset)

    (decay, drive), coeff_back = jax.vjp(
        coeff_local, ga_pre, gx_pre, mixed.astype(F32), param
    )
    prods, local_state = local_scan(decay, drive, False)
    incoming = entering(prods[group - 1], local_state[group - 1], hops, False)
    state = local_state + prods * incoming[None, :]
    merged = (state * branch).astype(BF16)
    mine_at, theirs_at = side * rows, (1 - side) * rows
    mix_theirs = jnp.dot(
        lax.dynamic_slice_in_dim(merged, theirs_at, rows, 0),
        wide_o,
        preferred_element_type=F32,
    )
    mix_got = tensor_swap(mix_theirs.astype(BF16))
    mix_mine = jnp.dot(
        lax.dynamic_slice_in_dim(merged, mine_at, rows, 0),
        wide_o,
        preferred_element_type=F32,
    )
    x_one = x_val + mix_mine + mix_got.astype(F32)
    n_two, norm_two_back = jax.vjp(normed, x_one, gain_two)

    h_own = n_two.astype(BF16)
    h_pairs, h_far = ring.gather(h_own)

    def pieces(own, pairs, far):
        return [
            jnp.concatenate([own, *pairs[0]]),
            *(jnp.concatenate(pair) for pair in pairs[1:]),
            far,
        ]

    h_list = pieces(h_own, h_pairs, h_far)
    dy_list = pieces(cotangent, dy_pairs, dy_far)
    acts, d_gates, d_ups, d_hs, downs = [], [], [], [], []
    for h_piece, dy_piece in zip(h_list, dy_list):
        gate_pre = cols_inner(h_piece, hid_g)
        up_val = cols_inner(h_piece, hid_u)
        gate_act, gate_back = jax.vjp(gelu_tanh, gate_pre)
        acts.append((gate_act * up_val).astype(BF16))
        d_act = cols_inner(dy_piece, hid_d)
        d_gate = gate_back(d_act * up_val)[0].astype(BF16)
        d_up = (d_act * gate_act).astype(BF16)
        d_gates.append(d_gate)
        d_ups.append(d_up)
        d_hs.append(
            (
                jnp.dot(d_gate, hid_g, preferred_element_type=F32)
                + jnp.dot(d_up, hid_u, preferred_element_type=F32)
            ).astype(BF16)
        )
        downs.append(jnp.dot(acts[-1], hid_d, preferred_element_type=F32).astype(BF16))

    def chunks(parts):
        own = parts[0][:rows]
        pairs = [(parts[0][rows : 2 * rows], parts[0][2 * rows :])]
        pairs += [(p[:rows], p[rows:]) for p in parts[1:-1]]
        return own, pairs, parts[-1]

    d_h_two = ring.scatter(*chunks(d_hs))
    downs = after(downs, d_h_two)
    block_output = (x_one + ring.scatter(*chunks(downs))).astype(BF16)
    h_all = jnp.concatenate(h_list)
    dy_all = jnp.concatenate(dy_list)
    s_gate = reduce_hidden(rows_inner(jnp.concatenate(d_gates), h_all)).T
    s_up = reduce_hidden(rows_inner(jnp.concatenate(d_ups), h_all)).T
    s_down = reduce_hidden(rows_inner(jnp.concatenate(acts), dy_all))

    d_x_norm_two, g_gain_two = norm_two_back(d_h_two)
    d_x_one = cotangent.astype(F32) + d_x_norm_two
    dz_own = d_x_one.astype(BF16)
    d_mix = ordered(side, dz_own, tensor_swap(dz_own))
    g_mixout = rows_inner(merged, d_mix)
    s_mixout = scatter_absolute(ring, [g_mixout.reshape(count, shard, width)])
    d_merged = cols_inner(d_mix, wide_o)
    d_state = d_merged * branch
    d_branch = branch_back(d_merged * state)[0].astype(BF16)
    g_branch_rows = rows_inner(d_branch, h_one)
    s_branch = scatter_absolute(ring, [g_branch_rows.reshape(count, shard, width)]).T
    shifted = jnp.concatenate([decay[1:], jnp.ones((1, channels), F32)])
    rev_prods, rev_state = local_scan(shifted, d_state, True)
    later = entering(decay[0] * rev_prods[0], decay[0] * rev_state[0], hops, True)
    d_total = rev_state + rev_prods * later[None, :]
    previous = jnp.concatenate([incoming[None, :], state[:-1]])
    d_ga, d_gx, d_mixed_direct, g_param = coeff_back((d_total * previous, d_total))
    d_ga_low = d_ga.astype(BF16).reshape(group, heads_here, BLOCK)
    d_gx_low = d_gx.astype(BF16).reshape(group, heads_here, BLOCK)
    g_input_rows = jnp.einsum("ghb,ghc->bhc", grouped, d_gx_low, preferred_element_type=F32)
    g_decay_rows = jnp.einsum("ghb,ghc->bhc", grouped, d_ga_low, preferred_element_type=F32)
    d_back_gates = jnp.einsum(
        "ghc,hbc->ghb", d_gx_low, wide_ig, preferred_element_type=F32
    ) + jnp.einsum("ghc,hbc->ghb", d_ga_low, wide_dg, preferred_element_type=F32)
    d_mixed = d_mixed_direct + d_back_gates.reshape(group, channels)
    d_padded, g_taps = conv_back(d_mixed)
    back_rim = from_behind(d_padded[:lag], -1)
    d_sig_full = d_padded[lag:]
    d_sig_full = jnp.concatenate(
        [
            d_sig_full[: group - lag],
            d_sig_full[group - lag :] + back_rim * tail_keep.astype(F32),
        ]
    )
    d_signal = d_sig_full.astype(BF16)

    def d_h_rows(at):
        return jnp.dot(
            lax.dynamic_slice_in_dim(d_branch, at, rows, 0), wide_b, preferred_element_type=F32
        ) + jnp.dot(
            lax.dynamic_slice_in_dim(d_signal, at, rows, 0), wide_s, preferred_element_type=F32
        )

    d_h_got = tensor_swap(d_h_rows(theirs_at).astype(BF16))
    d_h_one = d_h_rows(mine_at) + d_h_got.astype(F32)
    _, norm_one_back = jax.vjp(normed, x_val, gain_one)
    d_x_norm_one, g_gain_one = norm_one_back(d_h_one)
    grad_input = d_x_one + d_x_norm_one

    g_signal_rows = rows_inner(d_signal, h_one).reshape(count, shard, width)
    gate_rows = jnp.concatenate(
        [
            g_input_rows.reshape(count, BLOCK // count, heads_here, BLOCK)
            .swapaxes(1, 2)
            .reshape(count, n_gate // 2, width),
            g_decay_rows.reshape(count, BLOCK // count, heads_here, BLOCK)
            .swapaxes(1, 2)
            .reshape(count, n_gate // 2, width),
        ],
        axis=1,
    )
    small_rows = jnp.concatenate(
        [g_taps.reshape(count, shard * CONV), g_param.reshape(count, shard)], axis=1
    )
    n_rows = small_rows.shape[1]
    small_rows = jnp.pad(small_rows, ((0, 0), (0, width - n_rows)))[:, None]
    last = scatter_absolute(ring, [g_signal_rows, gate_rows, small_rows])
    s_signal = last[:shard].T
    s_gates = last[shard : shard + n_gate].reshape(2, *w_input_gate.shape)
    s_taps = last[shard + n_gate, : shard * CONV].reshape(shard, CONV)
    s_param = last[shard + n_gate, shard * CONV : n_rows]
    gains = jnp.stack([g_gain_one, g_gain_two])
    gains = gains + tensor_swap(gains)
    gains = lax.psum_scatter(gains, "dp", scatter_dimension=1, tiled=True)
    return (
        block_output,
        grad_input,
        gains[0],
        s_branch,
        s_signal,
        s_gates[0],
        s_gates[1],
        s_taps,
        s_param,
        s_mixout,
        gains[1],
        s_gate,
        s_up,
        s_down,
    )


def solution(mesh):
    placed = (
        P(("dp", "tensor"), None),
        P("dp"),
        P(("dp", "tensor"), None),
        P("dp"),
        P(None, ("tensor", "dp")),
        P(None, ("tensor", "dp")),
        P("tensor", "dp", None),
        P("tensor", "dp", None),
        P(("tensor", "dp"), None),
        P(("tensor", "dp")),
        P(("tensor", "dp"), None),
        P("dp"),
        P(None, ("tensor", "dp")),
        P(None, ("tensor", "dp")),
        P(("tensor", "dp"), None),
    )
    return jax.shard_map(
        per_device,
        mesh=mesh,
        in_specs=placed,
        out_specs=(
            P(("dp", "tensor"), None),
            P(("dp", "tensor"), None),
            P("dp"),
            P(None, ("tensor", "dp")),
            P(None, ("tensor", "dp")),
            P("tensor", "dp", None),
            P("tensor", "dp", None),
            P(("tensor", "dp"), None),
            P(("tensor", "dp")),
            P(("tensor", "dp"), None),
            P("dp"),
            P(None, ("tensor", "dp")),
            P(None, ("tensor", "dp")),
            P(("tensor", "dp"), None),
        ),
        check_vma=False,
    )
```

time: 2990 us -> 923 us (0.31)
  waiting for transfers between devices: 2030 us -> 362 us
  blocking collectives: 271 us -> 0 us
  local copies, waits for them, and re-layouts: 337 us -> 115 us
  starting transfers between devices: 5.31 us -> 128 us
  matrix products: 191 us -> 151 us
    reduce_scatter x12 -> x0, waiting for transfers between devices: 1670 us -> none  [the longest x1 384 us: per_device(): lax.psum_scatter(g_down, 'dp', scatter_dimension=0, tiled=True)]
    all_gather x10 -> x0, waiting for transfers between devices: 361 us -> none  [the longest x1 104 us: fetch_dense(): lax.all_gather(w_gate, 'dp', axis=1, tiled=True)]
    ppermute x2 -> x134, waiting for transfers between devices: 0.55 us -> 302 us  [the longest x40 166 us: up(): return lax.ppermute(value, 'dp', self.up_route)]
    slice x111 -> x30, local copies, waits for them, and re-layouts: 205 us -> 19.5 us  [the longest x3 9.91 us: reduce_hidden(): mine = grad[:2 * size] + core_swap(grad[2 * size:].astype(BF16)).astype(F32)]
    all_gather x7 -> x0, blocking collectives: 141 us -> none  [the longest x4 78.3 us: entering(): gathered = jax.tree.map(lambda a: lax.all_gather(a, axis), part)]
    ppermute x2 -> x134, starting transfers between devices: 3.63 us -> 128 us  [the longest x40 48.8 us: up(): return lax.ppermute(value, 'dp', self.up_route)]
    unnamed x2 -> x0, blocking collectives: 124 us -> none
    pad x56 -> x0, local copies, waits for them, and re-layouts: 71.2 us -> none  [the longest x28 35.9 us: per_device(): prods, local_state = lax.associative_scan(affine, (decay, drive), axis=0)]
  transfers between devices with their start and end apart: 25 -> 135, of which waited for: 18 -> 47; matrix products, arithmetic and copies ran while one was open for 12% -> 37% of each run, Pallas kernels for 0% -> 0%
where the time goes in v1:
time: 923 us; the launch traced here: 913 us
  waiting for transfers between devices  362 us (39%)
  matrix products  151 us (16%)
  starting transfers between devices  128 us (14%)
  local copies, waits for them, and re-layouts  115 us (12%)
  other arithmetic  111 us (12%)
  between operations  43.4 us (5%)
    ppermute x40, waiting for transfers between devices, up(): return lax.ppermute(value, 'dp', self.up_route)  166 us
    ppermute x40, waiting for transfers between devices, down(): return lax.ppermute(value, 'dp', self.down_route)  67 us
    ppermute x11, waiting for transfers between devices, tensor_swap(): return lax.ppermute(value, 'tensor', [(0, 1), (1, 0)])  63.8 us
    unnamed x2, waiting for transfers between devices  59.3 us
    dot_general x15, matrix products, cols_inner(): lax.dot_general(left, right, (((1,), (1,)), ((), ())), preferred_element_...  51.4 us
    ppermute x40, starting transfers between devices, up(): return lax.ppermute(value, 'dp', self.up_route)  48.8 us
    ppermute x40, starting transfers between devices, down(): return lax.ppermute(value, 'dp', self.down_route)  44.1 us
    unnamed x296, local copies, waits for them, and re-layouts  34.6 us
  transfers between devices with their start and end apart: 135, of which 47 were waited for; matrix products, arithmetic and copies ran while one was open for 37% of the time, Pallas kernels for 0%

profile of v1, /device:TPU:0, one launch (start us, length us, event | category | flops | bytes accessed | tf_op | source)
XLA Modules:
  0.0 913.0 jit_solution(12287168625382036047)
XLA Ops:
  73.3 9.1 collective-permute-done.9
  82.4 5.0 collective-permute-done.11
  97.9 7.5 collective-permute-done.13
  130.0 4.8 convolution_convert_fusion.8
  161.6 4.6 collective-permute-start.19
  190.5 6.4 collective-permute-done.35
  212.4 6.5 multiply_convert_fusion.3
  223.5 7.2 collective-permute-done.47
  240.0 15.7 %collective-permute-done.51 = bf16[40,2560]{1,0:T(8,128)(2,1)S(1)} collective-permute-done((bf16[40,2560]{1,0:T(8,128)(2,1)S(1)}, bf16[40,2560]{1,0:T(8,128)(2,1)S(1)}, u32[]{:S(2)}, u32[]{:S(2)}) %collective-permute-start.51) | collective-permute-done | bytes 204832 | tf_op jit(solution)/shard_map/ppermute | solution.py:46
  264.7 34.6 %collective-permute-done.54 = bf16[128,2560]{1,0:T(8,128)(2,1)S(1)} collective-permute-done((bf16[128,2560]{1,0:T(8,128)(2,1)S(1)}, bf16[128,2560]{1,0:T(8,128)(2,1)S(1)}, u32[]{:S(2)}, u32[]{:S(2)}) %collective-permute-start.54) | collective-permute-done | bytes 655392 | tf_op jit(solution)/shard_map/ppermute | solution.py:87
  306.9 11.5 %collective-permute-done.55 = bf16[128,2560]{1,0:T(8,128)(2,1)S(1)} collective-permute-done((bf16[128,2560]{1,0:T(8,128)(2,1)S(1)}, bf16[128,2560]{1,0:T(8,128)(2,1)S(1)}, u32[]{:S(2)}, u32[]{:S(2)}) %collective-permute-start.55) | collective-permute-done | bytes 655392 | tf_op jit(solution)/shard_map/ppermute | solution.py:46
  320.6 12.4 %collective-permute-done.74 = bf16[128,2560]{1,0:T(8,128)(2,1)S(1)} collective-permute-done((bf16[128,2560]{1,0:T(8,128)(2,1)S(1)}, bf16[128,2560]{1,0:T(8,128)(2,1)S(1)}, u32[]{:S(2)}, u32[]{:S(2)}) %collective-permute-start.74) | collective-permute-done | bytes 655392 | tf_op jit(solution)/shard_map/ppermute | solution.py:49
  337.0 15.3 %collective-permute-done.75 = bf16[64,2560]{1,0:T(8,128)(2,1)S(1)} collective-permute-done((bf16[64,2560]{1,0:T(8,128)(2,1)S(1)}, bf16[64,2560]{1,0:T(8,128)(2,1)S(1)}, u32[]{:S(2)}, u32[]{:S(2)}) %collective-permute-start.75) | collective-permute-done | bytes 327712 | tf_op jit(solution)/shard_map/ppermute | solution.py:46
  356.0 4.8 fusion.229
  360.8 8.4 collective-permute-done.65
  373.7 4.8 fusion.231
  378.6 20.7 %collective-permute-done.61 = bf16[240,2560]{1,0:T(8,128)(2,1)S(1)} collective-permute-done((bf16[240,2560]{1,0:T(8,128)(2,1)S(1)}, bf16[240,2560]{1,0:T(8,128)(2,1)S(1)}, u32[]{:S(2)}, u32[]{:S(2)}) %collective-permute-start.61) | collective-permute-done | bytes 1228832 | tf_op jit(solution)/shard_map/ppermute | solution.py:87
  418.4 4.7 fusion.147
  444.4 7.0 fusion.49
  451.4 7.3 fusion.19
  464.9 10.2 %fusion.27 = f32[960,2560]{1,0:T(8,128)} fusion(bf16[1024,2560]{1,0:T(8,128)(2,1)} %copy-done.91, bf16[128,960]{0,1:T(8,128)(2,1)S(1)} %copy-done.79, bf16[256,960]{0,1:T(8,128)(2,1)S(1)} %copy-done.65, bf16[256,960]{0,1:T(8,128)(2,1)S(1)} %copy-done.67, bf16[384,960]{0,1:T(8,128)(2,1)S(1)} %get-tuple-element.124), kind=kOutput, calls=%fused_computation.74 | convolution fusion | flops 5041029120 | bytes 17039360 | tf_op jit(solution)/shard_map/dot_general | solution.py:143
  475.1 4.1 slice.849
  485.1 4.6 fusion.3
  489.8 10.5 %collective-permute-done.79 = bf16[128,2560]{1,0:T(8,128)(2,1)S(1)} collective-permute-done((bf16[128,2560]{1,0:T(8,128)(2,1)S(1)}, bf16[128,2560]{1,0:T(8,128)(2,1)S(1)}, u32[]{:S(2)}, u32[]{:S(2)}) %collective-permute-start.79) | collective-permute-done | bytes 655392 | tf_op jit(solution)/shard_map/ppermute | solution.py:49
  502.7 10.4 %fusion.35 = f32[960,2560]{1,0:T(8,128)} fusion(bf16[1024,2560]{1,0:T(8,128)(2,1)} %constant_dynamic-update-slice_fusion.31, bf16[128,960]{0,1:T(8,128)(2,1)S(1)} %copy-done.77, bf16[256,960]{0,1:T(8,128)(2,1)S(1)} %get-tuple-element.137, bf16[256,960]{0,1:T(8,128)(2,1)S(1)} %get-tuple-element.134, bf16[384,960]{0,1:T(8,128)(2,1)S(1)} %copy-done.115), kind=kOutput, calls=%fused_computation.82 | convolution fusion | flops 5041029120 | bytes 17039360 | tf_op jit(solution)/shard_map/dot_general | solution.py:143
  534.3 5.7 slice_add_fusion
  557.1 5.0 fusion.157
  572.0 5.2 fusion.159
  582.0 4.3 multiply_reduce_fusion
  626.0 4.8 fusion.6
  641.6 6.7 collective-permute-done.99
  652.3 5.3 fusion.72
  657.8 9.5 %collective-permute-done.90 = bf16[128,2560]{1,0:T(8,128)(2,1)S(1)} collective-permute-done((bf16[128,2560]{1,0:T(8,128)(2,1)S(1)}, bf16[128,2560]{1,0:T(8,128)(2,1)S(1)}, u32[]{:S(2)}, u32[]{:S(2)}) %collective-permute-start.90) | collective-permute-done | bytes 655392 | tf_op jit(solution)/shard_map/ppermute | solution.py:46
  672.7 59.3 %reduce-scatter.4.cloned.1.call-done = f32[160,2]{1,0:T(8,128)} async-done(((f32[2560,2]{1,0:T(8,128)}), f32[160,2]{1,0:T(8,128)}) %reduce-scatter.4.cloned.1.call-update) | async-done | bytes 1296
  740.3 4.1 fusion.11
  744.4 4.5 collective-permute-done.87
  749.0 5.1 collective-permute-done.91
  759.7 8.1 collective-permute-done.92
  790.7 5.4 collective-permute-done.103
  797.4 7.4 collective-permute-done.121
  814.3 5.1 constant_dynamic-slice_fusion.8
  819.4 4.3 collective-permute-done.111
  824.8 6.4 collective-permute-done.115
  837.3 17.6 %collective-permute-done.108 = bf16[80,2560]{1,0:T(8,128)(2,1)S(1)} collective-permute-done((bf16[80,2560]{1,0:T(8,128)(2,1)S(1)}, bf16[80,2560]{1,0:T(8,128)(2,1)S(1)}, u32[]{:S(2)}, u32[]{:S(2)}) %collective-permute-start.108) | collective-permute-done | bytes 409632 | tf_op jit(solution)/shard_map/ppermute | solution.py:46
  856.5 6.3 collective-permute-done.126
  867.1 8.1 collective-permute-done.109
  878.3 14.2 %collective-permute-done.117 = bf16[97,2560]{1,0:T(8,128)(2,1)S(1)} collective-permute-done((bf16[97,2560]{1,0:T(8,128)(2,1)S(1)}, bf16[97,2560]{1,0:T(8,128)(2,1)S(1)}, u32[]{:S(2)}, u32[]{:S(2)}) %collective-permute-start.117) | collective-permute-done | bytes 496672 | tf_op jit(solution)/shard_map/ppermute | solution.py:46
  894.3 7.6 collective-permute-done.118
  (828 shorter events, 421.4 us)
Async XLA Ops:
  7.2 724.7 %reduce-scatter.4.cloned.1.call-start = ((), (), s32[]{:S(2)}) async-start(), calls=%async_computation.1 | async-start | bytes 1392640
  12.6 38.6 %collective-permute-start.1 = (bf16[112,2560]{1,0:T(8,128)(2,1)}, bf16[112,2560]{1,0:T(8,128)(2,1)}, u32[]{:S(2)}, u32[]{:S(2)}) collective-permute-start(bf16[112,2560]{1,0:T(8,128)(2,1)} %fusion.138), channel_id=1, source_target_pairs={{0,8},{2,10},{8,16},{10,18},{16,24},{18,26},{24,28},{26,30},{28,20... | collective-permute-start | bytes 1720328 | tf_op jit(solution)/shard_map/ppermute | solution.py:46
  15.7 41.6 %collective-permute-start.3 = (bf16[112,2560]{1,0:T(8,128)(2,1)}, bf16[112,2560]{1,0:T(8,128)(2,1)}, u32[]{:S(2)}, u32[]{:S(2)}) collective-permute-start(bf16[112,2560]{1,0:T(8,128)(2,1)} %fusion.138), channel_id=1, source_target_pairs={{8,0},{10,2},{16,8},{18,10},{24,16},{26,18},{28,24},{30,26},{20,28... | collective-permute-start | bytes 1720328 | tf_op jit(solution)/shard_map/ppermute | solution.py:49
  15.7 33.5 %collective-permute-start = (bf16[112,2560]{1,0:T(8,128)(2,1)}, bf16[112,2560]{1,0:T(8,128)(2,1)S(1)}, u32[]{:S(2)}, u32[]{:S(2)}) collective-permute-start(bf16[112,2560]{1,0:T(8,128)(2,1)} %fusion.138), channel_id=1, source_target_pairs={{0,2},{2,0},{4,6},{6,4},{8,10},{10,8},{12,14},{14,12},{16,18},{18,... | collective-permute-start | bytes 1720328 | tf_op jit(solution)/shard_map/ppermute | solution.py:83
  15.7 42.3 %collective-permute-start.16 = (bf16[128,2560]{1,0:T(8,128)(2,1)}, bf16[128,2560]{1,0:T(8,128)(2,1)S(1)}, u32[]{:S(2)}, u32[]{:S(2)}) collective-permute-start(bf16[128,2560]{1,0:T(8,128)(2,1)} %param.17), channel_id=1, source_target_pairs={{0,1},{1,0},{2,3},{3,2},{4,5},{5,4},{6,7},{7,6},{8,9},{9,8},{10,11... | collective-permute-start | bytes 1966088 | tf_op jit(solution)/shard_map/ppermute | solution.py:87
  58.8 36.0 %collective-permute-start.57 = (bf16[240,2560]{1,0:T(8,128)(2,1)S(1)}, bf16[240,2560]{1,0:T(8,128)(2,1)S(1)}, u32[]{:S(2)}, u32[]{:S(2)}) collective-permute-start(bf16[240,2560]{1,0:T(8,128)(2,1)S(1)} %bitcast.422), channel_id=1, source_target_pairs={{0,1},{1,0},{2,3},{3,2},{4,5},{5,4},{6,7},{7,6},{8,9},{9,8},{10,11... | collective-permute-start | bytes 3686408 | tf_op jit(solution)/shard_map/ppermute | solution.py:87
  111.8 55.4 %collective-permute-start.27 = (bf16[80,2560]{1,0:T(8,128)(2,1)}, bf16[80,2560]{1,0:T(8,128)(2,1)}, u32[]{:S(2)}, u32[]{:S(2)}) collective-permute-start(bf16[80,2560]{1,0:T(8,128)(2,1)} %collective-permute-done.23), channel_id=1, source_target_pairs={{0,8},{2,10},{8,16},{10,18},{16,24},{18,26},{24,28},{26,30},{28,20... | collective-permute-start | bytes 1228808 | tf_op jit(solution)/shard_map/ppermute | solution.py:46
  115.5 53.2 %collective-permute-start.29 = (bf16[80,2560]{1,0:T(8,128)(2,1)}, bf16[80,2560]{1,0:T(8,128)(2,1)}, u32[]{:S(2)}, u32[]{:S(2)}) collective-permute-start(bf16[80,2560]{1,0:T(8,128)(2,1)} %collective-permute-done.25), channel_id=1, source_target_pairs={{8,0},{10,2},{16,8},{18,10},{24,16},{26,18},{28,24},{30,26},{20,28... | collective-permute-start | bytes 1228808 | tf_op jit(solution)/shard_map/ppermute | solution.py:49
  178.7 59.5 %collective-permute-start.58 = (bf16[480,2560]{1,0:T(8,128)(2,1)S(1)}, bf16[480,2560]{1,0:T(8,128)(2,1)S(1)}, u32[]{:S(2)}, u32[]{:S(2)}) collective-permute-start(bf16[480,2560]{1,0:T(8,128)(2,1)S(1)} %copy-done.56), channel_id=1, source_target_pairs={{0,2},{2,0},{4,6},{6,4},{8,10},{10,8},{12,14},{14,12},{16,18},{18,... | collective-permute-start | bytes 7372808 | tf_op jit(solution)/shard_map/ppermute | solution.py:83
  180.6 23.7 %collective-permute-start.38 = (bf16[80,2560]{1,0:T(8,128)(2,1)S(1)}, bf16[80,2560]{1,0:T(8,128)(2,1)S(1)}, u32[]{:S(2)}, u32[]{:S(2)}) collective-permute-start(bf16[80,2560]{1,0:T(8,128)(2,1)S(1)} %copy-done.73), channel_id=1, source_target_pairs={{0,2},{2,0},{4,6},{6,4},{8,10},{10,8},{12,14},{14,12},{16,18},{18,... | collective-permute-start | bytes 1228808 | tf_op jit(solution)/shard_map/ppermute | solution.py:83
  233.7 27.2 %collective-permute-start.70 = (bf16[128,2560]{1,0:T(8,128)(2,1)S(1)}, bf16[128,2560]{1,0:T(8,128)(2,1)S(1)}, u32[]{:S(2)}, u32[]{:S(2)}) collective-permute-start(bf16[128,2560]{1,0:T(8,128)(2,1)S(1)} %copy-done.23), channel_id=1, source_target_pairs={{8,0},{10,2},{16,8},{18,10},{24,16},{26,18},{28,24},{30,26},{20,28... | collective-permute-start | bytes 1966088 | tf_op jit(solution)/shard_map/ppermute | solution.py:49
  235.2 26.2 %collective-permute-start.69 = (bf16[128,2560]{1,0:T(8,128)(2,1)S(1)}, bf16[128,2560]{1,0:T(8,128)(2,1)S(1)}, u32[]{:S(2)}, u32[]{:S(2)}) collective-permute-start(bf16[128,2560]{1,0:T(8,128)(2,1)S(1)} %copy-done.23), channel_id=1, source_target_pairs={{0,8},{2,10},{8,16},{10,18},{16,24},{18,26},{24,28},{26,30},{28,20... | collective-permute-start | bytes 1966088 | tf_op jit(solution)/shard_map/ppermute | solution.py:46
  255.7 50.9 %collective-permute-start.59 = (bf16[240,2560]{1,0:T(8,128)(2,1)S(1)}, bf16[240,2560]{1,0:T(8,128)(2,1)S(1)}, u32[]{:S(2)}, u32[]{:S(2)}) collective-permute-start(bf16[240,2560]{1,0:T(8,128)(2,1)S(1)} %bitcast.426), channel_id=1, source_target_pairs={{0,1},{1,0},{2,3},{3,2},{4,5},{5,4},{6,7},{7,6},{8,9},{9,8},{10,11... | collective-permute-start | bytes 3686408 | tf_op jit(solution)/shard_map/ppermute | solution.py:87
  259.4 39.9 %collective-permute-start.54 = (bf16[128,2560]{1,0:T(8,128)(2,1)S(1)}, bf16[128,2560]{1,0:T(8,128)(2,1)S(1)}, u32[]{:S(2)}, u32[]{:S(2)}) collective-permute-start(bf16[128,2560]{1,0:T(8,128)(2,1)S(1)} %convolution_convert_fusion.7), channel_id=1, source_target_pairs={{0,1},{1,0},{2,3},{3,2},{4,5},{5,4},{6,7},{7,6},{8,9},{9,8},{10,11... | collective-permute-start | bytes 1966088 | tf_op jit(solution)/shard_map/ppermute | solution.py:87
  260.9 41.9 %collective-permute-start.72 = (bf16[128,2560]{1,0:T(8,128)(2,1)S(1)}, bf16[128,2560]{1,0:T(8,128)(2,1)S(1)}, u32[]{:S(2)}, u32[]{:S(2)}) collective-permute-start(bf16[128,2560]{1,0:T(8,128)(2,1)S(1)} %collective-permute-done.70), channel_id=1, source_target_pairs={{8,0},{10,2},{16,8},{18,10},{24,16},{26,18},{28,24},{30,26},{20,28... | collective-permute-start | bytes 1966088 | tf_op jit(solution)/shard_map/ppermute | solution.py:49
  261.4 41.9 %collective-permute-start.71 = (bf16[128,2560]{1,0:T(8,128)(2,1)S(1)}, bf16[128,2560]{1,0:T(8,128)(2,1)S(1)}, u32[]{:S(2)}, u32[]{:S(2)}) collective-permute-start(bf16[128,2560]{1,0:T(8,128)(2,1)S(1)} %collective-permute-done.69), channel_id=1, source_target_pairs={{0,8},{2,10},{8,16},{10,18},{16,24},{18,26},{24,28},{26,30},{28,20... | collective-permute-start | bytes 1966088 | tf_op jit(solution)/shard_map/ppermute | solution.py:46
  302.8 30.2 %collective-permute-start.74 = (bf16[128,2560]{1,0:T(8,128)(2,1)S(1)}, bf16[128,2560]{1,0:T(8,128)(2,1)S(1)}, u32[]{:S(2)}, u32[]{:S(2)}) collective-permute-start(bf16[128,2560]{1,0:T(8,128)(2,1)S(1)} %collective-permute-done.72), channel_id=1, source_target_pairs={{8,0},{10,2},{16,8},{18,10},{24,16},{26,18},{28,24},{30,26},{20,28... | collective-permute-start | bytes 1966088 | tf_op jit(solution)/shard_map/ppermute | solution.py:49
  303.3 31.3 %collective-permute-start.73 = (bf16[128,2560]{1,0:T(8,128)(2,1)S(1)}, bf16[128,2560]{1,0:T(8,128)(2,1)S(1)}, u32[]{:S(2)}, u32[]{:S(2)}) collective-permute-start(bf16[128,2560]{1,0:T(8,128)(2,1)S(1)} %collective-permute-done.71), channel_id=1, source_target_pairs={{0,8},{2,10},{8,16},{10,18},{16,24},{18,26},{24,28},{26,30},{28,20... | collective-permute-start | bytes 1966088 | tf_op jit(solution)/shard_map/ppermute | solution.py:46
  306.8 65.0 %collective-permute-start.60 = (bf16[480,2560]{1,0:T(8,128)(2,1)S(1)}, bf16[480,2560]{1,0:T(8,128)(2,1)S(1)}, u32[]{:S(2)}, u32[]{:S(2)}) collective-permute-start(bf16[480,2560]{1,0:T(8,128)(2,1)S(1)} %pad_maximum_fusion.1), channel_id=1, source_target_pairs={{0,2},{2,0},{4,6},{6,4},{8,10},{10,8},{12,14},{14,12},{16,18},{18,... | collective-permute-start | bytes 7372808 | tf_op jit(solution)/shard_map/ppermute | solution.py:83
  318.4 35.4 %collective-permute-start.63 = (bf16[128,2560]{1,0:T(8,128)(2,1)S(1)}, bf16[128,2560]{1,0:T(8,128)(2,1)S(1)}, u32[]{:S(2)}, u32[]{:S(2)}) collective-permute-start(bf16[128,2560]{1,0:T(8,128)(2,1)S(1)} %collective-permute-done.55), channel_id=1, source_target_pairs={{0,8},{2,10},{8,16},{10,18},{16,24},{18,26},{24,28},{26,30},{28,20... | collective-permute-start | bytes 1966088 | tf_op jit(solution)/shard_map/ppermute | solution.py:46
  319.0 35.6 %collective-permute-start.64 = (bf16[128,2560]{1,0:T(8,128)(2,1)S(1)}, bf16[128,2560]{1,0:T(8,128)(2,1)S(1)}, u32[]{:S(2)}, u32[]{:S(2)}) collective-permute-start(bf16[128,2560]{1,0:T(8,128)(2,1)S(1)} %collective-permute-done.56), channel_id=1, source_target_pairs={{8,0},{10,2},{16,8},{18,10},{24,16},{26,18},{28,24},{30,26},{20,28... | collective-permute-start | bytes 1966088 | tf_op jit(solution)/shard_map/ppermute | solution.py:49
  373.0 26.3 %collective-permute-start.61 = (bf16[240,2560]{1,0:T(8,128)(2,1)S(1)}, bf16[240,2560]{1,0:T(8,128)(2,1)S(1)}, u32[]{:S(2)}, u32[]{:S(2)}) collective-permute-start(bf16[240,2560]{1,0:T(8,128)(2,1)S(1)} %copy-done.45), channel_id=1, source_target_pairs={{0,1},{1,0},{2,3},{3,2},{4,5},{5,4},{6,7},{7,6},{8,9},{9,8},{10,11... | collective-permute-start | bytes 3686408 | tf_op jit(solution)/shard_map/ppermute | solution.py:87
  427.5 33.9 %collective-permute-start.77 = (bf16[64,2560]{1,0:T(8,128)(2,1)S(1)}, bf16[64,2560]{1,0:T(8,128)(2,1)}, u32[]{:S(2)}, u32[]{:S(2)}) collective-permute-start(bf16[64,2560]{1,0:T(8,128)(2,1)S(1)} %get-tuple-element.229), channel_id=1, source_target_pairs={{8,0},{10,2},{16,8},{18,10},{24,16},{26,18},{28,24},{30,26},{20,28... | collective-permute-start | bytes 983048 | tf_op jit(solution)/shard_map/ppermute | solution.py:49
  427.9 33.5 %collective-permute-start.81 = (bf16[64,2560]{1,0:T(8,128)(2,1)S(1)}, bf16[64,2560]{1,0:T(8,128)(2,1)}, u32[]{:S(2)}, u32[]{:S(2)}) collective-permute-start(bf16[64,2560]{1,0:T(8,128)(2,1)S(1)} %get-tuple-element.230), channel_id=1, source_target_pairs={{0,8},{2,10},{8,16},{10,18},{16,24},{18,26},{24,28},{26,30},{28,20... | collective-permute-start | bytes 983048 | tf_op jit(solution)/shard_map/ppermute | solution.py:46
  460.5 64.0 %collective-permute-start.128 = (bf16[480,2560]{1,0:T(8,128)(2,1)}, bf16[480,2560]{1,0:T(8,128)(2,1)S(1)}, u32[]{:S(2)}, u32[]{:S(2)}) collective-permute-start(bf16[480,2560]{1,0:T(8,128)(2,1)} %slice.850), channel_id=1, source_target_pairs={{0,2},{2,0},{4,6},{6,4},{8,10},{10,8},{12,14},{14,12},{16,18},{18,... | collective-permute-start | bytes 7372808 | tf_op jit(solution)/shard_map/ppermute | solution.py:83
  479.2 48.3 %collective-permute-start.130 = (bf16[480,2560]{1,0:T(8,128)(2,1)}, bf16[480,2560]{1,0:T(8,128)(2,1)}, u32[]{:S(2)}, u32[]{:S(2)}) collective-permute-start(bf16[480,2560]{1,0:T(8,128)(2,1)} %slice.849), channel_id=1, source_target_pairs={{0,2},{2,0},{4,6},{6,4},{8,10},{10,8},{12,14},{14,12},{16,18},{18,... | collective-permute-start | bytes 7372808 | tf_op jit(solution)/shard_map/ppermute | solution.py:83
  528.8 205.5 %collective-permute-start.129 = (bf16[240,2560]{1,0:T(8,128)(2,1)}, bf16[240,2560]{1,0:T(8,128)(2,1)}, u32[]{:S(2)}, u32[]{:S(2)}) collective-permute-start(bf16[240,2560]{1,0:T(8,128)(2,1)} %slice.853), channel_id=1, source_target_pairs={{0,1},{1,0},{2,3},{3,2},{4,5},{5,4},{6,7},{7,6},{8,9},{9,8},{10,11... | collective-permute-start | bytes 3686408 | tf_op jit(solution)/shard_map/ppermute | solution.py:87
  551.5 25.7 %collective-permute-start.94 = (f32[2,1280]{1,0:T(2,128)S(1)}, f32[2,1280]{1,0:T(2,128)S(1)}, u32[]{:S(2)}, u32[]{:S(2)}) collective-permute-start(f32[2,1280]{1,0:T(2,128)S(1)} %pad_maximum_fusion.40), channel_id=1, source_target_pairs={{2,0},{4,2},{6,4},{8,6},{10,8},{12,10},{14,12},{16,14},{18,16},{20... | collective-permute-start | bytes 30728 | tf_op jit(solution)/shard_map/ppermute | solution.py:97
  552.8 24.9 %collective-permute-start.95 = (f32[2,1280]{1,0:T(2,128)S(1)}, f32[2,1280]{1,0:T(2,128)S(1)}, u32[]{:S(2)}, u32[]{:S(2)}) collective-permute-start(f32[2,1280]{1,0:T(2,128)S(1)} %pad_maximum_fusion.40), channel_id=1, source_target_pairs={{4,0},{6,2},{8,4},{10,6},{12,8},{14,10},{16,12},{18,14},{20,16},{2... | collective-permute-start | bytes 30728 | tf_op jit(solution)/shard_map/ppermute | solution.py:97
  554.1 25.1 %collective-permute-start.96 = (f32[2,1280]{1,0:T(2,128)S(1)}, f32[2,1280]{1,0:T(2,128)S(1)}, u32[]{:S(2)}, u32[]{:S(2)}) collective-permute-start(f32[2,1280]{1,0:T(2,128)S(1)} %pad_maximum_fusion.40), channel_id=1, source_target_pairs={{6,0},{8,2},{10,4},{12,6},{14,8},{16,10},{18,12},{20,14},{22,16},{... | collective-permute-start | bytes 30728 | tf_op jit(solution)/shard_map/ppermute | solution.py:97
  555.4 26.5 %collective-permute-start.97 = (f32[2,1280]{1,0:T(2,128)S(1)}, f32[2,1280]{1,0:T(2,128)S(1)}, u32[]{:S(2)}, u32[]{:S(2)}) collective-permute-start(f32[2,1280]{1,0:T(2,128)S(1)} %pad_maximum_fusion.40), channel_id=1, source_target_pairs={{8,0},{10,2},{12,4},{14,6},{16,8},{18,10},{20,12},{22,14},{24,16},... | collective-permute-start | bytes 30728 | tf_op jit(solution)/shard_map/ppermute | solution.py:97
  577.2 162.3 %collective-permute-start.131 = (bf16[240,2560]{1,0:T(8,128)(2,1)}, bf16[240,2560]{1,0:T(8,128)(2,1)}, u32[]{:S(2)}, u32[]{:S(2)}) collective-permute-start(bf16[240,2560]{1,0:T(8,128)(2,1)} %slice.852), channel_id=1, source_target_pairs={{0,1},{1,0},{2,3},{3,2},{4,5},{5,4},{6,7},{7,6},{8,9},{9,8},{10,11... | collective-permute-start | bytes 3686408 | tf_op jit(solution)/shard_map/ppermute | solution.py:87
  577.7 177.5 %collective-permute-start.133 = (bf16[240,2560]{1,0:T(8,128)(2,1)}, bf16[240,2560]{1,0:T(8,128)(2,1)}, u32[]{:S(2)}, u32[]{:S(2)}) collective-permute-start(bf16[240,2560]{1,0:T(8,128)(2,1)} %slice.851), channel_id=1, source_target_pairs={{0,1},{1,0},{2,3},{3,2},{4,5},{5,4},{6,7},{7,6},{8,9},{9,8},{10,11... | collective-permute-start | bytes 3686408 | tf_op jit(solution)/shard_map/ppermute | solution.py:87
  579.2 78.5 %collective-permute-start.86 = (bf16[128,2560]{1,0:T(8,128)(2,1)}, bf16[128,2560]{1,0:T(8,128)(2,1)}, u32[]{:S(2)}, u32[]{:S(2)}) collective-permute-start(bf16[128,2560]{1,0:T(8,128)(2,1)} %pad_maximum_fusion.22), channel_id=1, source_target_pairs={{8,0},{10,2},{16,8},{18,10},{24,16},{26,18},{28,24},{30,26},{20,28... | collective-permute-start | bytes 1966088 | tf_op jit(solution)/shard_map/ppermute | solution.py:49
  657.7 113.2 %collective-permute-start.101 = (bf16[8,80,2560]{2,1,0:T(8,128)(2,1)}, bf16[8,80,2560]{2,1,0:T(8,128)(2,1)}, u32[]{:S(2)}, u32[]{:S(2)}) collective-permute-start(bf16[8,80,2560]{2,1,0:T(8,128)(2,1)} %dynamic-slice_bitcast_fusion.2), channel_id=1, source_target_pairs={{0,2},{2,0},{4,6},{6,4},{8,10},{10,8},{12,14},{14,12},{16,18},{18,... | collective-permute-start | bytes 9830408 | tf_op jit(solution)/shard_map/ppermute | solution.py:83
  671.1 105.0 %collective-permute-start.119 = (bf16[8,80,2560]{2,1,0:T(8,128)(2,1)}, bf16[8,80,2560]{2,1,0:T(8,128)(2,1)}, u32[]{:S(2)}, u32[]{:S(2)}) collective-permute-start(bf16[8,80,2560]{2,1,0:T(8,128)(2,1)} %dynamic-slice_bitcast_fusion.1), channel_id=1, source_target_pairs={{0,2},{2,0},{4,6},{6,4},{8,10},{10,8},{12,14},{14,12},{16,18},{18,... | collective-permute-start | bytes 9830408 | tf_op jit(solution)/shard_map/ppermute | solution.py:83
  749.0 57.5 %collective-permute-start.110 = (bf16[8,97,2560]{2,0,1:T(8,128)(2,1)}, bf16[8,97,2560]{2,0,1:T(8,128)(2,1)}, u32[]{:S(2)}, u32[]{:S(2)}) collective-permute-start(bf16[8,97,2560]{2,0,1:T(8,128)(2,1)} %dynamic-slice_bitcast_fusion), channel_id=1, source_target_pairs={{0,2},{2,0},{4,6},{6,4},{8,10},{10,8},{12,14},{14,12},{16,18},{18,... | collective-permute-start | bytes 11919368 | tf_op jit(solution)/shard_map/ppermute | solution.py:83
  784.9 48.6 %collective-permute-start.107 = (bf16[80,2560]{1,0:T(8,128)(2,1)S(1)}, bf16[80,2560]{1,0:T(8,128)(2,1)S(1)}, u32[]{:S(2)}, u32[]{:S(2)}) collective-permute-start(bf16[80,2560]{1,0:T(8,128)(2,1)S(1)} %pad_maximum_fusion.27), channel_id=1, source_target_pairs={{0,8},{2,10},{8,16},{10,18},{16,24},{18,26},{24,28},{26,30},{28,20... | collective-permute-start | bytes 1228808 | tf_op jit(solution)/shard_map/ppermute | solution.py:46
  790.1 44.9 %collective-permute-start.125 = (bf16[80,2560]{1,0:T(8,128)(2,1)S(1)}, bf16[80,2560]{1,0:T(8,128)(2,1)S(1)}, u32[]{:S(2)}, u32[]{:S(2)}) collective-permute-start(bf16[80,2560]{1,0:T(8,128)(2,1)S(1)} %pad_maximum_fusion.29), channel_id=1, source_target_pairs={{0,8},{2,10},{8,16},{10,18},{16,24},{18,26},{24,28},{26,30},{28,20... | collective-permute-start | bytes 1228808 | tf_op jit(solution)/shard_map/ppermute | solution.py:46
  796.1 37.5 %collective-permute-start.104 = (bf16[80,2560]{1,0:T(8,128)(2,1)S(1)}, bf16[80,2560]{1,0:T(8,128)(2,1)S(1)}, u32[]{:S(2)}, u32[]{:S(2)}) collective-permute-start(bf16[80,2560]{1,0:T(8,128)(2,1)S(1)} %fusion.124), channel_id=1, source_target_pairs={{8,0},{10,2},{16,8},{18,10},{24,16},{26,18},{28,24},{30,26},{20,28... | collective-permute-start | bytes 1228808 | tf_op jit(solution)/shard_map/ppermute | solution.py:49
  804.9 31.0 %collective-permute-start.122 = (bf16[80,2560]{1,0:T(8,128)(2,1)S(1)}, bf16[80,2560]{1,0:T(8,128)(2,1)S(1)}, u32[]{:S(2)}, u32[]{:S(2)}) collective-permute-start(bf16[80,2560]{1,0:T(8,128)(2,1)S(1)} %fusion.119), channel_id=1, source_target_pairs={{8,0},{10,2},{16,8},{18,10},{24,16},{26,18},{28,24},{30,26},{20,28... | collective-permute-start | bytes 1228808 | tf_op jit(solution)/shard_map/ppermute | solution.py:49
  831.2 32.3 %collective-permute-start.112 = (bf16[97,2560]{1,0:T(8,128)(2,1)S(1)}, bf16[97,2560]{1,0:T(8,128)(2,1)S(1)}, u32[]{:S(2)}, u32[]{:S(2)}) collective-permute-start(bf16[97,2560]{1,0:T(8,128)(2,1)S(1)} %pad_maximum_fusion.24), channel_id=1, source_target_pairs={{8,0},{10,2},{16,8},{18,10},{24,16},{26,18},{28,24},{30,26},{20,28... | collective-permute-start | bytes 1489928 | tf_op jit(solution)/shard_map/ppermute | solution.py:49
  833.5 31.4 %collective-permute-start.116 = (bf16[97,2560]{1,0:T(8,128)(2,1)S(1)}, bf16[97,2560]{1,0:T(8,128)(2,1)S(1)}, u32[]{:S(2)}, u32[]{:S(2)}) collective-permute-start(bf16[97,2560]{1,0:T(8,128)(2,1)S(1)} %pad_maximum_fusion.25), channel_id=1, source_target_pairs={{0,8},{2,10},{8,16},{10,18},{16,24},{18,26},{24,28},{26,30},{28,20... | collective-permute-start | bytes 1489928 | tf_op jit(solution)/shard_map/ppermute | solution.py:46
  835.1 30.8 %collective-permute-start.105 = (bf16[80,2560]{1,0:T(8,128)(2,1)S(1)}, bf16[80,2560]{1,0:T(8,128)(2,1)S(1)}, u32[]{:S(2)}, u32[]{:S(2)}) collective-permute-start(bf16[80,2560]{1,0:T(8,128)(2,1)S(1)} %get-tuple-element.115), channel_id=1, source_target_pairs={{8,0},{10,2},{16,8},{18,10},{24,16},{26,18},{28,24},{30,26},{20,28... | collective-permute-start | bytes 1228808 | tf_op jit(solution)/shard_map/ppermute | solution.py:49
  836.1 26.7 %collective-permute-start.126 = (bf16[80,2560]{1,0:T(8,128)(2,1)S(1)}, bf16[80,2560]{1,0:T(8,128)(2,1)S(1)}, u32[]{:S(2)}, u32[]{:S(2)}) collective-permute-start(bf16[80,2560]{1,0:T(8,128)(2,1)S(1)} %get-tuple-element.108), channel_id=1, source_target_pairs={{0,8},{2,10},{8,16},{10,18},{16,24},{18,26},{24,28},{26,30},{28,20... | collective-permute-start | bytes 1228808 | tf_op jit(solution)/shard_map/ppermute | solution.py:46
  854.9 38.3 %collective-permute-start.123 = (bf16[80,2560]{1,0:T(8,128)(2,1)S(1)}, bf16[80,2560]{1,0:T(8,128)(2,1)S(1)}, u32[]{:S(2)}, u32[]{:S(2)}) collective-permute-start(bf16[80,2560]{1,0:T(8,128)(2,1)S(1)} %get-tuple-element.107), channel_id=1, source_target_pairs={{8,0},{10,2},{16,8},{18,10},{24,16},{26,18},{28,24},{30,26},{20,28... | collective-permute-start | bytes 1228808 | tf_op jit(solution)/shard_map/ppermute | solution.py:49
  863.5 29.7 %collective-permute-start.127 = (bf16[80,2560]{1,0:T(8,128)(2,1)S(1)}, bf16[80,2560]{1,0:T(8,128)(2,1)S(1)}, u32[]{:S(2)}, u32[]{:S(2)}) collective-permute-start(bf16[80,2560]{1,0:T(8,128)(2,1)S(1)} %fusion.118), channel_id=1, source_target_pairs={{0,8},{2,10},{8,16},{10,18},{16,24},{18,26},{24,28},{26,30},{28,20... | collective-permute-start | bytes 1228808 | tf_op jit(solution)/shard_map/ppermute | solution.py:46
  865.9 26.6 %collective-permute-start.117 = (bf16[97,2560]{1,0:T(8,128)(2,1)S(1)}, bf16[97,2560]{1,0:T(8,128)(2,1)S(1)}, u32[]{:S(2)}, u32[]{:S(2)}) collective-permute-start(bf16[97,2560]{1,0:T(8,128)(2,1)S(1)} %fusion.88), channel_id=1, source_target_pairs={{0,8},{2,10},{8,16},{10,18},{16,24},{18,26},{24,28},{26,30},{28,20... | collective-permute-start | bytes 1489928 | tf_op jit(solution)/shard_map/ppermute | solution.py:46
  (217 other events, 3332.6 us)
Sparse Core Ops, SparseCore 0:
  672.8 59.1 reduce-scatter.3

commit v2 on v0

v2 whole, which is shorter than its diff:
```python
import functools

import jax
import jax.numpy as jnp
from jax import lax
from jax.experimental import pallas as pl
from jax.experimental.pallas import tpu as pltpu
from jax.sharding import PartitionSpec as P

BLOCK = 256
CONV = 4
MAXLEN = 1024
EPS = 1e-06
HALO = 16
BF16 = jnp.bfloat16
F32 = jnp.float32


def ring_order(chips):
    return list(range(0, chips, 2)) + list(range(chips - 1, 0, -2))


class Ring:
    def __init__(self):
        count = lax.axis_size("dp")
        self.chips = count // 2
        self.reach = self.chips // 2
        order = ring_order(self.chips)
        self.up_route = [
            (order[p] * 2 + c, order[(p + 1) % self.chips] * 2 + c)
            for p in range(self.chips)
            for c in range(2)
        ]
        self.down_route = [(b, a) for a, b in self.up_route]
        me = lax.axis_index("dp")
        chip = me // 2
        self.core = lax.rem(me, 2)
        self.place = jnp.where(
            lax.rem(chip, 2) == 0, chip // 2, self.chips - 1 - chip // 2
        )

    def chip_at(self, distance):
        p = lax.rem(self.place - distance + self.chips, self.chips)
        return jnp.where(p < self.reach, 2 * p, 2 * (self.chips - 1 - p) + 1)

    def up(self, value):
        return lax.ppermute(value, "dp", self.up_route)

    def down(self, value):
        return lax.ppermute(value, "dp", self.down_route)


class Order:
    def __init__(self):
        self.token = None

    def tie(self, *values):
        if self.token is not None:
            values = lax.optimization_barrier((values, self.token))[0]
        return values if len(values) > 1 else values[0]

    def arrive(self, *values):
        values = lax.optimization_barrier((values, self.token))[0]
        self.token = values[-1]
        return values if len(values) > 1 else values[0]

    def run(self, function, *values):
        values = self.tie(*values)
        out = function(*values) if isinstance(values, tuple) else function(values)
        self.token = jax.tree.leaves(out)[-1]
        return out


SHOWN = 4


class Gather:
    def __init__(self, ring, order, value, both_cores=False):
        self.ring, self.order = ring, order
        self.own = value
        self.half = value.shape[0] // 32 * 16 or value.shape[0] // 2
        self.flight = (value, value)
        self.pairs, self.far = [], None
        self.theirs = [] if both_cores else None
        self.steps = 0

    def start(self):
        if self.theirs is not None:
            self.theirs.append((core_swap(self.own),))
        self.send()
        for _ in range(self.ring.reach - SHOWN):
            self.next()

    def send(self):
        self.steps += 1
        u, d = self.order.tie(*self.flight)
        if self.steps == self.ring.reach:
            u, d = u[: self.half], d[self.half :]
        self.flight = (self.ring.up(u), self.ring.down(d))

    def land(self):
        self.flight = self.order.arrive(*self.flight)
        if self.theirs is not None:
            self.theirs.append(tuple(core_swap(v) for v in self.flight))

    def next(self):
        self.land()
        self.pairs.append(self.flight)
        self.send()

    def finish(self):
        self.land()
        self.far = self.flight


class Scatter:
    def __init__(self, ring, order, parts, half):
        self.ring, self.order = ring, order
        self.parts, self.half = list(parts), half
        self.steps = 0

    def start(self):
        far = self.parts.pop()
        self.flight = self.order.run(
            lambda *v: (far(v, 0, self.half), far(v, self.half, None)), *far.values
        )
        self.send()
        for _ in range(self.ring.reach - SHOWN):
            self.next()

    def send(self):
        self.steps += 1
        u, d = self.order.tie(*self.flight)
        self.flight = (self.ring.down(u), self.ring.up(d))

    def next(self):
        ahead, behind = self.parts.pop(), self.parts.pop()
        half, first = self.half, self.steps == 1

        def add(to_down, to_up, *values):
            u_values, d_values = values[: len(behind.values)], values[len(behind.values) :]
            if first:
                return (
                    jnp.concatenate(
                        [behind(u_values, 0, half, to_down), behind(u_values, half, None)]
                    ),
                    jnp.concatenate(
                        [ahead(d_values, 0, half), ahead(d_values, half, None, to_up)]
                    ),
                )
            return behind(u_values, 0, None, to_down), ahead(d_values, 0, None, to_up)

        self.flight = self.order.run(add, *self.flight, *behind.values, *ahead.values)
        self.send()

    def finish(self, function=None, *more):
        own = self.parts.pop()

        def total(to_down, to_up, *values):
            count = len(own.values)
            out = own(values[:count], 0, None, to_down, to_up, F32)
            return function(out, *values[count:]) if function else out

        return self.order.run(total, *self.flight, *own.values, *more)


class Part:
    def __init__(self, cut, *values):
        self.cut, self.values = cut, values

    def __call__(self, values, first, last, *others):
        dtype = BF16
        if others and others[-1] is F32:
            others, dtype = others[:-1], F32
        total = self.cut(*values)[first:last]
        for other in others:
            total = total + other.astype(F32)
        return total.astype(dtype)


def plain_parts(values):
    return [Part(lambda v: v.astype(F32), value) for value in values]


def plus(a, b):
    return (a.astype(F32) + b.astype(F32)).astype(BF16)


def core_swap(value):
    count = lax.axis_size("dp")
    return lax.ppermute(value, "dp", [(i, i ^ 1) for i in range(count)])


def tensor_swap(value):
    return lax.ppermute(value, "tensor", [(0, 1), (1, 0)])


def from_behind(block, distance):
    devices = range(lax.axis_size("dp"))
    route = [(i - distance, i) for i in devices if i - distance in devices]
    return lax.ppermute(block, "dp", route)


class Entering:
    def __init__(self, order, window, hops, reverse):
        self.order, self.sign = order, (-1 if reverse else 1)
        size = 1
        while 4 * size < hops:
            window = follow(from_behind(window, self.sign * size), window)
            size *= 2
        self.size, self.hops, self.window = size, hops, window
        if size < hops:
            self.behind = from_behind(window, self.sign * size)

    def next(self):
        if 2 * self.size < self.hops:
            self.window = self.order.run(follow, self.behind, self.window)
            self.size *= 2
        self.near = from_behind(self.window, self.sign)
        if self.size < self.hops:
            self.rest = from_behind(self.window, self.sign * (1 + self.size))

    def finish(self):
        if self.size >= self.hops:
            return self.order.arrive(self.near)[1:]
        return self.order.run(lambda n, r: n[:1] * r[1:] + n[1:], self.near, self.rest)


def follow(first, second):
    return jnp.stack([first[0] * second[0], second[0] * first[1] + second[1]])


def normed(value, gain):
    return value * lax.rsqrt(jnp.mean(value * value, axis=-1, keepdims=True) + EPS) * gain


def gelu_tanh(value):
    return jax.nn.gelu(value, approximate=True)


GELU_IN = 0.7978845608028654
GELU_CUBE = 0.044715


def gelu_and_slope(value):
    square = value * value
    t = jnp.tanh(GELU_IN * (value + GELU_CUBE * (square * value)))
    half = 0.5 * (1.0 + t)
    slope = half + 0.5 * value * (1.0 - t * t) * (GELU_IN * (1.0 + 3.0 * GELU_CUBE * square))
    return value * half, slope


def rows_inner(left, right):
    return lax.dot_general(
        left, right, (((0,), (0,)), ((), ())), preferred_element_type=F32
    )


def cols_inner(left, right):
    return lax.dot_general(
        left, right, (((1,), (1,)), ((), ())), preferred_element_type=F32
    )


def scan_rows(reverse, a_ref, b_ref, p_ref, s_ref):
    rows, width = a_ref.shape
    blocks = rows // 8
    row = lax.broadcasted_iota(jnp.int32, (8, width), 0)

    def step(i, carry):
        p_in, s_in = carry
        at = (blocks - 1 - i) if reverse else i
        here = pl.ds(pl.multiple_of(at * 8, 8), 8)
        a = a_ref[here, :]
        b = b_ref[here, :]
        for shift in (1, 2, 4):
            turn = 8 - shift if reverse else shift
            inside = (row < 8 - shift) if reverse else (row >= shift)
            a_prev = jnp.where(inside, pltpu.roll(a, turn, 0), 1.0)
            b_prev = jnp.where(inside, pltpu.roll(b, turn, 0), 0.0)
            b = a * b_prev + b
            a = a * a_prev
        b = b + a * s_in
        a = a * p_in
        p_ref[here, :] = a
        s_ref[here, :] = b
        last = 0 if reverse else 7
        return (a[last : last + 1], b[last : last + 1])

    return lax.fori_loop(
        0, blocks, step, (jnp.ones((1, width), F32), jnp.zeros((1, width), F32))
    )


def lru_gates(mixed, w_ig, w_dg, param):
    gx_pre = jnp.dot(mixed, w_ig, preferred_element_type=F32)
    ga_pre = jnp.dot(mixed, w_dg, preferred_element_type=F32)
    return jax.nn.sigmoid(gx_pre), jax.nn.sigmoid(ga_pre), jax.nn.softplus(param)


def one_minus_square(log_a, e):
    x = 2.0 * log_a
    series = -x * (
        1.0 + x * (1 / 2 + x * (1 / 6 + x * (1 / 24 + x * (1 / 120 + x * (1 / 720)))))
    )
    return jnp.where(x > -0.3, series, 1.0 - e * e)


def mix_body(pad_ref, marks_ref, params_ref, ig_ref, dg_ref, *refs):
    mixed_ref, decay_ref, prods_ref, state_ref, ends_ref, a_scr, b_scr = refs
    block = pl.program_id(0)
    rows = mixed_ref.shape[0]
    pad = pad_ref[...].astype(F32)
    total = params_ref[0:1, :] * pad[HALO:] * marks_ref[:, 0:1]
    for k in range(1, CONV):
        behind = pltpu.roll(pad, k, 0)[HALO:]
        total = total + params_ref[k : k + 1, :] * behind * marks_ref[:, k : k + 1]
    mixed = total.astype(BF16)
    mixed_ref[...] = mixed
    gate_x, gate_a, soft = lru_gates(mixed, ig_ref[...], dg_ref[...], params_ref[CONV : CONV + 1, :])
    reset = marks_ref[:, CONV : CONV + 1]
    keep = 1.0 - reset
    log_a = -8.0 * gate_a * soft
    e = jnp.exp(log_a)
    decay = e * keep
    multiplier = jnp.sqrt(one_minus_square(log_a, e)) * keep + reset
    decay_ref[...] = decay
    here = pl.ds(pl.multiple_of(block * BLOCK, BLOCK), BLOCK)
    a_scr[:, here] = decay
    b_scr[:, here] = gate_x * mixed.astype(F32) * multiplier

    @pl.when(block == pl.num_programs(0) - 1)
    def _():
        p_end, s_end = scan_rows(False, a_scr, b_scr, prods_ref, state_ref)
        ends_ref[0:1, :] = p_end
        ends_ref[1:2, :] = s_end


def back_scan_body(dz_ref, wide_ref, pre_ref, decay_ref, prods_ref, state_ref, in_ref, *refs):
    branch_ref, rev_p_ref, rev_s_ref, ends_ref, a_scr, b_scr, first_scr = refs
    block = pl.program_id(0)
    rows = pre_ref.shape[0]
    d_merged = lax.dot_general(
        dz_ref[...], wide_ref[...], (((1,), (1,)), ((), ())), preferred_element_type=F32
    )
    branch, slope = gelu_and_slope(pre_ref[...])
    state = state_ref[...] + prods_ref[...] * in_ref[...]
    branch_ref[...] = (d_merged * state * slope).astype(BF16)
    decay = decay_ref[...]
    row = lax.broadcasted_iota(jnp.int32, decay.shape, 0)
    ahead = jnp.where(row == rows - 1, 1.0, pltpu.roll(decay, rows - 1, 0))
    here = pl.ds(pl.multiple_of(block * BLOCK, BLOCK), BLOCK)
    a_scr[:, here] = ahead
    b_scr[:, here] = d_merged * branch
    first_scr[:, here] = decay[0:8]

    @pl.when(block == pl.num_programs(0) - 1)
    def _():
        p_end, s_end = scan_rows(True, a_scr, b_scr, rev_p_ref, rev_s_ref)
        first = first_scr[0:1, :]
        ends_ref[0:1, :] = first * p_end
        ends_ref[1:2, :] = first * s_end


def back_mix_body(*refs):
    (rev_p_ref, rev_s_ref, later_ref, prods_ref, state_ref, in_ref) = refs[:6]
    (mixed_ref, pad_ref, marks_ref, params_ref, ig_ref, dg_ref) = refs[6:12]
    sig_ref, tail_ref, rim_ref, sums_ref, gates_ref = refs[12:]
    rows = mixed_ref.shape[0]
    g = rev_s_ref[...] + rev_p_ref[...] * later_ref[...]
    entering_row = in_ref[...]
    state = state_ref[...] + prods_ref[...] * entering_row
    row = lax.broadcasted_iota(jnp.int32, state.shape, 0)
    previous = jnp.where(row == 0, entering_row, pltpu.roll(state, 1, 0))
    mixed = mixed_ref[...]
    mixed_f = mixed.astype(F32)
    param = params_ref[CONV : CONV + 1, :]
    gate_x, gate_a, soft = lru_gates(mixed, ig_ref[...], dg_ref[...], param)
    reset = marks_ref[:, CONV : CONV + 1]
    keep = 1.0 - reset
    log_a = -8.0 * gate_a * soft
    e = jnp.exp(log_a)
    root = jnp.sqrt(one_minus_square(log_a, e))
    multiplier = root * keep + reset
    d_multiplier = g * gate_x * mixed_f
    d_log_a = keep * (g * previous * e - d_multiplier * (e * e) / root)
    d_gate_a = d_log_a * (-8.0 * soft)
    d_param = jnp.sum(d_log_a * (-8.0 * gate_a), axis=0, keepdims=True) * jax.nn.sigmoid(param)
    d_ga = (d_gate_a * gate_a * (1.0 - gate_a)).astype(BF16)
    d_gx = (g * mixed_f * multiplier * gate_x * (1.0 - gate_x)).astype(BF16)
    for half, d_pre in enumerate((d_gx, d_ga)):
        at = (half * pl.num_programs(0) + pl.program_id(0)) * BLOCK
        gates_ref[:, pl.ds(pl.multiple_of(at, BLOCK), BLOCK)] = lax.dot_general(
            mixed, d_pre, (((0,), (0,)), ((), ())), preferred_element_type=F32
        ).astype(BF16)
    d_mixed = (
        g * gate_x * multiplier
        + lax.dot_general(d_gx, ig_ref[...], (((1,), (1,)), ((), ())), preferred_element_type=F32)
        + lax.dot_general(d_ga, dg_ref[...], (((1,), (1,)), ((), ())), preferred_element_type=F32)
    )
    pad = pad_ref[...].astype(F32)
    front = jnp.zeros((HALO, BLOCK), F32)
    d_pad = None
    for k in range(CONV):
        masked = d_mixed * marks_ref[:, k : k + 1]
        behind = pad if k == 0 else pltpu.roll(pad, k, 0)
        sums_ref[k : k + 1, :] = jnp.sum(masked * behind[HALO:], axis=0, keepdims=True)
        term = jnp.concatenate([front, masked * params_ref[k : k + 1, :]])
        if k:
            term = pltpu.roll(term, rows + HALO - k, 0)
        d_pad = term if d_pad is None else d_pad + term
    sums_ref[CONV : CONV + 1, :] = d_param
    sums_ref[CONV + 1 : 8, :] = jnp.zeros((8 - CONV - 1, BLOCK), F32)
    rim_ref[...] = d_pad[HALO - 8 : HALO]
    sig_ref[...] = d_pad[HALO:].astype(BF16)
    tail_ref[...] = d_pad[HALO + rows - 8 :]


def rows_spec(rows):
    return pl.BlockSpec((rows, BLOCK), lambda h: (0, h))


def whole_spec(*shape):
    return pl.BlockSpec(shape, lambda h: (0,) * len(shape))


def gate_specs(heads):
    return [
        pl.BlockSpec((BLOCK, BLOCK), lambda h: (0, h)),
        pl.BlockSpec((BLOCK, BLOCK), lambda h: (0, heads + h)),
    ]


BIG = pltpu.CompilerParams(vmem_limit_bytes=48 << 20)


def shaped(rows, width, dtype=F32):
    return jax.ShapeDtypeStruct((rows, width), dtype)


def mix(padded, marks, params, w_gates):
    rows, width = padded.shape[0] - HALO, padded.shape[1]
    return pl.pallas_call(
        mix_body,
        grid=(width // BLOCK,),
        in_specs=[
            rows_spec(rows + HALO),
            whole_spec(rows, 8),
            rows_spec(8),
            *gate_specs(width // BLOCK),
        ],
        out_specs=[
            rows_spec(rows),
            rows_spec(rows),
            whole_spec(rows, width),
            whole_spec(rows, width),
            whole_spec(2, width),
        ],
        out_shape=[
            shaped(rows, width, BF16),
            shaped(rows, width),
            shaped(rows, width),
            shaped(rows, width),
            shaped(2, width),
        ],
        scratch_shapes=[pltpu.VMEM((rows, width), F32)] * 2,
        cost_estimate=pl.CostEstimate(
            flops=4 * rows * width * BLOCK,
            bytes_accessed=18 * rows * width,
            transcendentals=6 * rows * width,
        ),
        compiler_params=BIG,
    )(padded, marks, params, w_gates, w_gates)


def back_scan(dz, wide, pre, decay, prods, state, incoming):
    rows, width = pre.shape
    depth = dz.shape[1]
    return pl.pallas_call(
        back_scan_body,
        grid=(width // BLOCK,),
        in_specs=[
            whole_spec(rows, depth),
            pl.BlockSpec((BLOCK, depth), lambda h: (h, 0)),
            rows_spec(rows),
            rows_spec(rows),
            rows_spec(rows),
            rows_spec(rows),
            rows_spec(1),
        ],
        out_specs=[
            rows_spec(rows),
            whole_spec(rows, width),
            whole_spec(rows, width),
            whole_spec(2, width),
        ],
        out_shape=[
            shaped(rows, width, BF16),
            shaped(rows, width),
            shaped(rows, width),
            shaped(2, width),
        ],
        scratch_shapes=[
            pltpu.VMEM((rows, width), F32),
            pltpu.VMEM((rows, width), F32),
            pltpu.VMEM((8, width), F32),
        ],
        cost_estimate=pl.CostEstimate(
            flops=2 * rows * width * depth,
            bytes_accessed=2 * (rows + width) * depth + 26 * rows * width,
            transcendentals=rows * width,
        ),
        compiler_params=BIG,
    )(dz, wide, pre, decay, prods, state, incoming)


def back_mix(rev_p, rev_s, later, prods, state, incoming, mixed, padded, marks, params, w_gates):
    rows, width = mixed.shape
    heads = width // BLOCK
    return pl.pallas_call(
        back_mix_body,
        grid=(heads,),
        in_specs=[
            rows_spec(rows),
            rows_spec(rows),
            rows_spec(1),
            rows_spec(rows),
            rows_spec(rows),
            rows_spec(1),
            rows_spec(rows),
            rows_spec(rows + HALO),
            whole_spec(rows, 8),
            rows_spec(8),
            *gate_specs(heads),
        ],
        out_specs=[
            rows_spec(rows),
            rows_spec(8),
            rows_spec(8),
            rows_spec(8),
            whole_spec(BLOCK, 2 * width),
        ],
        out_shape=[
            shaped(rows, width, BF16),
            shaped(8, width),
            shaped(8, width),
            shaped(8, width),
            shaped(BLOCK, 2 * width, BF16),
        ],
        cost_estimate=pl.CostEstimate(
            flops=12 * rows * width * BLOCK,
            bytes_accessed=24 * rows * width,
            transcendentals=6 * rows * width,
        ),
        compiler_params=BIG,
    )(rev_p, rev_s, later, prods, state, incoming, mixed, padded, marks, params, w_gates, w_gates)


def assemble_body(sizes, runs, places, at_ref, *refs):
    count = len(runs)
    chunks = refs[:count]
    outs = refs[count : count + len(sizes)]
    scratch, in_sems, out_sems = refs[count + len(sizes) :]
    loads = [
        pltpu.make_async_copy(
            chunk, scratch.at[slot, pl.ds(first, rows)], in_sems.at[i]
        )
        for i, (chunk, (slot, first, rows)) in enumerate(zip(chunks, runs))
    ]
    for load in loads:
        load.start()
    stores = []
    for slot in range(places):
        for load, run in zip(loads, runs):
            if run[0] == slot:
                load.wait()
        base = 0
        for out, size in zip(outs, sizes):
            target = pl.ds(pl.multiple_of(at_ref[slot] * size, 16), size)
            stores.append(
                pltpu.make_async_copy(
                    scratch.at[slot, pl.ds(base, size)],
                    out.at[target],
                    out_sems.at[len(stores)],
                )
            )
            stores[-1].start()
            base += size
    for store in stores:
        store.wait()


def assemble(ring, sizes, gathered):
    near = [(0, (gathered.own,))]
    for k, (u, d) in enumerate(gathered.pairs, 1):
        near += [(k, (u,)), (-k, (d,))]
    near.append((ring.reach, gathered.far))
    their = [gathered.theirs[0]]
    for pair in gathered.theirs[1:-1]:
        their += [(v,) for v in pair]
    their.append(gathered.theirs[-1])
    rows, width = gathered.own.shape
    slots = []
    for (distance, mine), theirs in zip(near, their):
        chip = ring.chip_at(distance)
        slots += [(2 * chip + ring.core, mine), (2 * chip + 1 - ring.core, theirs)]
    at = jnp.stack([place for place, _ in slots]).astype(jnp.int32)
    places = len(slots)
    if any(size % 16 for size in sizes):
        every = jnp.stack([jnp.concatenate(v) if len(v) > 1 else v[0] for _, v in slots])
        every = jnp.zeros_like(every).at[at].set(every)
        cuts = [sum(sizes[:i]) for i in range(len(sizes) + 1)]
        return [every[:, a:b].reshape(-1, width) for a, b in zip(cuts, cuts[1:])]
    chunks, runs = [], []
    for slot, (_, values) in enumerate(slots):
        first = 0
        for value in values:
            chunks.append(value)
            runs.append((slot, first, value.shape[0]))
            first += value.shape[0]
    anywhere = pl.BlockSpec(memory_space=pl.ANY)
    return pl.pallas_call(
        functools.partial(assemble_body, sizes, runs, places),
        out_shape=[shaped(places * size, width, BF16) for size in sizes],
        in_specs=[pl.BlockSpec(memory_space=pltpu.SMEM)] + [anywhere] * len(chunks),
        out_specs=[anywhere] * len(sizes),
        scratch_shapes=[
            pltpu.VMEM((places, rows, width), BF16),
            pltpu.SemaphoreType.DMA((len(chunks),)),
            pltpu.SemaphoreType.DMA((places * len(sizes),)),
        ],
        cost_estimate=pl.CostEstimate(
            flops=0, bytes_accessed=4 * places * rows * width, transcendentals=0
        ),
        compiler_params=BIG,
    )(at, *chunks)


def ring_distances(ring):
    out = [0]
    for k in range(1, ring.reach):
        out += [k, -k]
    return out + [ring.reach]


def ring_grads_body(shard, chips, pairs, extra, at_ref, *refs):
    lefts, rights = refs[:pairs], refs[pairs : 2 * pairs]
    rest = refs[2 * pairs :]
    if extra:
        extra_ref, rest = rest[0], rest[1:]
    mine_ref, theirs_ref, turned, full, sems = rest
    core = at_ref[chips]
    width = full.shape[2]
    copies = []

    def send(source, size, base):
        for slot in range(chips):
            for out, c in ((mine_ref, core), (theirs_ref, 1 - core)):
                first = pl.multiple_of((2 * at_ref[slot] + c) * size, 16)
                copies.append(
                    pltpu.make_async_copy(
                        source.at[pl.ds(first, size)],
                        out.at[slot, pl.ds(base, size)],
                        sems.at[len(copies)],
                    )
                )
                copies[-1].start()

    if extra:
        send(extra_ref, extra, pairs * shard)
    for pair in range(pairs):
        turned[...] = lefts[pair][...].astype(F32).T.astype(BF16)

        def column(n, _):
            here = pl.ds(pl.multiple_of(n * BLOCK, BLOCK), BLOCK)
            full[pair, :, here] = jnp.dot(
                turned[...], rights[pair][:, here], preferred_element_type=F32
            ).astype(BF16)
            return 0

        lax.fori_loop(0, width // BLOCK, column, 0)
        send(full.at[pair], shard, pair * shard)
    for copy in copies:
        copy.wait()


def ring_grads(ring, shard, lefts, rights, extra=None):
    pairs, chips = len(lefts), ring.chips
    rows, channels = lefts[0].shape
    width = rights[0].shape[1]
    more = 0 if extra is None else extra.shape[0] // (2 * chips)
    at = [ring.chip_at(distance) for distance in ring_distances(ring)]
    if shard % 16 or more % 16:
        values = [rows_inner(a, b).astype(BF16) for a, b in zip(lefts, rights)]
        values += [] if extra is None else [extra]
        values = jnp.concatenate([v.reshape(chips, 2, -1, width) for v in values], axis=2)
        values = values[jnp.stack(at)]
        return (
            lax.dynamic_index_in_dim(values, ring.core, 1, False),
            lax.dynamic_index_in_dim(values, 1 - ring.core, 1, False),
        )
    in_vmem = pl.BlockSpec(memory_space=pltpu.VMEM)
    anywhere = pl.BlockSpec(memory_space=pl.ANY)
    out = jax.ShapeDtypeStruct((chips, pairs * shard + more, width), BF16)
    return pl.pallas_call(
        functools.partial(ring_grads_body, shard, chips, pairs, more),
        out_shape=[out, out],
        in_specs=[pl.BlockSpec(memory_space=pltpu.SMEM)]
        + [in_vmem] * (2 * pairs + (extra is not None)),
        out_specs=[anywhere, anywhere],
        scratch_shapes=[
            pltpu.VMEM((channels, rows), BF16),
            pltpu.VMEM((pairs, channels, width), BF16),
            pltpu.SemaphoreType.DMA((2 * chips * (pairs + (extra is not None)),)),
        ],
        cost_estimate=pl.CostEstimate(
            flops=2 * pairs * rows * channels * width,
            bytes_accessed=2 * pairs * (channels * width + rows * (channels + width)),
            transcendentals=0,
        ),
        compiler_params=BIG,
    )(
        jnp.stack(at + [ring.core]).astype(jnp.int32),
        *lefts,
        *rights,
        *(() if extra is None else (extra,)),
    )


def ring_parts(mine, theirs):
    def part(k):
        return Part(lambda a, b: a[k].astype(F32) + b[k].astype(F32), mine, theirs)

    return [part(k) for k in range(mine.shape[0])]


def ordered(ring_tensor, own, other):
    first = jnp.where(ring_tensor == 0, own, other)
    second = jnp.where(ring_tensor == 0, other, own)
    return jnp.concatenate([first, second])


def per_device(
    block_input,
    starts,
    cotangent,
    gain_mixer,
    w_branch,
    w_signal,
    w_input_gate,
    w_decay_gate,
    conv_taps,
    decay_param,
    w_mixout,
    gain_dense,
    w_gate,
    w_up,
    w_down,
):
    ring = Ring()
    side = lax.axis_index("tensor")
    count = lax.axis_size("dp")
    group = starts.shape[0]
    rows, width = block_input.shape
    shard = w_branch.shape[1]
    channels = shard * count
    lag = CONV - 1
    hops = -(-MAXLEN // group)
    heads_here = w_input_gate.shape[0]

    order = Order()
    mine_at, theirs_at = side * rows, (1 - side) * rows

    small = jnp.concatenate(
        [gain_mixer, gain_dense, conv_taps.reshape(-1), decay_param]
    )
    n_small = small.shape[0]
    small = jnp.pad(small, (0, 16 * width - n_small)).reshape(16, width)
    n_gate = w_input_gate.shape[1]
    gates = jnp.concatenate(
        [jnp.swapaxes(w, 0, 1).reshape(n_gate, channels) for w in (w_input_gate, w_decay_gate)],
        axis=1,
    )
    x_other = tensor_swap(block_input)
    one = Gather(ring, order, jnp.concatenate([w_signal.T, gates, small]), True)
    order.token = one.own
    one.start()
    hid_own = order.run(lambda *w: jnp.stack(w), w_gate.T, w_up.T, w_down)
    pack_two = order.run(lambda *w: jnp.concatenate(w), w_branch.T, w_mixout)
    cumulative = jnp.cumsum(starts)
    padded_cum = jnp.concatenate([jnp.zeros((lag,), jnp.int32), cumulative])
    masks = [
        (cumulative - padded_cum[lag - k : lag - k + group] == 0).astype(F32)
        for k in range(CONV)
    ]
    marks = jnp.stack(masks + [starts.astype(F32)] * (8 - CONV), axis=1)
    tail_keep = (cumulative[group - 1] - cumulative[group - HALO :] == 0)[:, None]
    x_low = order.run(functools.partial(ordered, side), block_input, x_other)
    halo = from_behind(x_low[group - HALO :] * tail_keep.astype(BF16), 1)
    hid_other = tensor_swap(order.tie(hid_own))
    one.next()
    one.next()
    one.next()

    two = Gather(ring, order, pack_two, True)
    two.start()
    one.finish()
    wide_s, wide_gates, wide_small = order.run(
        lambda *_: assemble(ring, (shard, n_gate, 16), one), one.theirs[-1][0]
    )
    wide_small = wide_small.reshape(count, 16, width)[:, 0]
    n_gain = gain_mixer.shape[0]
    gain_one = wide_small[:, :n_gain].reshape(width).astype(F32)
    gain_two = wide_small[:, n_gain : 2 * n_gain].reshape(width).astype(F32)
    taps = wide_small[:, 2 * n_gain : 2 * n_gain + shard * CONV]
    taps = taps.reshape(channels, CONV)
    param = wide_small[:, 2 * n_gain + shard * CONV : n_small].reshape(channels, 1)
    params = jnp.concatenate([taps] + [param] * (8 - CONV), axis=1).T.astype(F32)
    h_pad = order.run(
        lambda x, g: normed(x.astype(F32), g).astype(BF16),
        jnp.concatenate([halo, x_low]),
        gain_one,
    )
    h_one = h_pad[HALO:]
    two.next()
    padded = order.run(lambda h, w: cols_inner(h, w).astype(BF16), h_pad, wide_s)
    mixed, decay, prods, local_state, ends = order.run(
        mix, padded, marks, params, wide_gates
    )
    enter = Entering(order, ends, hops, False)
    two.next()
    enter.next()
    two.next()
    dy = Gather(ring, order, cotangent)
    dy.start()
    incoming = enter.finish()
    hid_other = order.arrive(hid_other)
    hid_theirs = core_swap(hid_own), core_swap(hid_other)
    two.finish()
    wide_b, wide_o = order.run(
        lambda *_: assemble(ring, (shard, shard), two), two.theirs[-1][0]
    )
    dy.next()

    def merge(h, w, local, p, inc):
        pre = cols_inner(h, w)
        return pre, ((local + p * inc) * gelu_tanh(pre)).astype(BF16)

    branch_pre, merged = order.run(merge, h_one, wide_b, local_state, prods, incoming)

    def mix_out(m, w, at):
        return jnp.dot(
            lax.dynamic_slice_in_dim(m, at, rows, 0), w, preferred_element_type=F32
        )

    mix_theirs = order.run(lambda m, w: mix_out(m, w, theirs_at).astype(BF16), merged, wide_o)
    mix_got = tensor_swap(mix_theirs)
    mix_mine = order.run(lambda m, w: mix_out(m, w, mine_at), merged, wide_o)
    dy.next()
    hidden = order.run(
        lambda *parts: jnp.concatenate(parts, axis=1), hid_own, hid_other, *hid_theirs
    )
    hid_g, hid_u, hid_d = hidden[0], hidden[1], hidden[2]
    x_val = block_input.astype(F32)
    x_one = order.run(lambda x, m, t: x + m + t.astype(F32), x_val, mix_mine, mix_got)
    n_two, norm_two_back = jax.vjp(normed, x_one, gain_two)
    h_own = n_two.astype(BF16)

    ff = Gather(ring, order, h_own)
    ff.start()
    dy.next()
    acts, d_gates, d_ups, d_hs, h_list, dy_list = [], [], [], [], [], []

    def piece(h_piece, dy_piece, w_g, w_u, w_d):
        gate_pre = cols_inner(h_piece, w_g)
        up_val = cols_inner(h_piece, w_u)
        gate_act, slope = gelu_and_slope(gate_pre)
        act = (gate_act * up_val).astype(BF16)
        d_act = cols_inner(dy_piece, w_d)
        d_gate = (d_act * up_val * slope).astype(BF16)
        d_up = (d_act * gate_act).astype(BF16)
        d_h = jnp.dot(d_gate, w_g, preferred_element_type=F32) + jnp.dot(
            d_up, w_u, preferred_element_type=F32
        )
        return act, d_gate, d_up, d_h.astype(BF16)

    def do_piece(h_piece, dy_piece):
        out = order.run(piece, h_piece, dy_piece, hid_g, hid_u, hid_d)
        for kept, value in zip((acts, d_gates, d_ups, d_hs, h_list, dy_list), (*out, h_piece, dy_piece)):
            kept.append(value)

    do_piece(h_own, cotangent)
    for step in range(ring.reach - SHOWN, ring.reach - 1):
        ff.next()
        if step == ring.reach - SHOWN:
            first = 0
        else:
            first = step
        if step == ring.reach - 3:
            dy.finish()
        for k in range(first, step + 1):
            do_piece(jnp.concatenate(ff.pairs[k]), jnp.concatenate(dy.pairs[k]))
    ff.finish()
    do_piece(jnp.concatenate(ff.far), jnp.concatenate(dy.far))

    def chunks(parts):
        out = plain_parts(parts[:1])
        for pair in parts[1:-1]:
            out += [Part(lambda v: v[:rows].astype(F32), pair)]
            out += [Part(lambda v: v[rows:].astype(F32), pair)]
        return out + plain_parts(parts[-1:])

    back = Scatter(ring, order, chunks(d_hs), rows // 2)
    back.start()
    downs = [
        order.run(lambda a, w: jnp.dot(a, w, preferred_element_type=F32).astype(BF16), a, hid_d)
        for a in acts
    ]

    def hidden_grad(lefts, rights):
        return order.run(
            lambda a, b: rows_inner(a, b).astype(BF16),
            jnp.concatenate(lefts),
            jnp.concatenate(rights),
        )

    back.next()
    g_gate = hidden_grad(d_gates, h_list)
    back.next()
    g_up = hidden_grad(d_ups, h_list)
    back.next()
    g_down = hidden_grad(acts, dy_list)
    unit = g_gate.shape[0] // 4
    hid_back = [core_swap(g[2 * unit :]) for g in (g_gate, g_up, g_down)]

    def dense_back(d_h, dy_own):
        d_x, g_gain = norm_two_back(d_h)
        d_x = dy_own.astype(F32) + d_x
        return d_x, g_gain, d_x.astype(BF16)

    d_x_one, g_gain_two, dz_own = back.finish(dense_back, cotangent)
    dz_other = tensor_swap(dz_own)
    down = Scatter(ring, order, chunks(downs), rows // 2)
    down.start()
    hid_mine, hid_got = [], []

    def hidden_add(g, t):
        mine, send = order.run(
            lambda a, b: (
                a[:unit].astype(F32) + b[:unit].astype(F32),
                plus(a[unit : 2 * unit], b[unit:]),
            ),
            g,
            t,
        )
        hid_mine.append(mine)
        hid_got.append(send)

    hidden_add(g_gate, hid_back[0])
    hidden_add(g_up, hid_back[1])
    down.next()
    hidden_add(g_down, hid_back[2])
    d_mix = order.run(functools.partial(ordered, side), dz_own, dz_other)
    hid_got = [tensor_swap(order.tie(send)) for send in hid_got]
    d_branch, rev_prods, rev_state, back_ends = order.run(
        back_scan, d_mix, wide_o, branch_pre, decay, prods, local_state, incoming
    )
    leave = Entering(order, back_ends, hops, True)
    down.next()
    mine_two, theirs_two = order.run(
        lambda *v: ring_grads(ring, shard, v[:2], v[2:]), d_branch, merged, h_one, d_mix
    )
    theirs_two = core_swap(theirs_two)
    leave.next()
    later = leave.finish()
    down.next()
    d_sig, sig_tail, rim, sums, g_gates = order.run(
        back_mix,
        rev_prods,
        rev_state,
        later,
        prods,
        local_state,
        incoming,
        mixed,
        padded,
        marks,
        params,
        wide_gates,
    )
    rim = from_behind(rim, -1)
    ring_two = Scatter(ring, order, ring_parts(mine_two, theirs_two), shard)
    ring_two.start()

    def with_rim(sig, tail, edge):
        tail = tail + edge * tail_keep[HALO - 8 :].astype(F32)
        return lax.dynamic_update_slice(sig, tail.astype(BF16), (group - 8, 0))

    d_signal = order.run(with_rim, d_sig, sig_tail, rim)

    def d_h_rows(branch, signal, w_b, w_s, at):
        return jnp.dot(
            lax.dynamic_slice_in_dim(branch, at, rows, 0), w_b, preferred_element_type=F32
        ) + jnp.dot(
            lax.dynamic_slice_in_dim(signal, at, rows, 0), w_s, preferred_element_type=F32
        )

    d_h_theirs = order.run(
        functools.partial(d_h_rows, at=theirs_at), d_branch, d_signal, wide_b, wide_s
    )
    d_h_got = tensor_swap(d_h_theirs.astype(BF16))
    d_h_mine = order.run(
        functools.partial(d_h_rows, at=mine_at), d_branch, d_signal, wide_b, wide_s
    )

    def gain_sum(mine, theirs, x, other, g_two):
        def unit(v):
            v = v.astype(F32)
            return v * lax.rsqrt(jnp.mean(v * v, axis=-1, keepdims=True) + EPS)

        return jnp.stack([jnp.sum(mine * unit(x) + theirs * unit(other), axis=0), g_two])

    gains = order.run(gain_sum, d_h_mine, d_h_theirs, block_input, x_other, g_gain_two)
    gains_other = tensor_swap(gains)
    ring_two.next()
    block_output = down.finish(lambda d, x: (x + d).astype(BF16), x_one)

    mine_last, theirs_last = order.run(
        lambda a, b, g: ring_grads(ring, shard, (a,), (b,), g), d_signal, h_one, g_gates
    )
    theirs_last = core_swap(theirs_last)
    n_rows = shard * (CONV + 1) + 2 * n_gain

    def small_rows(total, gain, gain_other):
        gain = gain + gain_other
        return jnp.concatenate(
            [
                total[:CONV].T.reshape(count, shard * CONV),
                total[CONV].reshape(count, shard),
                gain[0].reshape(count, n_gain),
                gain[1].reshape(count, n_gain),
            ],
            axis=1,
        )

    smalls = order.run(small_rows, sums, gains, gains_other)
    smalls_other = core_swap(smalls)

    def input_back(mine, got, d_x):
        _, norm_one_back = jax.vjp(lambda v: normed(v, gain_one), x_val)
        return d_x + norm_one_back(mine + got.astype(F32))[0]

    grad_input = order.run(input_back, d_h_mine, d_h_got, d_x_one)
    ring_two.next()
    smalls = order.run(
        lambda a, b: jnp.pad(a + b, ((0, 0), (0, width - n_rows))), smalls, smalls_other
    )

    def last_part(k, distance):
        at = 2 * ring.chip_at(distance) + ring.core

        def cut(a, b, small):
            big = a[k].astype(F32) + b[k].astype(F32)
            return jnp.concatenate([big, lax.dynamic_slice_in_dim(small, at, 1, 0)])

        return Part(cut, mine_last, theirs_last, smalls)

    ring_last = Scatter(
        ring,
        order,
        [last_part(k, distance) for k, distance in enumerate(ring_distances(ring))],
        (shard + n_gate) // 32 * 16 or shard // 2,
    )
    ring_last.start()
    hid_sums = [
        order.run(lambda a, b: a + b.astype(F32), mine, got)
        for mine, got in zip(hid_mine[:2], hid_got[:2])
    ]
    ring_two.next()
    ring_last.next()
    hid_sums.append(order.run(lambda a, b: a + b.astype(F32), hid_mine[2], hid_got[2]))
    s_gate, s_up, s_down = hid_sums[0].T, hid_sums[1].T, hid_sums[2]
    ring_last.next()
    total_two = ring_two.finish()
    s_branch = total_two[:shard].T
    s_mixout = total_two[shard:]
    ring_last.next()
    last = ring_last.finish()
    s_signal = last[:shard].T
    s_gates = [
        jnp.swapaxes(v.reshape(n_gate, heads_here, BLOCK), 0, 1)
        for v in jnp.split(last[shard : shard + n_gate], 2, axis=1)
    ]
    s_small = last[shard + n_gate]
    s_taps = s_small[: shard * CONV].reshape(shard, CONV)
    s_param = s_small[shard * CONV : shard * (CONV + 1)]
    s_gain_one = s_small[n_rows - 2 * n_gain : n_rows - n_gain]
    s_gain_two = s_small[n_rows - n_gain : n_rows]
    return (
        block_output,
        grad_input,
        s_gain_one,
        s_branch,
        s_signal,
        s_gates[0],
        s_gates[1],
        s_taps,
        s_param,
        s_mixout,
        s_gain_two,
        s_gate,
        s_up,
        s_down,
    )


def solution(mesh):
    placed = (
        P(("dp", "tensor"), None),
        P("dp"),
        P(("dp", "tensor"), None),
        P("dp"),
        P(None, ("tensor", "dp")),
        P(None, ("tensor", "dp")),
        P("tensor", "dp", None),
        P("tensor", "dp", None),
        P(("tensor", "dp"), None),
        P(("tensor", "dp")),
        P(("tensor", "dp"), None),
        P("dp"),
        P(None, ("tensor", "dp")),
        P(None, ("tensor", "dp")),
        P(("tensor", "dp"), None),
    )
    return jax.shard_map(
        per_device,
        mesh=mesh,
        in_specs=placed,
        out_specs=(
            P(("dp", "tensor"), None),
            P(("dp", "tensor"), None),
            P("dp"),
            P(None, ("tensor", "dp")),
            P(None, ("tensor", "dp")),
            P("tensor", "dp", None),
            P("tensor", "dp", None),
            P(("tensor", "dp"), None),
            P(("tensor", "dp")),
            P(("tensor", "dp"), None),
            P("dp"),
            P(None, ("tensor", "dp")),
            P(None, ("tensor", "dp")),
            P(("tensor", "dp"), None),
        ),
        check_vma=False,
    )
```

time: 2990 us -> 636 us (0.21)
  waiting for transfers between devices: 2030 us -> 192 us
  blocking collectives: 271 us -> 0 us
  local copies, waits for them, and re-layouts: 337 us -> 67.9 us
  starting transfers between devices: 5.31 us -> 123 us
  matrix products: 191 us -> 93.6 us
  Pallas kernels: 0 us -> 57.9 us
    reduce_scatter x12 -> x0, waiting for transfers between devices: 1670 us -> none  [the longest x1 384 us: per_device(): lax.psum_scatter(g_down, 'dp', scatter_dimension=0, tiled=True)]
    all_gather x10 -> x0, waiting for transfers between devices: 361 us -> none  [the longest x1 104 us: fetch_dense(): lax.all_gather(w_gate, 'dp', axis=1, tiled=True)]
    ppermute x2 -> x107, waiting for transfers between devices: 0.55 us -> 192 us  [the longest x32 102 us: down(): return lax.ppermute(value, 'dp', self.down_route)]
    slice x114 -> x29, local copies, waits for them, and re-layouts: 206 us -> 14.7 us  [the longest x8 5.49 us: send(): u, d = (u[:self.half], d[self.half:])]
    all_gather x7 -> x0, blocking collectives: 141 us -> none  [the longest x4 78.3 us: entering(): gathered = jax.tree.map(lambda a: lax.all_gather(a, axis), part)]
    unnamed x2 -> x0, blocking collectives: 124 us -> none
    ppermute x2 -> x107, starting transfers between devices: 3.63 us -> 123 us  [the longest x32 45.2 us: up(): return lax.ppermute(value, 'dp', self.up_route)]
    pad x56 -> x1, local copies, waits for them, and re-layouts: 71.2 us -> 0.01 us  [per_device(): jnp.pad(a + b, ((0, 0), (0, width - n_rows)))]
  transfers between devices with their start and end apart: 25 -> 107, of which waited for: 18 -> 49; matrix products, arithmetic and copies ran while one was open for 12% -> 31% of each run, Pallas kernels for 0% -> 8%
where the time goes in v2:
time: 636 us; the launch traced here: 626 us
  waiting for transfers between devices  192 us (30%)
  starting transfers between devices  123 us (19%)
  matrix products  93.6 us (15%)
  other arithmetic  88.3 us (14%)
  local copies, waits for them, and re-layouts  67.9 us (11%)
  Pallas kernels  57.9 us (9%)
    ppermute x32, waiting for transfers between devices, down(): return lax.ppermute(value, 'dp', self.down_route)  102 us
    ppermute x32, waiting for transfers between devices, up(): return lax.ppermute(value, 'dp', self.up_route)  68.1 us
    ppermute x32, starting transfers between devices, up(): return lax.ppermute(value, 'dp', self.up_route)  45.2 us
    dot_general x17, matrix products, cols_inner(): lax.dot_general(left, right, (((1,), (1,)), ((), ())), preferred_element_...  39.4 us
    unnamed x162, local copies, waits for them, and re-layouts  39.1 us
    ppermute x32, starting transfers between devices, down(): return lax.ppermute(value, 'dp', self.down_route)  31.2 us
    dot_general x3, matrix products, rows_inner(): lax.dot_general(left, right, (((0,), (0,)), ((), ())), preferred_element_...  21.3 us
    ppermute x8, starting transfers between devices, from_behind(): return lax.ppermute(block, 'dp', route)  18.2 us
  transfers between devices with their start and end apart: 107, of which 49 were waited for; matrix products, arithmetic and copies ran while one was open for 31% of the time, Pallas kernels for 8%

profile of v2, /device:TPU:0, one launch (start us, length us, event | category | flops | bytes accessed | tf_op | source)
XLA Modules:
  0.0 625.8 jit_solution(14845063294980381283)
XLA Ops:
  5.2 3.1 collective-permute-start.3
  10.2 3.4 pad_maximum_fusion
  15.7 9.1 %collective-permute-done = bf16[128,2560]{1,0:T(8,128)(2,1)} collective-permute-done((bf16[128,2560]{1,0:T(8,128)(2,1)}, bf16[128,2560]{1,0:T(8,128)(2,1)}, u32[]{:S(2)}, u32[]{:S(2)}) %collective-permute-start) | collective-permute-done | bytes 655392 | tf_op jit(solution)/shard_map/ppermute | solution.py:195
  29.0 11.5 %collective-permute-done.7.refs_6_ = bf16[112,2560]{1,0:T(8,128)(2,1)S(1)} collective-permute-done((bf16[112,2560]{1,0:T(8,128)(2,1)S(1)}, bf16[112,2560]{1,0:T(8,128)(2,1)S(1)}, u32[]{:S(2)}, u32[]{:S(2)}) %collective-permute-start.7) | collective-permute-done | bytes 573472 | tf_op jit(solution)/shard_map/ppermute | solution.py:47
  47.6 7.0 %collective-permute-done.11.refs_10_ = bf16[112,2560]{1,0:T(8,128)(2,1)} collective-permute-done((bf16[112,2560]{1,0:T(8,128)(2,1)S(1)}, bf16[112,2560]{1,0:T(8,128)(2,1)}, u32[]{:S(2)}, u32[]{:S(2)}) %collective-permute-start.11) | collective-permute-done | bytes 573472 | tf_op jit(solution)/shard_map/ppermute | solution.py:47
  56.5 9.5 %collective-permute-done.12.refs_12_ = bf16[112,2560]{1,0:T(8,128)(2,1)S(1)} collective-permute-done((bf16[112,2560]{1,0:T(8,128)(2,1)}, bf16[112,2560]{1,0:T(8,128)(2,1)S(1)}, u32[]{:S(2)}, u32[]{:S(2)}) %collective-permute-start.12) | collective-permute-done | bytes 573472 | tf_op jit(solution)/shard_map/ppermute | solution.py:50
  71.5 3.0 collective-permute-start.15
  74.5 5.5 collective-permute-done.15.refs_14_
  86.9 7.2 %shard_map.254 = (bf16[1280,2560]{1,0:T(8,128)(2,1)}, bf16[256,2560]{1,0:T(8,128)(2,1)}, bf16[256,2560]{1,0:T(8,128)(2,1)}) custom-call(s32[16]{0:T(128)S(1)} %stack.189.at_ref, bf16[112,2560]{1,0:T(8,128)(2,1)S(1)} %pad_maximum_fusion.19.refs_0_, bf16[112,2560]{1,0:T(8,128)(2,1)} %collective-permute-done.2.refs_1_, ...), custom_call_target="tpu_custom_call" | custom-call | bytes 18350080 | tf_op jit(solution)/shard_map/pallas_call | solution.py:622
  98.5 6.6 %collective-permute-done.20.refs_2_ = bf16[160,2560]{1,0:T(8,128)(2,1)} collective-permute-done((bf16[160,2560]{1,0:T(8,128)(2,1)S(1)}, bf16[160,2560]{1,0:T(8,128)(2,1)}, u32[]{:S(2)}, u32[]{:S(2)}) %collective-permute-start.20) | collective-permute-done | bytes 819232 | tf_op jit(solution)/shard_map/ppermute | solution.py:47
  108.7 5.7 convolution_convert_fusion.9.pad_ref.refs_7_
  117.2 6.6 %shard_map.255 = (bf16[256,1280]{1,0:T(8,128)(2,1)S(1)}, f32[256,1280]{1,0:T(8,128)S(1)}, f32[256,1280]{1,0:T(8,128)S(1)}, f32[256,1280]{1,0:T(8,128)S(1)}, f32[2,1280]{1,0:T(2,128)S(1)}) custom-call(bf16[272,1280]{1,0:T(8,128)(2,1)S(1)} %copy-done.13, f32[256,8]{1,0:T(8,128)S(1)} %copy-done.21, f32[8,1280]{1,0:T(8,128)S(1)} %convert_bitcast_fusion.1.params_ref.refs_9_, ...), custom_call_target="tpu_custom_call" | custom-call | flops 335544320 | bytes 5898240 | tf_op jit(solution)/shard_map/pallas_call | solution.py:443
  131.6 8.6 %collective-permute-start.22 = (bf16[160,2560]{1,0:T(8,128)(2,1)}, bf16[160,2560]{1,0:T(8,128)(2,1)S(1)}, u32[]{:S(2)}, u32[]{:S(2)}) collective-permute-start(bf16[160,2560]{1,0:T(8,128)(2,1)} %collective-permute-done.20.refs_2_), channel_id=1, source_target_pairs={{0,2},{2,0},{4,6},{6,4},{8,10},{10,8},{12,14},{14,12},{16,18},{18,... | collective-permute-start | bytes 2457608 | tf_op jit(solution)/shard_map/ppermute | solution.py:191
  140.2 4.1 collective-permute-done.28.refs_10_
  153.6 8.0 %collective-permute-start.37 = (f32[2,1280]{1,0:T(2,128)S(1)}, f32[2,1280]{1,0:T(2,128)S(1)}, u32[]{:S(2)}, u32[]{:S(2)}) collective-permute-start(f32[2,1280]{1,0:T(2,128)S(1)} %pad_maximum_fusion.24), channel_id=1, source_target_pairs={{0,6},{2,8},{4,10},{6,12},{8,14},{10,16},{12,18},{14,20},{16,22},{... | collective-permute-start | bytes 30728 | tf_op jit(solution)/shard_map/ppermute | solution.py:201
  178.3 9.9 %shard_map.256 = (bf16[1280,2560]{1,0:T(8,128)(2,1)}, bf16[1280,2560]{1,0:T(8,128)(2,1)}) custom-call(s32[16]{0:T(128)S(1)} %stack.189.at_ref, bf16[160,2560]{1,0:T(8,128)(2,1)S(1)} %constant_dynamic-update-slice_fusion.refs_0_, bf16[160,2560]{1,0:T(8,128)(2,1)S(1)} %copy-done.10, bf16[160,2560]{1,0:T(8,128)(2,1)} %collective-permute-done.20.refs_2_, ...), custom_call_target="tpu_custom_call" | custom-call | bytes 26214400 | tf_op jit(solution)/shard_map/pallas_call | solution.py:622
  188.2 5.3 fusion.147.pre_ref
  205.4 8.9 %collective-permute-done.45 = bf16[128,2560]{1,0:T(8,128)(2,1)} collective-permute-done((bf16[128,2560]{1,0:T(8,128)(2,1)}, bf16[128,2560]{1,0:T(8,128)(2,1)}, u32[]{:S(2)}, u32[]{:S(2)}) %collective-permute-start.45) | collective-permute-done | bytes 655392 | tf_op jit(solution)/shard_map/ppermute | solution.py:47
  242.0 3.3 constant_dynamic-update-slice_fusion.24
  265.3 2.7 constant_dynamic-update-slice_fusion.23
  271.3 4.5 collective-permute-done.51
  281.9 2.7 constant_dynamic-update-slice_fusion.22
  297.9 2.7 constant_dynamic-update-slice_fusion.21
  322.4 7.5 %collective-permute-done.59 = bf16[64,2560]{1,0:T(8,128)(2,1)S(1)} collective-permute-done((bf16[64,2560]{1,0:T(8,128)(2,1)S(1)}, bf16[64,2560]{1,0:T(8,128)(2,1)S(1)}, u32[]{:S(2)}, u32[]{:S(2)}) %collective-permute-start.59) | collective-permute-done | bytes 327712 | tf_op jit(solution)/shard_map/ppermute | solution.py:50
  332.7 8.0 %convolution_convert_fusion.2 = bf16[960,2560]{1,0:T(8,128)(2,1)S(1)} fusion(bf16[1024,960]{0,1:T(8,128)(2,1)S(1)} %get-tuple-element.522, bf16[1024,2560]{1,0:T(8,128)(2,1)} %copy-done.55), kind=kOutput, calls=%fused_computation.2 | convolution fusion | flops 5035622400 | bytes 12124160 | tf_op jit(solution)/shard_map/dot_general | solution.py:254
  343.7 5.5 convolution_convert_fusion.1
  350.8 7.8 %collective-permute-done.63 = bf16[128,2560]{1,0:T(8,128)(2,1)S(1)} collective-permute-done((bf16[128,2560]{1,0:T(8,128)(2,1)S(1)}, bf16[128,2560]{1,0:T(8,128)(2,1)S(1)}, u32[]{:S(2)}, u32[]{:S(2)}) %collective-permute-start.63) | collective-permute-done | bytes 655392 | tf_op jit(solution)/shard_map/ppermute | solution.py:50
  361.1 7.9 %convolution_convert_fusion = bf16[960,2560]{1,0:T(8,128)(2,1)S(1)} fusion(bf16[1024,960]{0,1:T(8,128)(2,1)S(1)} %copy-done.62, bf16[1024,2560]{1,0:T(8,128)(2,1)} %constant_dynamic-update-slice_fusion.30), kind=kOutput, calls=%fused_computation | convolution fusion | flops 5035622400 | bytes 12124160 | tf_op jit(solution)/shard_map/dot_general | solution.py:254
  369.3 5.8 collective-permute-done.65
  376.4 2.7 fusion.133
  395.8 8.0 %shard_map.257 = (bf16[256,1280]{1,0:T(8,128)(2,1)S(1)}, f32[256,1280]{1,0:T(8,128)S(1)}, f32[256,1280]{1,0:T(8,128)S(1)}, f32[2,1280]{1,0:T(2,128)S(1)}) custom-call(bf16[256,2560]{1,0:T(8,128)(2,1)S(1)} %pad_maximum_fusion.9.dz_ref.refs_3_, bf16[1280,2560]{1,0:T(8,128)(2,1)} %get-tuple-element.563.wide_ref, f32[256,1280]{1,0:T(8,128)S(1)} %copy-done.3, ...), custom_call_target="tpu_custom_call" | custom-call | flops 1677721600 | bytes 16384000 | tf_op jit(solution)/shard_map/pallas_call | solution.py:479
  406.9 10.7 %shard_map.258 = (bf16[8,160,2560]{2,1,0:T(8,128)(2,1)}, bf16[8,160,2560]{2,1,0:T(8,128)(2,1)}) custom-call(s32[9]{0:T(128)S(1)} %stack.209.at_ref, bf16[256,1280]{1,0:T(8,128)(2,1)S(1)} %get-tuple-element.622.refs_0_, bf16[256,1280]{1,0:T(8,128)(2,1)S(1)} %copy-done.5, bf16[256,2560]{1,0:T(8,128)(2,1)S(1)} %copy-done.8, ...), custom_call_target="tpu_custom_call" | custom-call | flops 3355443200 | bytes 17039360 | tf_op jit(solution)/shard_map/pallas_call | solution.py:705
  420.0 2.7 collective-permute-start.75
  422.7 5.5 collective-permute-done.77
  432.6 3.1 collective-permute-done.79
  445.8 8.4 %shard_map.259 = (bf16[256,1280]{1,0:T(8,128)(2,1)S(1)}, f32[8,1280]{1,0:T(8,128)S(1)}, f32[8,1280]{1,0:T(8,128)S(1)}, f32[8,1280]{1,0:T(8,128)S(1)}, bf16[256,2560]{1,0:T(8,128)(2,1)S(1)}) custom-call(f32[256,1280]{1,0:T(8,128)S(1)} %get-tuple-element.596.refs_0_, f32[256,1280]{1,0:T(8,128)} %copy-done.7, f32[1,1280]{1,0:T(1,128)S(1)} %slice_add_fusion.refs_2_, ...), custom_call_target="tpu_custom_call" | custom-call | flops 1006632960 | bytes 7864320 | tf_op jit(solution)/shard_map/pallas_call | solution.py:520
  457.3 3.0 collective-permute-start.83
  461.8 4.0 fusion.107
  480.1 10.0 %collective-permute-done.81 = bf16[128,2560]{1,0:T(8,128)(2,1)S(1)} collective-permute-done((bf16[128,2560]{1,0:T(8,128)(2,1)S(1)}, bf16[128,2560]{1,0:T(8,128)(2,1)S(1)}, u32[]{:S(2)}, u32[]{:S(2)}) %collective-permute-start.81) | collective-permute-done | bytes 655392 | tf_op jit(solution)/shard_map/ppermute | solution.py:47
  492.4 7.1 %shard_map.260 = (bf16[8,96,2560]{2,1,0:T(8,128)(2,1)}, bf16[8,96,2560]{2,1,0:T(8,128)(2,1)}) custom-call(s32[9]{0:T(128)S(1)} %stack.209.at_ref, bf16[256,1280]{1,0:T(8,128)(2,1)S(1)} %fusion.120.refs_0_, bf16[256,2560]{1,0:T(8,128)(2,1)S(1)} %copy-done.8, bf16[256,2560]{1,0:T(8,128)(2,1)S(1)} %get-tuple-element.641.refs_2_), custom_call_target="tpu_custom_call" | custom-call | flops 1677721600 | bytes 8519680 | tf_op jit(solution)/shard_map/pallas_call | solution.py:705
  510.9 2.7 fusion.29
  513.6 14.2 %collective-permute-done.90 = bf16[160,2560]{1,0:T(8,128)(2,1)S(1)} collective-permute-done((bf16[160,2560]{1,0:T(8,128)(2,1)S(1)}, bf16[160,2560]{1,0:T(8,128)(2,1)S(1)}, u32[]{:S(2)}, u32[]{:S(2)}) %collective-permute-start.90) | collective-permute-done | bytes 819232 | tf_op jit(solution)/shard_map/ppermute | solution.py:50
  537.1 3.2 convert_add_fusion.3
  541.4 3.0 convert_add_fusion.2
  544.5 9.3 %collective-permute-done.94 = bf16[160,2560]{1,0:T(8,128)(2,1)S(1)} collective-permute-done((bf16[160,2560]{1,0:T(8,128)(2,1)S(1)}, bf16[160,2560]{1,0:T(8,128)(2,1)S(1)}, u32[]{:S(2)}, u32[]{:S(2)}) %collective-permute-start.94) | collective-permute-done | bytes 819232 | tf_op jit(solution)/shard_map/ppermute | solution.py:50
  568.1 20.1 %collective-permute-done.98 = bf16[97,2560]{1,0:T(8,128)(2,1)S(1)} collective-permute-done((bf16[97,2560]{1,0:T(8,128)(2,1)S(1)}, bf16[97,2560]{1,0:T(8,128)(2,1)S(1)}, u32[]{:S(2)}, u32[]{:S(2)}) %collective-permute-start.98) | collective-permute-done | bytes 496672 | tf_op jit(solution)/shard_map/ppermute | solution.py:50
  595.6 7.9 %collective-permute-done.101 = bf16[97,2560]{1,0:T(8,128)(2,1)S(1)} collective-permute-done((bf16[97,2560]{1,0:T(8,128)(2,1)S(1)}, bf16[97,2560]{1,0:T(8,128)(2,1)S(1)}, u32[]{:S(2)}, u32[]{:S(2)}) %collective-permute-start.101) | collective-permute-done | bytes 496672 | tf_op jit(solution)/shard_map/ppermute | solution.py:50
  611.6 8.0 %collective-permute-done.105 = bf16[97,2560]{1,0:T(8,128)(2,1)S(1)} collective-permute-done((bf16[97,2560]{1,0:T(8,128)(2,1)S(1)}, bf16[97,2560]{1,0:T(8,128)(2,1)S(1)}, u32[]{:S(2)}, u32[]{:S(2)}) %collective-permute-start.105) | collective-permute-done | bytes 496672 | tf_op jit(solution)/shard_map/ppermute | solution.py:50
  (566 shorter events, 308.1 us)
Async XLA Ops:
  5.2 21.8 %collective-permute-start.3 = (bf16[112,2560]{1,0:T(8,128)(2,1)S(1)}, bf16[112,2560]{1,0:T(8,128)(2,1)S(1)}, u32[]{:S(2)}, u32[]{:S(2)}) collective-permute-start(bf16[112,2560]{1,0:T(8,128)(2,1)S(1)} %pad_maximum_fusion.19.refs_0_), channel_id=1, source_target_pairs={{0,8},{2,10},{8,16},{10,18},{16,24},{18,26},{24,28},{26,30},{28,20... | collective-permute-start | bytes 1720328 | tf_op jit(solution)/shard_map/ppermute | solution.py:47
  8.2 18.8 %collective-permute-start.4 = (bf16[112,2560]{1,0:T(8,128)(2,1)S(1)}, bf16[112,2560]{1,0:T(8,128)(2,1)S(1)}, u32[]{:S(2)}, u32[]{:S(2)}) collective-permute-start(bf16[112,2560]{1,0:T(8,128)(2,1)S(1)} %pad_maximum_fusion.19.refs_0_), channel_id=1, source_target_pairs={{8,0},{10,2},{16,8},{18,10},{24,16},{26,18},{28,24},{30,26},{20,28... | collective-permute-start | bytes 1720328 | tf_op jit(solution)/shard_map/ppermute | solution.py:50
  44.1 24.5 %collective-permute-start.2 = (bf16[112,2560]{1,0:T(8,128)(2,1)S(1)}, bf16[112,2560]{1,0:T(8,128)(2,1)}, u32[]{:S(2)}, u32[]{:S(2)}) collective-permute-start(bf16[112,2560]{1,0:T(8,128)(2,1)S(1)} %pad_maximum_fusion.19.refs_0_), channel_id=1, source_target_pairs={{0,2},{2,0},{4,6},{6,4},{8,10},{10,8},{12,14},{14,12},{16,18},{18,... | collective-permute-start | bytes 1720328 | tf_op jit(solution)/shard_map/ppermute | solution.py:191
  46.6 27.9 %collective-permute-start.5 = (bf16[112,2560]{1,0:T(8,128)(2,1)S(1)}, bf16[112,2560]{1,0:T(8,128)(2,1)}, u32[]{:S(2)}, u32[]{:S(2)}) collective-permute-start(bf16[112,2560]{1,0:T(8,128)(2,1)S(1)} %collective-permute-done.3.refs_2_), channel_id=1, source_target_pairs={{0,2},{2,0},{4,6},{6,4},{8,10},{10,8},{12,14},{14,12},{16,18},{18,... | collective-permute-start | bytes 1720328 | tf_op jit(solution)/shard_map/ppermute | solution.py:191
  47.1 33.6 %collective-permute-start.6 = (bf16[112,2560]{1,0:T(8,128)(2,1)S(1)}, bf16[112,2560]{1,0:T(8,128)(2,1)}, u32[]{:S(2)}, u32[]{:S(2)}) collective-permute-start(bf16[112,2560]{1,0:T(8,128)(2,1)S(1)} %collective-permute-done.4.refs_4_), channel_id=1, source_target_pairs={{0,2},{2,0},{4,6},{6,4},{8,10},{10,8},{12,14},{14,12},{16,18},{18,... | collective-permute-start | bytes 1720328 | tf_op jit(solution)/shard_map/ppermute | solution.py:191
  47.1 34.1 %collective-permute-start.9 = (bf16[112,2560]{1,0:T(8,128)(2,1)S(1)}, bf16[112,2560]{1,0:T(8,128)(2,1)}, u32[]{:S(2)}, u32[]{:S(2)}) collective-permute-start(bf16[112,2560]{1,0:T(8,128)(2,1)S(1)} %collective-permute-done.7.refs_6_), channel_id=1, source_target_pairs={{0,2},{2,0},{4,6},{6,4},{8,10},{10,8},{12,14},{14,12},{16,18},{18,... | collective-permute-start | bytes 1720328 | tf_op jit(solution)/shard_map/ppermute | solution.py:191
  83.8 82.3 %collective-permute-start.35 = (bf16[3,240,2560]{2,1,0:T(8,128)(2,1)}, bf16[3,240,2560]{2,1,0:T(8,128)(2,1)}, u32[]{:S(2)}, u32[]{:S(2)}) collective-permute-start(bf16[3,240,2560]{2,1,0:T(8,128)(2,1)} %pad_maximum_fusion), channel_id=1, source_target_pairs={{0,1},{1,0},{2,3},{3,2},{4,5},{5,4},{6,7},{7,6},{8,9},{9,8},{10,11... | collective-permute-start | bytes 11059208 | tf_op jit(solution)/shard_map/ppermute | solution.py:195
  84.7 20.4 %collective-permute-start.20 = (bf16[160,2560]{1,0:T(8,128)(2,1)S(1)}, bf16[160,2560]{1,0:T(8,128)(2,1)}, u32[]{:S(2)}, u32[]{:S(2)}) collective-permute-start(bf16[160,2560]{1,0:T(8,128)(2,1)S(1)} %constant_dynamic-update-slice_fusion.refs_0_), channel_id=1, source_target_pairs={{0,8},{2,10},{8,16},{10,18},{16,24},{18,26},{24,28},{26,30},{28,20... | collective-permute-start | bytes 2457608 | tf_op jit(solution)/shard_map/ppermute | solution.py:47
  86.9 19.8 %collective-permute-start.21 = (bf16[160,2560]{1,0:T(8,128)(2,1)S(1)}, bf16[160,2560]{1,0:T(8,128)(2,1)}, u32[]{:S(2)}, u32[]{:S(2)}) collective-permute-start(bf16[160,2560]{1,0:T(8,128)(2,1)S(1)} %constant_dynamic-update-slice_fusion.refs_0_), channel_id=1, source_target_pairs={{8,0},{10,2},{16,8},{18,10},{24,16},{26,18},{28,24},{30,26},{20,28... | collective-permute-start | bytes 2457608 | tf_op jit(solution)/shard_map/ppermute | solution.py:50
  106.7 19.1 %collective-permute-start.24 = (bf16[160,2560]{1,0:T(8,128)(2,1)}, bf16[160,2560]{1,0:T(8,128)(2,1)}, u32[]{:S(2)}, u32[]{:S(2)}) collective-permute-start(bf16[160,2560]{1,0:T(8,128)(2,1)} %collective-permute-done.20.refs_2_), channel_id=1, source_target_pairs={{0,8},{2,10},{8,16},{10,18},{16,24},{18,26},{24,28},{26,30},{28,20... | collective-permute-start | bytes 2457608 | tf_op jit(solution)/shard_map/ppermute | solution.py:47
  107.6 18.8 %collective-permute-start.25 = (bf16[160,2560]{1,0:T(8,128)(2,1)}, bf16[160,2560]{1,0:T(8,128)(2,1)}, u32[]{:S(2)}, u32[]{:S(2)}) collective-permute-start(bf16[160,2560]{1,0:T(8,128)(2,1)} %collective-permute-done.21.refs_4_), channel_id=1, source_target_pairs={{8,0},{10,2},{16,8},{18,10},{24,16},{26,18},{28,24},{30,26},{20,28... | collective-permute-start | bytes 2457608 | tf_op jit(solution)/shard_map/ppermute | solution.py:50
  126.5 17.8 %collective-permute-start.28 = (bf16[160,2560]{1,0:T(8,128)(2,1)}, bf16[160,2560]{1,0:T(8,128)(2,1)S(1)}, u32[]{:S(2)}, u32[]{:S(2)}) collective-permute-start(bf16[160,2560]{1,0:T(8,128)(2,1)} %collective-permute-done.24.refs_6_), channel_id=1, source_target_pairs={{0,8},{2,10},{8,16},{10,18},{16,24},{18,26},{24,28},{26,30},{28,20... | collective-permute-start | bytes 2457608 | tf_op jit(solution)/shard_map/ppermute | solution.py:47
  128.2 17.7 %collective-permute-start.29 = (bf16[160,2560]{1,0:T(8,128)(2,1)}, bf16[160,2560]{1,0:T(8,128)(2,1)}, u32[]{:S(2)}, u32[]{:S(2)}) collective-permute-start(bf16[160,2560]{1,0:T(8,128)(2,1)} %collective-permute-done.25.refs_8_), channel_id=1, source_target_pairs={{8,0},{10,2},{16,8},{18,10},{24,16},{26,18},{28,24},{30,26},{20,28... | collective-permute-start | bytes 2457608 | tf_op jit(solution)/shard_map/ppermute | solution.py:50
  145.9 18.7 %collective-permute-start.26 = (bf16[160,2560]{1,0:T(8,128)(2,1)}, bf16[160,2560]{1,0:T(8,128)(2,1)S(1)}, u32[]{:S(2)}, u32[]{:S(2)}) collective-permute-start(bf16[160,2560]{1,0:T(8,128)(2,1)} %collective-permute-done.24.refs_6_), channel_id=1, source_target_pairs={{0,2},{2,0},{4,6},{6,4},{8,10},{10,8},{12,14},{14,12},{16,18},{18,... | collective-permute-start | bytes 2457608 | tf_op jit(solution)/shard_map/ppermute | solution.py:191
  146.9 19.2 %collective-permute-start.33 = (bf16[80,2560]{1,0:T(8,128)(2,1)S(1)}, bf16[80,2560]{1,0:T(8,128)(2,1)}, u32[]{:S(2)}, u32[]{:S(2)}) collective-permute-start(bf16[80,2560]{1,0:T(8,128)(2,1)S(1)} %slice.502), channel_id=1, source_target_pairs={{0,8},{2,10},{8,16},{10,18},{16,24},{18,26},{24,28},{26,30},{28,20... | collective-permute-start | bytes 1228808 | tf_op jit(solution)/shard_map/ppermute | solution.py:47
  166.1 22.0 %collective-permute-start.40 = (bf16[128,2560]{1,0:T(8,128)(2,1)}, bf16[128,2560]{1,0:T(8,128)(2,1)}, u32[]{:S(2)}, u32[]{:S(2)}) collective-permute-start(bf16[128,2560]{1,0:T(8,128)(2,1)} %param.17), channel_id=1, source_target_pairs={{0,8},{2,10},{8,16},{10,18},{16,24},{18,26},{24,28},{26,30},{28,20... | collective-permute-start | bytes 1966088 | tf_op jit(solution)/shard_map/ppermute | solution.py:47
  167.4 20.8 %collective-permute-start.41 = (bf16[128,2560]{1,0:T(8,128)(2,1)}, bf16[128,2560]{1,0:T(8,128)(2,1)}, u32[]{:S(2)}, u32[]{:S(2)}) collective-permute-start(bf16[128,2560]{1,0:T(8,128)(2,1)} %param.17), channel_id=1, source_target_pairs={{8,0},{10,2},{16,8},{18,10},{24,16},{26,18},{28,24},{30,26},{20,28... | collective-permute-start | bytes 1966088 | tf_op jit(solution)/shard_map/ppermute | solution.py:50
  175.4 49.1 %collective-permute-start.43 = (bf16[3,240,2560]{2,1,0:T(8,128)(2,1)}, bf16[3,240,2560]{2,1,0:T(8,128)(2,1)}, u32[]{:S(2)}, u32[]{:S(2)}) collective-permute-start(bf16[3,240,2560]{2,1,0:T(8,128)(2,1)} %pad_maximum_fusion), channel_id=1, source_target_pairs={{0,2},{2,0},{4,6},{6,4},{8,10},{10,8},{12,14},{14,12},{16,18},{18,... | collective-permute-start | bytes 11059208 | tf_op jit(solution)/shard_map/ppermute | solution.py:191
  175.8 48.7 %collective-permute-start.44 = (bf16[3,240,2560]{2,1,0:T(8,128)(2,1)}, bf16[3,240,2560]{2,1,0:T(8,128)(2,1)}, u32[]{:S(2)}, u32[]{:S(2)}) collective-permute-start(bf16[3,240,2560]{2,1,0:T(8,128)(2,1)} %collective-permute-done.35), channel_id=1, source_target_pairs={{0,2},{2,0},{4,6},{6,4},{8,10},{10,8},{12,14},{14,12},{16,18},{18,... | collective-permute-start | bytes 11059208 | tf_op jit(solution)/shard_map/ppermute | solution.py:191
  196.5 36.4 %collective-permute-start.42 = (bf16[128,2560]{1,0:T(8,128)(2,1)}, bf16[128,2560]{1,0:T(8,128)(2,1)}, u32[]{:S(2)}, u32[]{:S(2)}) collective-permute-start(bf16[128,2560]{1,0:T(8,128)(2,1)} %convolution_convert_fusion.8), channel_id=1, source_target_pairs={{0,1},{1,0},{2,3},{3,2},{4,5},{5,4},{6,7},{7,6},{8,9},{9,8},{10,11... | collective-permute-start | bytes 1966088 | tf_op jit(solution)/shard_map/ppermute | solution.py:195
  215.9 19.1 %collective-permute-start.49 = (bf16[128,2560]{1,0:T(8,128)(2,1)}, bf16[128,2560]{1,0:T(8,128)(2,1)}, u32[]{:S(2)}, u32[]{:S(2)}) collective-permute-start(bf16[128,2560]{1,0:T(8,128)(2,1)} %collective-permute-done.45), channel_id=1, source_target_pairs={{0,8},{2,10},{8,16},{10,18},{16,24},{18,26},{24,28},{26,30},{28,20... | collective-permute-start | bytes 1966088 | tf_op jit(solution)/shard_map/ppermute | solution.py:47
  217.1 17.9 %collective-permute-start.50 = (bf16[128,2560]{1,0:T(8,128)(2,1)}, bf16[128,2560]{1,0:T(8,128)(2,1)}, u32[]{:S(2)}, u32[]{:S(2)}) collective-permute-start(bf16[128,2560]{1,0:T(8,128)(2,1)} %collective-permute-done.46), channel_id=1, source_target_pairs={{8,0},{10,2},{16,8},{18,10},{24,16},{26,18},{28,24},{30,26},{20,28... | collective-permute-start | bytes 1966088 | tf_op jit(solution)/shard_map/ppermute | solution.py:50
  240.0 17.7 %collective-permute-start.47 = (bf16[128,2560]{1,0:T(8,128)(2,1)S(1)}, bf16[128,2560]{1,0:T(8,128)(2,1)S(1)}, u32[]{:S(2)}, u32[]{:S(2)}) collective-permute-start(bf16[128,2560]{1,0:T(8,128)(2,1)S(1)} %get-tuple-element.455), channel_id=1, source_target_pairs={{0,8},{2,10},{8,16},{10,18},{16,24},{18,26},{24,28},{26,30},{28,20... | collective-permute-start | bytes 1966088 | tf_op jit(solution)/shard_map/ppermute | solution.py:47
  241.2 17.7 %collective-permute-start.48 = (bf16[128,2560]{1,0:T(8,128)(2,1)S(1)}, bf16[128,2560]{1,0:T(8,128)(2,1)S(1)}, u32[]{:S(2)}, u32[]{:S(2)}) collective-permute-start(bf16[128,2560]{1,0:T(8,128)(2,1)S(1)} %get-tuple-element.455), channel_id=1, source_target_pairs={{8,0},{10,2},{16,8},{18,10},{24,16},{26,18},{28,24},{30,26},{20,28... | collective-permute-start | bytes 1966088 | tf_op jit(solution)/shard_map/ppermute | solution.py:50
  247.2 29.6 %collective-permute-start.55 = (bf16[64,2560]{1,0:T(8,128)(2,1)S(1)}, bf16[64,2560]{1,0:T(8,128)(2,1)S(1)}, u32[]{:S(2)}, u32[]{:S(2)}) collective-permute-start(bf16[64,2560]{1,0:T(8,128)(2,1)S(1)} %slice.511), channel_id=1, source_target_pairs={{0,8},{2,10},{8,16},{10,18},{16,24},{18,26},{24,28},{26,30},{28,20... | collective-permute-start | bytes 983048 | tf_op jit(solution)/shard_map/ppermute | solution.py:47
  249.5 27.4 %collective-permute-start.56 = (bf16[64,2560]{1,0:T(8,128)(2,1)S(1)}, bf16[64,2560]{1,0:T(8,128)(2,1)S(1)}, u32[]{:S(2)}, u32[]{:S(2)}) collective-permute-start(bf16[64,2560]{1,0:T(8,128)(2,1)S(1)} %slice.512), channel_id=1, source_target_pairs={{8,0},{10,2},{16,8},{18,10},{24,16},{26,18},{28,24},{30,26},{20,28... | collective-permute-start | bytes 983048 | tf_op jit(solution)/shard_map/ppermute | solution.py:50
  340.8 41.4 %collective-permute-start.70 = (bf16[480,2560]{1,0:T(8,128)(2,1)S(1)}, bf16[480,2560]{1,0:T(8,128)(2,1)S(1)}, u32[]{:S(2)}, u32[]{:S(2)}) collective-permute-start(bf16[480,2560]{1,0:T(8,128)(2,1)S(1)} %slice.636), channel_id=1, source_target_pairs={{0,2},{2,0},{4,6},{6,4},{8,10},{10,8},{12,14},{14,12},{16,18},{18,... | collective-permute-start | bytes 7372808 | tf_op jit(solution)/shard_map/ppermute | solution.py:191
  350.8 35.2 %collective-permute-start.69 = (bf16[480,2560]{1,0:T(8,128)(2,1)}, bf16[480,2560]{1,0:T(8,128)(2,1)S(1)}, u32[]{:S(2)}, u32[]{:S(2)}) collective-permute-start(bf16[480,2560]{1,0:T(8,128)(2,1)} %slice.635), channel_id=1, source_target_pairs={{0,2},{2,0},{4,6},{6,4},{8,10},{10,8},{12,14},{14,12},{16,18},{18,... | collective-permute-start | bytes 7372808 | tf_op jit(solution)/shard_map/ppermute | solution.py:191
  369.2 22.9 %collective-permute-start.74 = (bf16[480,2560]{1,0:T(8,128)(2,1)S(1)}, bf16[480,2560]{1,0:T(8,128)(2,1)S(1)}, u32[]{:S(2)}, u32[]{:S(2)}) collective-permute-start(bf16[480,2560]{1,0:T(8,128)(2,1)S(1)} %slice.637), channel_id=1, source_target_pairs={{0,2},{2,0},{4,6},{6,4},{8,10},{10,8},{12,14},{14,12},{16,18},{18,... | collective-permute-start | bytes 7372808 | tf_op jit(solution)/shard_map/ppermute | solution.py:191
  417.6 37.9 %collective-permute-start.82 = (bf16[8,160,2560]{2,1,0:T(8,128)(2,1)}, bf16[8,160,2560]{2,1,0:T(8,128)(2,1)}, u32[]{:S(2)}, u32[]{:S(2)}) collective-permute-start(bf16[8,160,2560]{2,1,0:T(8,128)(2,1)} %get-tuple-element.581), channel_id=1, source_target_pairs={{0,2},{2,0},{4,6},{6,4},{8,10},{10,8},{12,14},{14,12},{16,18},{18,... | collective-permute-start | bytes 19660808 | tf_op jit(solution)/shard_map/ppermute | solution.py:191
  420.0 18.2 %collective-permute-start.75 = (bf16[128,2560]{1,0:T(8,128)(2,1)}, bf16[128,2560]{1,0:T(8,128)(2,1)}, u32[]{:S(2)}, u32[]{:S(2)}) collective-permute-start(bf16[128,2560]{1,0:T(8,128)(2,1)} %add_convert_fusion.8), channel_id=1, source_target_pairs={{8,0},{10,2},{16,8},{18,10},{24,16},{26,18},{28,24},{30,26},{20,28... | collective-permute-start | bytes 1966088 | tf_op jit(solution)/shard_map/ppermute | solution.py:50
  431.3 108.9 %collective-permute-start.96 = (bf16[240,2560]{1,0:T(8,128)(2,1)}, bf16[240,2560]{1,0:T(8,128)(2,1)}, u32[]{:S(2)}, u32[]{:S(2)}) collective-permute-start(bf16[240,2560]{1,0:T(8,128)(2,1)} %get-tuple-element.670), channel_id=1, source_target_pairs={{0,1},{1,0},{2,3},{3,2},{4,5},{5,4},{6,7},{7,6},{8,9},{9,8},{10,11... | collective-permute-start | bytes 3686408 | tf_op jit(solution)/shard_map/ppermute | solution.py:195
  435.7 100.4 %collective-permute-start.97 = (bf16[240,2560]{1,0:T(8,128)(2,1)}, bf16[240,2560]{1,0:T(8,128)(2,1)}, u32[]{:S(2)}, u32[]{:S(2)}) collective-permute-start(bf16[240,2560]{1,0:T(8,128)(2,1)} %get-tuple-element.671), channel_id=1, source_target_pairs={{0,1},{1,0},{2,3},{3,2},{4,5},{5,4},{6,7},{7,6},{8,9},{9,8},{10,11... | collective-permute-start | bytes 3686408 | tf_op jit(solution)/shard_map/ppermute | solution.py:195
  442.6 35.8 %collective-permute-start.80 = (bf16[128,2560]{1,0:T(8,128)(2,1)}, bf16[128,2560]{1,0:T(8,128)(2,1)}, u32[]{:S(2)}, u32[]{:S(2)}) collective-permute-start(bf16[128,2560]{1,0:T(8,128)(2,1)} %add_convert_fusion.6), channel_id=1, source_target_pairs={{8,0},{10,2},{16,8},{18,10},{24,16},{26,18},{28,24},{30,26},{20,28... | collective-permute-start | bytes 1966088 | tf_op jit(solution)/shard_map/ppermute | solution.py:50
  475.4 24.2 %collective-permute-start.87 = (f32[2,2560]{1,0:T(2,128)S(1)}, f32[2,2560]{1,0:T(2,128)S(1)}, u32[]{:S(2)}, u32[]{:S(2)}) collective-permute-start(f32[2,2560]{1,0:T(2,128)S(1)} %pad_maximum_fusion.23), channel_id=1, source_target_pairs={{0,1},{1,0},{2,3},{3,2},{4,5},{5,4},{6,7},{7,6},{8,9},{9,8},{10,11... | collective-permute-start | bytes 61448 | tf_op jit(solution)/shard_map/ppermute | solution.py:195
  478.4 30.6 %collective-permute-start.86 = (bf16[128,2560]{1,0:T(8,128)(2,1)}, bf16[128,2560]{1,0:T(8,128)(2,1)}, u32[]{:S(2)}, u32[]{:S(2)}) collective-permute-start(bf16[128,2560]{1,0:T(8,128)(2,1)} %get-tuple-element.870), channel_id=1, source_target_pairs={{0,1},{1,0},{2,3},{3,2},{4,5},{5,4},{6,7},{7,6},{8,9},{9,8},{10,11... | collective-permute-start | bytes 1966088 | tf_op jit(solution)/shard_map/ppermute | solution.py:195
  499.5 34.2 %collective-permute-start.88 = (bf16[8,96,2560]{2,1,0:T(8,128)(2,1)}, bf16[8,96,2560]{2,1,0:T(8,128)(2,1)}, u32[]{:S(2)}, u32[]{:S(2)}) collective-permute-start(bf16[8,96,2560]{2,1,0:T(8,128)(2,1)} %get-tuple-element.642), channel_id=1, source_target_pairs={{0,2},{2,0},{4,6},{6,4},{8,10},{10,8},{12,14},{14,12},{16,18},{18,... | collective-permute-start | bytes 11796488 | tf_op jit(solution)/shard_map/ppermute | solution.py:191
  507.1 20.7 %collective-permute-start.90 = (bf16[160,2560]{1,0:T(8,128)(2,1)S(1)}, bf16[160,2560]{1,0:T(8,128)(2,1)S(1)}, u32[]{:S(2)}, u32[]{:S(2)}) collective-permute-start(bf16[160,2560]{1,0:T(8,128)(2,1)S(1)} %pad_maximum_fusion.11), channel_id=1, source_target_pairs={{8,0},{10,2},{16,8},{18,10},{24,16},{26,18},{28,24},{30,26},{20,28... | collective-permute-start | bytes 2457608 | tf_op jit(solution)/shard_map/ppermute | solution.py:50
  509.0 20.3 %collective-permute-start.91 = (bf16[160,2560]{1,0:T(8,128)(2,1)}, bf16[160,2560]{1,0:T(8,128)(2,1)S(1)}, u32[]{:S(2)}, u32[]{:S(2)}) collective-permute-start(bf16[160,2560]{1,0:T(8,128)(2,1)} %pad_maximum_fusion.10), channel_id=1, source_target_pairs={{0,8},{2,10},{8,16},{10,18},{16,24},{18,26},{24,28},{26,30},{28,20... | collective-permute-start | bytes 2457608 | tf_op jit(solution)/shard_map/ppermute | solution.py:47
  527.8 38.5 %collective-permute-start.100 = (bf16[240,2560]{1,0:T(8,128)(2,1)S(1)}, bf16[240,2560]{1,0:T(8,128)(2,1)S(1)}, u32[]{:S(2)}, u32[]{:S(2)}) collective-permute-start(bf16[240,2560]{1,0:T(8,128)(2,1)S(1)} %copy-done.46), channel_id=1, source_target_pairs={{0,1},{1,0},{2,3},{3,2},{4,5},{5,4},{6,7},{7,6},{8,9},{9,8},{10,11... | collective-permute-start | bytes 3686408 | tf_op jit(solution)/shard_map/ppermute | solution.py:195
  532.7 21.1 %collective-permute-start.94 = (bf16[160,2560]{1,0:T(8,128)(2,1)S(1)}, bf16[160,2560]{1,0:T(8,128)(2,1)S(1)}, u32[]{:S(2)}, u32[]{:S(2)}) collective-permute-start(bf16[160,2560]{1,0:T(8,128)(2,1)S(1)} %fusion.11), channel_id=1, source_target_pairs={{8,0},{10,2},{16,8},{18,10},{24,16},{26,18},{28,24},{30,26},{20,28... | collective-permute-start | bytes 2457608 | tf_op jit(solution)/shard_map/ppermute | solution.py:50
  533.7 21.1 %collective-permute-start.95 = (bf16[160,2560]{1,0:T(8,128)(2,1)S(1)}, bf16[160,2560]{1,0:T(8,128)(2,1)S(1)}, u32[]{:S(2)}, u32[]{:S(2)}) collective-permute-start(bf16[160,2560]{1,0:T(8,128)(2,1)S(1)} %fusion.12), channel_id=1, source_target_pairs={{0,8},{2,10},{8,16},{10,18},{16,24},{18,26},{24,28},{26,30},{28,20... | collective-permute-start | bytes 2457608 | tf_op jit(solution)/shard_map/ppermute | solution.py:47
  536.2 23.8 %collective-permute-start.92 = (bf16[48,2560]{1,0:T(8,128)(2,1)S(1)}, bf16[48,2560]{1,0:T(8,128)(2,1)S(1)}, u32[]{:S(2)}, u32[]{:S(2)}) collective-permute-start(bf16[48,2560]{1,0:T(8,128)(2,1)S(1)} %slice_bitcast_fusion.10), channel_id=1, source_target_pairs={{8,0},{10,2},{16,8},{18,10},{24,16},{26,18},{28,24},{30,26},{20,28... | collective-permute-start | bytes 737288 | tf_op jit(solution)/shard_map/ppermute | solution.py:50
  540.3 20.0 %collective-permute-start.93 = (bf16[49,2560]{1,0:T(8,128)(2,1)S(1)}, bf16[49,2560]{1,0:T(8,128)(2,1)S(1)}, u32[]{:S(2)}, u32[]{:S(2)}) collective-permute-start(bf16[49,2560]{1,0:T(8,128)(2,1)S(1)} %pad_maximum_fusion.21), channel_id=1, source_target_pairs={{0,8},{2,10},{8,16},{10,18},{16,24},{18,26},{24,28},{26,30},{28,20... | collective-permute-start | bytes 752648 | tf_op jit(solution)/shard_map/ppermute | solution.py:47
  557.8 36.2 %collective-permute-start.103 = (bf16[160,2560]{1,0:T(8,128)(2,1)S(1)}, bf16[160,2560]{1,0:T(8,128)(2,1)S(1)}, u32[]{:S(2)}, u32[]{:S(2)}) collective-permute-start(bf16[160,2560]{1,0:T(8,128)(2,1)S(1)} %fusion.9), channel_id=1, source_target_pairs={{8,0},{10,2},{16,8},{18,10},{24,16},{26,18},{28,24},{30,26},{20,28... | collective-permute-start | bytes 2457608 | tf_op jit(solution)/shard_map/ppermute | solution.py:50
  559.4 34.7 %collective-permute-start.104 = (bf16[160,2560]{1,0:T(8,128)(2,1)S(1)}, bf16[160,2560]{1,0:T(8,128)(2,1)S(1)}, u32[]{:S(2)}, u32[]{:S(2)}) collective-permute-start(bf16[160,2560]{1,0:T(8,128)(2,1)S(1)} %fusion.10), channel_id=1, source_target_pairs={{0,8},{2,10},{8,16},{10,18},{16,24},{18,26},{24,28},{26,30},{28,20... | collective-permute-start | bytes 2457608 | tf_op jit(solution)/shard_map/ppermute | solution.py:47
  564.1 24.1 %collective-permute-start.98 = (bf16[97,2560]{1,0:T(8,128)(2,1)S(1)}, bf16[97,2560]{1,0:T(8,128)(2,1)S(1)}, u32[]{:S(2)}, u32[]{:S(2)}) collective-permute-start(bf16[97,2560]{1,0:T(8,128)(2,1)S(1)} %fusion.76), channel_id=1, source_target_pairs={{8,0},{10,2},{16,8},{18,10},{24,16},{26,18},{28,24},{30,26},{20,28... | collective-permute-start | bytes 1489928 | tf_op jit(solution)/shard_map/ppermute | solution.py:50
  566.3 23.0 %collective-permute-start.99 = (bf16[97,2560]{1,0:T(8,128)(2,1)S(1)}, bf16[97,2560]{1,0:T(8,128)(2,1)S(1)}, u32[]{:S(2)}, u32[]{:S(2)}) collective-permute-start(bf16[97,2560]{1,0:T(8,128)(2,1)S(1)} %pad_maximum_fusion.20), channel_id=1, source_target_pairs={{0,8},{2,10},{8,16},{10,18},{16,24},{18,26},{24,28},{26,30},{28,20... | collective-permute-start | bytes 1489928 | tf_op jit(solution)/shard_map/ppermute | solution.py:47
  (128 other events, 1630.2 us)

commit v3 on v2

--- a/solution.py
+++ b/solution.py
@@ -67,7 +67,7 @@
     def run(self, function, *values):
         values = self.tie(*values)
         out = function(*values) if isinstance(values, tuple) else function(values)
-        self.token = jax.tree.leaves(out)[-1]
+        self.token = tuple(jax.tree.leaves(out))
         return out
 
 
@@ -82,14 +82,18 @@
         self.flight = (value, value)
         self.pairs, self.far = [], None
         self.theirs = [] if both_cores else None
+        self.settled = False
         self.steps = 0
 
     def start(self):
-        if self.theirs is not None:
-            self.theirs.append((core_swap(self.own),))
         self.send()
+        self.swap(self.own)
         for _ in range(self.ring.reach - SHOWN):
             self.next()
+
+    def swap(self, *values):
+        if self.theirs is not None:
+            self.theirs.append(tuple(core_swap(v) for v in values))
 
     def send(self):
         self.steps += 1
@@ -99,18 +103,29 @@
         self.flight = (self.ring.up(u), self.ring.down(d))
 
     def land(self):
-        self.flight = self.order.arrive(*self.flight)
-        if self.theirs is not None:
-            self.theirs.append(tuple(core_swap(v) for v in self.flight))
+        swapped = self.theirs.pop() if self.theirs and not self.settled else ()
+        self.settled = False
+        landed = self.order.arrive(*swapped, *self.flight)
+        self.flight = landed[len(swapped) :]
+        if swapped:
+            self.theirs.append(landed[: len(swapped)])
 
     def next(self):
         self.land()
-        self.pairs.append(self.flight)
+        landed = self.flight
+        self.pairs.append(landed)
         self.send()
+        self.swap(*landed)
+
+    def settle(self):
+        swapped = self.order.arrive(*self.theirs.pop())
+        self.theirs.append(swapped)
+        self.settled = True
 
     def finish(self):
         self.land()
         self.far = self.flight
+        self.swap(*self.far)
 
 
 class Scatter:
@@ -189,6 +204,29 @@
 def core_swap(value):
     count = lax.axis_size("dp")
     return lax.ppermute(value, "dp", [(i, i ^ 1) for i in range(count)])
+
+
+def holder_groups():
+    return [
+        [(2 * chip + core) * 2 + side for core in range(2) for side in range(2)]
+        for chip in range(lax.axis_size("dp") // 2)
+    ]
+
+
+def holders_gather(value):
+    return lax.all_gather(
+        value, ("dp", "tensor"), axis=0, tiled=True, axis_index_groups=holder_groups()
+    )
+
+
+def holders_sum(value):
+    return lax.psum_scatter(
+        value,
+        ("dp", "tensor"),
+        scatter_dimension=0,
+        tiled=True,
+        axis_index_groups=holder_groups(),
+    )
 
 
 def tensor_swap(value):
@@ -432,6 +470,8 @@
 
 
 BIG = pltpu.CompilerParams(vmem_limit_bytes=48 << 20)
+LIGHT = pl.CostEstimate(flops=0, bytes_accessed=0, transcendentals=0)
+HEAVY = pl.CostEstimate(flops=500_000_000_000, bytes_accessed=0, transcendentals=0)
 
 
 def shaped(rows, width, dtype=F32):
@@ -464,11 +504,7 @@
             shaped(2, width),
         ],
         scratch_shapes=[pltpu.VMEM((rows, width), F32)] * 2,
-        cost_estimate=pl.CostEstimate(
-            flops=4 * rows * width * BLOCK,
-            bytes_accessed=18 * rows * width,
-            transcendentals=6 * rows * width,
-        ),
+        cost_estimate=LIGHT,
         compiler_params=BIG,
     )(padded, marks, params, w_gates, w_gates)
 
@@ -505,11 +541,7 @@
             pltpu.VMEM((rows, width), F32),
             pltpu.VMEM((8, width), F32),
         ],
-        cost_estimate=pl.CostEstimate(
-            flops=2 * rows * width * depth,
-            bytes_accessed=2 * (rows + width) * depth + 26 * rows * width,
-            transcendentals=rows * width,
-        ),
+        cost_estimate=LIGHT,
         compiler_params=BIG,
     )(dz, wide, pre, decay, prods, state, incoming)
 
@@ -547,11 +579,7 @@
             shaped(8, width),
             shaped(BLOCK, 2 * width, BF16),
         ],
-        cost_estimate=pl.CostEstimate(
-            flops=12 * rows * width * BLOCK,
-            bytes_accessed=24 * rows * width,
-            transcendentals=6 * rows * width,
-        ),
+        cost_estimate=HEAVY,
         compiler_params=BIG,
     )(rev_p, rev_s, later, prods, state, incoming, mixed, padded, marks, params, w_gates, w_gates)
 
@@ -629,9 +657,7 @@
             pltpu.SemaphoreType.DMA((len(chunks),)),
             pltpu.SemaphoreType.DMA((places * len(sizes),)),
         ],
-        cost_estimate=pl.CostEstimate(
-            flops=0, bytes_accessed=4 * places * rows * width, transcendentals=0
-        ),
+        cost_estimate=LIGHT,
         compiler_params=BIG,
     )(at, *chunks)
 
@@ -713,11 +739,7 @@
             pltpu.VMEM((pairs, channels, width), BF16),
             pltpu.SemaphoreType.DMA((2 * chips * (pairs + (extra is not None)),)),
         ],
-        cost_estimate=pl.CostEstimate(
-            flops=2 * pairs * rows * channels * width,
-            bytes_accessed=2 * pairs * (channels * width + rows * (channels + width)),
-            transcendentals=0,
-        ),
+        cost_estimate=LIGHT,
         compiler_params=BIG,
     )(
         jnp.stack(at + [ring.core]).astype(jnp.int32),
@@ -725,6 +747,233 @@
         *rights,
         *(() if extra is None else (extra,)),
     )
+
+
+def hidden_grad_body(heights, right_heights, which, *refs):
+    count = len(right_heights)
+    lefts, rights = refs[: len(heights)], refs[len(heights) : len(heights) + count]
+    out_ref, turned, held, made, in_sems, out_sems = refs[-6:]
+    parts, _, columns = held.shape
+    holders, _, unit, _ = out_ref.shape
+    loads, stores = [], []
+    for part in range(parts):
+        first = 0
+        for i, height in enumerate(right_heights):
+            loads.append(
+                pltpu.make_async_copy(
+                    rights[i].at[:, pl.ds(part * columns, columns)],
+                    held.at[part, pl.ds(first, height)],
+                    in_sems.at[part * count + i],
+                )
+            )
+            loads[-1].start()
+            first += height
+    first = 0
+    for left, height in zip(lefts, heights):
+        turned[:, first : first + height] = left[...].astype(F32).T.astype(BF16)
+        first += height
+    for part in range(parts):
+        for load in loads[part * count : (part + 1) * count]:
+            load.wait()
+
+        def column(n, _, part=part):
+            here = pl.ds(pl.multiple_of(n * BLOCK, BLOCK), BLOCK)
+            made[part, :, here] = jnp.dot(
+                turned[...], held[part, :, here], preferred_element_type=F32
+            ).astype(BF16)
+            return 0
+
+        lax.fori_loop(0, columns // BLOCK, column, 0)
+        for holder in range(holders):
+            stores.append(
+                pltpu.make_async_copy(
+                    made.at[part, pl.ds(holder * unit, unit)],
+                    out_ref.at[holder, which, :, pl.ds(part * columns, columns)],
+                    out_sems.at[part * holders + holder],
+                )
+            )
+            stores[-1].start()
+    for store in stores:
+        store.wait()
+
+
+def hidden_grad(which, into, lefts, rights):
+    heights = [left.shape[0] for left in lefts]
+    right_heights = [right.shape[0] for right in rights]
+    depth, width = lefts[0].shape[1], rights[0].shape[1]
+    unit = depth // 4
+    if unit % 16 or any(height % 128 for height in heights):
+        grad = rows_inner(jnp.concatenate(lefts), jnp.concatenate(rights)).astype(BF16)
+        grad = grad.reshape(4, 1, unit, width)
+        return grad if into is None else jnp.concatenate([into, grad], axis=1)
+    parts = 2
+    in_vmem = pl.BlockSpec(memory_space=pltpu.VMEM)
+    anywhere = pl.BlockSpec(memory_space=pl.ANY)
+    more = () if into is None else (into,)
+    return pl.pallas_call(
+        functools.partial(hidden_grad_body, heights, right_heights, which),
+        out_shape=jax.ShapeDtypeStruct((4, 3, unit, width), BF16),
+        in_specs=[in_vmem] * len(lefts) + [anywhere] * (len(rights) + len(more)),
+        out_specs=anywhere,
+        input_output_aliases={len(lefts) + len(rights): 0} if more else {},
+        scratch_shapes=[
+            pltpu.VMEM((depth, sum(heights)), BF16),
+            pltpu.VMEM((parts, sum(heights), width // parts), BF16),
+            pltpu.VMEM((parts, depth, width // parts), BF16),
+            pltpu.SemaphoreType.DMA((parts * len(rights),)),
+            pltpu.SemaphoreType.DMA((parts * 4,)),
+        ],
+        cost_estimate=LIGHT,
+        compiler_params=BIG,
+    )(*lefts, *rights, *more)
+
+
+def piece_body(count, cuts, tiles, *refs):
+    ins, dys, weights = refs[:count], refs[count : 2 * count], refs[2 * count : 2 * count + 3]
+    act_ref, d_gate_ref, d_up_ref = refs[2 * count + 3 : 2 * count + 6]
+    outs = refs[2 * count + 6 : 2 * count + 6 + len(cuts)]
+    h, dy, w_g, w_u, w_d, total, row_sems, w_sems = refs[2 * count + 6 + len(cuts) :]
+    row_loads, w_loads = [], []
+    for to, sources in ((h, ins), (dy, dys)):
+        first = 0
+        for source in sources:
+            size = source.shape[0]
+            row_loads.append(
+                pltpu.make_async_copy(
+                    source, to.at[pl.ds(first, size)], row_sems.at[len(row_loads)]
+                )
+            )
+            row_loads[-1].start()
+            first += size
+    for low, high in tiles:
+        here = pl.ds(low, high - low)
+        for source, to in zip(weights, (w_g, w_u, w_d)):
+            w_loads.append(
+                pltpu.make_async_copy(source.at[here], to.at[here], w_sems.at[len(w_loads)])
+            )
+            w_loads[-1].start()
+    for load in row_loads:
+        load.wait()
+    for i, (low, high) in enumerate(tiles):
+        for load in w_loads[3 * i : 3 * i + 3]:
+            load.wait()
+        gate_act, slope = gelu_and_slope(cols_inner(h[...], w_g[low:high, :]))
+        up_val = cols_inner(h[...], w_u[low:high, :])
+        d_act = cols_inner(dy[...], w_d[low:high, :])
+        d_gate = (d_act * up_val * slope).astype(BF16)
+        d_up = (d_act * gate_act).astype(BF16)
+        act_ref[:, low:high] = (gate_act * up_val).astype(BF16)
+        d_gate_ref[:, low:high] = d_gate
+        d_up_ref[:, low:high] = d_up
+        part = jnp.dot(d_gate, w_g[low:high, :], preferred_element_type=F32) + jnp.dot(
+            d_up, w_u[low:high, :], preferred_element_type=F32
+        )
+        total[...] = part if i == 0 else total[...] + part
+    first = 0
+    for out, size in zip(outs, cuts):
+        out[...] = total[first : first + size, :].astype(BF16)
+        first += size
+
+
+def piece(hs, dys, cuts, w_g, w_u, w_d):
+    depth, width = w_g.shape
+    rows = sum(cuts)
+    tiles = [(low, min(low + BLOCK, depth)) for low in range(0, depth, BLOCK)]
+    in_vmem = pl.BlockSpec(memory_space=pltpu.VMEM)
+    anywhere = pl.BlockSpec(memory_space=pl.ANY)
+    return pl.pallas_call(
+        functools.partial(piece_body, len(hs), cuts, tiles),
+        out_shape=[shaped(rows, depth, BF16)] * 3 + [shaped(cut, width, BF16) for cut in cuts],
+        in_specs=[anywhere] * (2 * len(hs) + 3),
+        out_specs=[in_vmem] * (3 + len(cuts)),
+        scratch_shapes=[
+            pltpu.VMEM((rows, width), BF16),
+            pltpu.VMEM((rows, width), BF16),
+            pltpu.VMEM((depth, width), BF16),
+            pltpu.VMEM((depth, width), BF16),
+            pltpu.VMEM((depth, width), BF16),
+            pltpu.VMEM((rows, width), F32),
+            pltpu.SemaphoreType.DMA((2 * len(hs),)),
+            pltpu.SemaphoreType.DMA((3 * len(tiles),)),
+        ],
+        cost_estimate=LIGHT,
+        compiler_params=BIG,
+    )(*hs, *dys, w_g, w_u, w_d)
+
+
+def widen_body(in_ref, *outs):
+    first = 0
+    for out in outs:
+        size = out.shape[0]
+        out[...] = in_ref[first : first + size, :].astype(F32)
+        first += size
+
+
+def widen(value, parts):
+    rows, width = value.shape
+    if rows // parts % 16:
+        return [v.astype(F32) for v in jnp.split(value, parts)]
+    columns = 2 * BLOCK
+    size = rows // parts
+    return pl.pallas_call(
+        widen_body,
+        grid=(width // columns,),
+        in_specs=[pl.BlockSpec((rows, columns), lambda n: (0, n))],
+        out_specs=[pl.BlockSpec((size, columns), lambda n: (0, n))] * parts,
+        out_shape=[shaped(size, width)] * parts,
+        cost_estimate=LIGHT,
+        compiler_params=BIG,
+    )(value)
+
+
+def hidden_down_body(count, *refs):
+    acts, w_ref, outs = refs[:count], refs[count], refs[count + 1 :]
+    columns = 2 * BLOCK
+
+    def column(n, _):
+        here = pl.ds(pl.multiple_of(n * columns, columns), columns)
+        for act, out in zip(acts, outs):
+            out[:, here] = jnp.dot(
+                act[...], w_ref[:, here], preferred_element_type=F32
+            ).astype(BF16)
+        return 0
+
+    lax.fori_loop(0, w_ref.shape[1] // columns, column, 0)
+
+
+def hidden_down(acts, w_down):
+    depth, width = w_down.shape
+    if sum(a.shape[0] for a in acts) > 2048:
+        return [jnp.dot(a, w_down, preferred_element_type=F32).astype(BF16) for a in acts]
+    in_vmem = pl.BlockSpec(memory_space=pltpu.VMEM)
+    return pl.pallas_call(
+        functools.partial(hidden_down_body, len(acts)),
+        out_shape=[shaped(a.shape[0], width, BF16) for a in acts],
+        in_specs=[in_vmem] * (len(acts) + 1),
+        out_specs=[in_vmem] * len(acts),
+        cost_estimate=LIGHT,
+        compiler_params=BIG,
+    )(*acts, w_down)
+
+
+def input_back_body(x_ref, mine_ref, got_ref, d_x_ref, gain_ref, out_ref):
+    x = x_ref[...].astype(F32)
+    scaled = (mine_ref[...] + got_ref[...].astype(F32)) * gain_ref[...]
+    r = lax.rsqrt(jnp.mean(x * x, axis=-1, keepdims=True) + EPS)
+    along = jnp.mean(scaled * x, axis=-1, keepdims=True)
+    out_ref[...] = d_x_ref[...] + r * scaled - (r * r * r) * along * x
+
+
+def input_back(x, mine, got, d_x, gain):
+    in_vmem = pl.BlockSpec(memory_space=pltpu.VMEM)
+    return pl.pallas_call(
+        input_back_body,
+        out_shape=shaped(*x.shape),
+        in_specs=[in_vmem] * 5,
+        out_specs=in_vmem,
+        cost_estimate=LIGHT,
+        compiler_params=BIG,
+    )(x, mine, got, d_x, gain)
 
 
 def ring_parts(mine, theirs):
@@ -781,11 +1030,11 @@
         [jnp.swapaxes(w, 0, 1).reshape(n_gate, channels) for w in (w_input_gate, w_decay_gate)],
         axis=1,
     )
-    x_other = tensor_swap(block_input)
     one = Gather(ring, order, jnp.concatenate([w_signal.T, gates, small]), True)
     order.token = one.own
     one.start()
-    hid_own = order.run(lambda *w: jnp.stack(w), w_gate.T, w_up.T, w_down)
+    x_other = tensor_swap(block_input)
+    hid_g, hid_u, hid_d = [holders_gather(w) for w in (w_gate.T, w_up.T, w_down)]
     pack_two = order.run(lambda *w: jnp.concatenate(w), w_branch.T, w_mixout)
     cumulative = jnp.cumsum(starts)
     padded_cum = jnp.concatenate([jnp.zeros((lag,), jnp.int32), cumulative])
@@ -795,10 +1044,9 @@
     ]
     marks = jnp.stack(masks + [starts.astype(F32)] * (8 - CONV), axis=1)
     tail_keep = (cumulative[group - 1] - cumulative[group - HALO :] == 0)[:, None]
+    one.next()
     x_low = order.run(functools.partial(ordered, side), block_input, x_other)
     halo = from_behind(x_low[group - HALO :] * tail_keep.astype(BF16), 1)
-    hid_other = tensor_swap(order.tie(hid_own))
-    one.next()
     one.next()
     one.next()
 
@@ -829,14 +1077,14 @@
     )
     enter = Entering(order, ends, hops, False)
     two.next()
+    two.settle()
     enter.next()
+    incoming = enter.finish()
     two.next()
+    hid_g = order.arrive(hid_g)
+    two.finish()
     dy = Gather(ring, order, cotangent)
     dy.start()
-    incoming = enter.finish()
-    hid_other = order.arrive(hid_other)
-    hid_theirs = core_swap(hid_own), core_swap(hid_other)
-    two.finish()
     wide_b, wide_o = order.run(
         lambda *_: assemble(ring, (shard, shard), two), two.theirs[-1][0]
     )
@@ -857,10 +1105,6 @@
     mix_got = tensor_swap(mix_theirs)
     mix_mine = order.run(lambda m, w: mix_out(m, w, mine_at), merged, wide_o)
     dy.next()
-    hidden = order.run(
-        lambda *parts: jnp.concatenate(parts, axis=1), hid_own, hid_other, *hid_theirs
-    )
-    hid_g, hid_u, hid_d = hidden[0], hidden[1], hidden[2]
     x_val = block_input.astype(F32)
     x_one = order.run(lambda x, m, t: x + m + t.astype(F32), x_val, mix_mine, mix_got)
     n_two, norm_two_back = jax.vjp(normed, x_one, gain_two)
@@ -868,10 +1112,25 @@
 
     ff = Gather(ring, order, h_own)
     ff.start()
-    dy.next()
     acts, d_gates, d_ups, d_hs, h_list, dy_list = [], [], [], [], [], []
 
-    def piece(h_piece, dy_piece, w_g, w_u, w_d):
+    def do_piece(hs, dys, cuts):
+        count = len(hs)
+        out = order.run(
+            lambda *v: piece(v[:count], v[count : 2 * count], cuts, *v[2 * count :]),
+            *hs,
+            *dys,
+            hid_g,
+            hid_u,
+            hid_d,
+        )
+        for kept, value in zip((acts, d_gates, d_ups), out):
+            kept.append(value)
+        d_hs.extend(out[3:])
+        h_list.extend(hs)
+        dy_list.extend(dys)
+
+    def plain_piece(h_piece, dy_piece, w_g, w_u, w_d):
         gate_pre = cols_inner(h_piece, w_g)
         up_val = cols_inner(h_piece, w_u)
         gate_act, slope = gelu_and_slope(gate_pre)
@@ -884,12 +1143,18 @@
         )
         return act, d_gate, d_up, d_h.astype(BF16)
 
-    def do_piece(h_piece, dy_piece):
-        out = order.run(piece, h_piece, dy_piece, hid_g, hid_u, hid_d)
-        for kept, value in zip((acts, d_gates, d_ups, d_hs, h_list, dy_list), (*out, h_piece, dy_piece)):
+    def do_plain(hs, dys):
+        h_piece, dy_piece = jnp.concatenate(hs), jnp.concatenate(dys)
+        out = order.run(plain_piece, h_piece, dy_piece, hid_g, hid_u, hid_d)
+        for kept, value in zip((acts, d_gates, d_ups, h_list, dy_list), (*out[:3], h_piece, dy_piece)):
             kept.append(value)
-
-    do_piece(h_own, cotangent)
+        parts = [out[3]]
+        if h_piece.shape[0] > rows:
+            parts = [out[3][:rows], out[3][rows:]]
+        d_hs.extend(parts)
+
+    do_piece((h_own,), (cotangent,), (rows,))
+    dy.next()
     for step in range(ring.reach - SHOWN, ring.reach - 1):
         ff.next()
         if step == ring.reach - SHOWN:
@@ -899,9 +1164,9 @@
         if step == ring.reach - 3:
             dy.finish()
         for k in range(first, step + 1):
-            do_piece(jnp.concatenate(ff.pairs[k]), jnp.concatenate(dy.pairs[k]))
+            do_plain(ff.pairs[k], dy.pairs[k])
     ff.finish()
-    do_piece(jnp.concatenate(ff.far), jnp.concatenate(dy.far))
+    do_plain(ff.far, dy.far)
 
     def chunks(parts):
         out = plain_parts(parts[:1])
@@ -910,28 +1175,26 @@
             out += [Part(lambda v: v[rows:].astype(F32), pair)]
         return out + plain_parts(parts[-1:])
 
-    back = Scatter(ring, order, chunks(d_hs), rows // 2)
+    back = Scatter(ring, order, plain_parts(d_hs), rows // 2)
     back.start()
-    downs = [
-        order.run(lambda a, w: jnp.dot(a, w, preferred_element_type=F32).astype(BF16), a, hid_d)
-        for a in acts
-    ]
-
-    def hidden_grad(lefts, rights):
+    def run_grad(which, into, lefts, rights):
+        count, every = len(lefts), len(lefts) + len(rights)
+        more = () if into is None else (into,)
         return order.run(
-            lambda a, b: rows_inner(a, b).astype(BF16),
-            jnp.concatenate(lefts),
-            jnp.concatenate(rights),
+            lambda *v: hidden_grad(
+                which, v[every] if more else None, v[:count], v[count:every]
+            ),
+            *lefts,
+            *rights,
+            *more,
         )
 
     back.next()
-    g_gate = hidden_grad(d_gates, h_list)
+    downs = order.run(lambda *v: hidden_down(v[:-1], v[-1]), *acts, hid_d)
     back.next()
-    g_up = hidden_grad(d_ups, h_list)
+    hid_grads = run_grad(0, None, d_gates, h_list)
     back.next()
-    g_down = hidden_grad(acts, dy_list)
-    unit = g_gate.shape[0] // 4
-    hid_back = [core_swap(g[2 * unit :]) for g in (g_gate, g_up, g_down)]
+    hid_grads = run_grad(1, hid_grads, d_ups, h_list)
 
     def dense_back(d_h, dy_own):
         d_x, g_gain = norm_two_back(d_h)
@@ -942,26 +1205,10 @@
     dz_other = tensor_swap(dz_own)
     down = Scatter(ring, order, chunks(downs), rows // 2)
     down.start()
-    hid_mine, hid_got = [], []
-
-    def hidden_add(g, t):
-        mine, send = order.run(
-            lambda a, b: (
-                a[:unit].astype(F32) + b[:unit].astype(F32),
-                plus(a[unit : 2 * unit], b[unit:]),
-            ),
-            g,
-            t,
-        )
-        hid_mine.append(mine)
-        hid_got.append(send)
-
-    hidden_add(g_gate, hid_back[0])
-    hidden_add(g_up, hid_back[1])
+    hid_grads = run_grad(2, hid_grads, acts, dy_list)
+    hid_grads = holders_sum(hid_grads.reshape(-1, width))
     down.next()
-    hidden_add(g_down, hid_back[2])
     d_mix = order.run(functools.partial(ordered, side), dz_own, dz_other)
-    hid_got = [tensor_swap(order.tie(send)) for send in hid_got]
     d_branch, rev_prods, rev_state, back_ends = order.run(
         back_scan, d_mix, wide_o, branch_pre, decay, prods, local_state, incoming
     )
@@ -971,9 +1218,9 @@
         lambda *v: ring_grads(ring, shard, v[:2], v[2:]), d_branch, merged, h_one, d_mix
     )
     theirs_two = core_swap(theirs_two)
+    down.next()
     leave.next()
     later = leave.finish()
-    down.next()
     d_sig, sig_tail, rim, sums, g_gates = order.run(
         back_mix,
         rev_prods,
@@ -991,6 +1238,7 @@
     rim = from_behind(rim, -1)
     ring_two = Scatter(ring, order, ring_parts(mine_two, theirs_two), shard)
     ring_two.start()
+    block_output = down.finish(lambda d, x: (x + d).astype(BF16), x_one)
 
     def with_rim(sig, tail, edge):
         tail = tail + edge * tail_keep[HALO - 8 :].astype(F32)
@@ -1009,6 +1257,12 @@
         functools.partial(d_h_rows, at=theirs_at), d_branch, d_signal, wide_b, wide_s
     )
     d_h_got = tensor_swap(d_h_theirs.astype(BF16))
+    ring_two.next()
+
+    mine_last, theirs_last = order.run(
+        lambda a, b, g: ring_grads(ring, shard, (a,), (b,), g), d_signal, h_one, g_gates
+    )
+    theirs_last = core_swap(theirs_last)
     d_h_mine = order.run(
         functools.partial(d_h_rows, at=mine_at), d_branch, d_signal, wide_b, wide_s
     )
@@ -1023,12 +1277,7 @@
     gains = order.run(gain_sum, d_h_mine, d_h_theirs, block_input, x_other, g_gain_two)
     gains_other = tensor_swap(gains)
     ring_two.next()
-    block_output = down.finish(lambda d, x: (x + d).astype(BF16), x_one)
-
-    mine_last, theirs_last = order.run(
-        lambda a, b, g: ring_grads(ring, shard, (a,), (b,), g), d_signal, h_one, g_gates
-    )
-    theirs_last = core_swap(theirs_last)
+
     n_rows = shard * (CONV + 1) + 2 * n_gain
 
     def small_rows(total, gain, gain_other):
@@ -1045,13 +1294,6 @@
 
     smalls = order.run(small_rows, sums, gains, gains_other)
     smalls_other = core_swap(smalls)
-
-    def input_back(mine, got, d_x):
-        _, norm_one_back = jax.vjp(lambda v: normed(v, gain_one), x_val)
-        return d_x + norm_one_back(mine + got.astype(F32))[0]
-
-    grad_input = order.run(input_back, d_h_mine, d_h_got, d_x_one)
-    ring_two.next()
     smalls = order.run(
         lambda a, b: jnp.pad(a + b, ((0, 0), (0, width - n_rows))), smalls, smalls_other
     )
@@ -1071,20 +1313,25 @@
         [last_part(k, distance) for k, distance in enumerate(ring_distances(ring))],
         (shard + n_gate) // 32 * 16 or shard // 2,
     )
+    grad_input = order.run(
+        input_back, block_input, d_h_mine, d_h_got, d_x_one, gain_one[None, :]
+    )
+    def land_both():
+        flight = order.arrive(*ring_two.flight, *ring_last.flight)
+        ring_two.flight, ring_last.flight = flight[:2], flight[2:]
+
     ring_last.start()
-    hid_sums = [
-        order.run(lambda a, b: a + b.astype(F32), mine, got)
-        for mine, got in zip(hid_mine[:2], hid_got[:2])
-    ]
+    land_both()
     ring_two.next()
     ring_last.next()
-    hid_sums.append(order.run(lambda a, b: a + b.astype(F32), hid_mine[2], hid_got[2]))
-    s_gate, s_up, s_down = hid_sums[0].T, hid_sums[1].T, hid_sums[2]
+    land_both()
     ring_last.next()
     total_two = ring_two.finish()
     s_branch = total_two[:shard].T
     s_mixout = total_two[shard:]
     ring_last.next()
+    s_gate, s_up, s_down = order.run(lambda g: widen(g, 3), hid_grads)
+    s_gate, s_up = s_gate.T, s_up.T
     last = ring_last.finish()
     s_signal = last[:shard].T
     s_gates = [

time: 636 us -> 603 us (0.948)
  Pallas kernels: 57.9 us -> 116 us
  matrix products: 93.6 us -> 57.9 us
  local copies, waits for them, and re-layouts: 67.9 us -> 42.5 us
  starting transfers between devices: 123 us -> 104 us
  other arithmetic: 88.3 us -> 71.2 us
  between operations: 2.72 us -> 16.6 us
    pallas_call x0 -> x7, Pallas kernels: none -> 57.3 us  [the longest x3 29.2 us: hidden_grad(): pl.pallas_call(functools.partial(hidden_grad_body, heights, right_heights...]
    dot_general x18 -> x8, matrix products: 42.3 us -> 12.1 us  [the longest x4 6.64 us: plain_piece(): jnp.dot(d_up, w_u, preferred_element_type=F32)]
    add x7 -> x0, other arithmetic: 17.8 us -> none  [the longest x3 7.95 us: per_device(): a + b.astype(F32)]
    unnamed x162 -> x224, local copies, waits for them, and re-layouts: 39.1 us -> 22.4 us
    convert_element_type x24, other arithmetic: 15.3 us -> 25.6 us  [__call__(): return total.astype(dtype)]
    ppermute x26 -> x21, starting transfers between devices: 15.9 us -> 6.82 us  [core_swap(): return lax.ppermute(value, 'dp', [(i, i ^ 1) for i in range(count)])]
    ppermute x32, waiting for transfers between devices: 102 us -> 93.3 us  [down(): return lax.ppermute(value, 'dp', self.down_route)]
    ppermute x32, waiting for transfers between devices: 68.1 us -> 75.4 us  [up(): return lax.ppermute(value, 'dp', self.up_route)]
  transfers between devices with their start and end apart: 107 -> 102, of which waited for: 49 -> 48; matrix products, arithmetic and copies ran while one was open for 31% -> 22% of each run, Pallas kernels for 8% -> 19%
where the time goes in v3:
time: 603 us; the launch traced here: 594 us
  waiting for transfers between devices  186 us (31%)
  Pallas kernels  116 us (19%)
  starting transfers between devices  104 us (17%)
  other arithmetic  71.2 us (12%)
  matrix products  57.9 us (10%)
  local copies, waits for them, and re-layouts  42.5 us (7%)
  between operations  16.6 us (3%)
    ppermute x32, waiting for transfers between devices, down(): return lax.ppermute(value, 'dp', self.down_route)  93.3 us
    ppermute x32, waiting for transfers between devices, up(): return lax.ppermute(value, 'dp', self.up_route)  75.4 us
    ppermute x32, starting transfers between devices, up(): return lax.ppermute(value, 'dp', self.up_route)  38.7 us
    ppermute x32, starting transfers between devices, down(): return lax.ppermute(value, 'dp', self.down_route)  33.6 us
    dot_general x14, matrix products, cols_inner(): lax.dot_general(left, right, (((1,), (1,)), ((), ())), preferred_element_...  32.9 us
    pallas_call x3, Pallas kernels, hidden_grad(): pl.pallas_call(functools.partial(hidden_grad_body, heights, right_heights...  29.2 us
    convert_element_type x24, other arithmetic, __call__(): return total.astype(dtype)  25.6 us
    unnamed x224, local copies, waits for them, and re-layouts  22.4 us
  transfers between devices with their start and end apart: 102, of which 48 were waited for; matrix products, arithmetic and copies ran while one was open for 22% of the time, Pallas kernels for 19%

profile of v3, /device:TPU:0, one launch (start us, length us, event | category | flops | bytes accessed | tf_op | source)
XLA Modules:
  0.0 594.4 jit_solution(3399271736009044619)
XLA Ops:
  9.9 2.6 collective-permute-start.2
  16.5 9.5 %collective-permute-done.2.refs_2_ = bf16[112,2560]{1,0:T(8,128)(2,1)S(1)} collective-permute-done((bf16[112,2560]{1,0:T(8,128)(2,1)S(1)}, bf16[112,2560]{1,0:T(8,128)(2,1)S(1)}, u32[]{:S(2)}, u32[]{:S(2)}) %collective-permute-start.2) | collective-permute-done | bytes 573472 | tf_op jit(solution)/shard_map/ppermute | solution.py:47
  32.6 4.6 collective-permute-done
  37.1 4.8 collective-permute-done.7.refs_6_
  48.1 11.2 %collective-permute-done.11.refs_10_ = bf16[112,2560]{1,0:T(8,128)(2,1)} collective-permute-done((bf16[112,2560]{1,0:T(8,128)(2,1)}, bf16[112,2560]{1,0:T(8,128)(2,1)}, u32[]{:S(2)}, u32[]{:S(2)}) %collective-permute-start.11) | collective-permute-done | bytes 573472 | tf_op jit(solution)/shard_map/ppermute | solution.py:47
  71.0 4.9 collective-permute-done.16.refs_15_
  81.0 7.4 %shard_map.254 = (bf16[1280,2560]{1,0:T(8,128)(2,1)}, bf16[256,2560]{1,0:T(8,128)(2,1)}, bf16[256,2560]{1,0:T(8,128)(2,1)}) custom-call(s32[16]{0:T(128)S(1)} %stack.173.at_ref, bf16[112,2560]{1,0:T(8,128)(2,1)S(1)} %pad_maximum_fusion.9.refs_0_, bf16[112,2560]{1,0:T(8,128)(2,1)S(1)} %collective-permute-done.1.refs_1_, bf16[112,2560]{1,0:T(8,128)(2,1)S(1)} %copy-done.32, ...), custom_call_target="tpu_custom_call" | custom-call | tf_op jit(solution)/shard_map/pallas_call | solution.py:650
  93.2 6.1 %collective-permute-done.20.refs_2_ = bf16[160,2560]{1,0:T(8,128)(2,1)} collective-permute-done((bf16[160,2560]{1,0:T(8,128)(2,1)S(1)}, bf16[160,2560]{1,0:T(8,128)(2,1)}, u32[]{:S(2)}, u32[]{:S(2)}) %collective-permute-start.20) | collective-permute-done | bytes 819232 | tf_op jit(solution)/shard_map/ppermute | solution.py:47
  103.0 6.1 %convolution_convert_fusion.1.pad_ref.refs_7_ = bf16[272,1280]{1,0:T(8,128)(2,1)} fusion(bf16[272,2560]{1,0:T(8,128)(2,1)} %fusion.6, bf16[1280,2560]{1,0:T(8,128)(2,1)} %get-tuple-element.710), kind=kOutput, calls=%fused_computation.16 | convolution fusion | flops 1782927360 | bytes 8642560 | tf_op jit(solution)/shard_map/dot_general | solution.py:298
  110.3 6.6 %shard_map.255 = (bf16[256,1280]{1,0:T(8,128)(2,1)S(1)}, f32[256,1280]{1,0:T(8,128)S(1)}, f32[256,1280]{1,0:T(8,128)S(1)}, f32[256,1280]{1,0:T(8,128)S(1)}, f32[2,1280]{1,0:T(2,128)S(1)}) custom-call(bf16[272,1280]{1,0:T(8,128)(2,1)S(1)} %copy-done.25, f32[256,8]{1,0:T(8,128)S(1)} %copy.139.marks_ref, ...), custom_call_target="tpu_custom_call" | custom-call | tf_op jit(solution)/shard_map/pallas_call | solution.py:483
  126.3 3.8 collective-permute-start.32
  130.1 3.3 collective-permute-start.31
  133.4 11.7 %collective-permute-done.32 = f32[2,1280]{1,0:T(2,128)S(1)} collective-permute-done((f32[2,1280]{1,0:T(2,128)S(1)}, f32[2,1280]{1,0:T(2,128)S(1)}, u32[]{:S(2)}, u32[]{:S(2)}) %collective-permute-start.32) | collective-permute-done | bytes 10272 | tf_op jit(solution)/shard_map/ppermute | solution.py:239
  151.3 10.0 %collective-permute-done.36.refs_15_ = bf16[80,2560]{1,0:T(8,128)(2,1)} collective-permute-done((bf16[80,2560]{1,0:T(8,128)(2,1)}, bf16[80,2560]{1,0:T(8,128)(2,1)}, u32[]{:S(2)}, u32[]{:S(2)}) %collective-permute-start.36) | collective-permute-done | bytes 409632 | tf_op jit(solution)/shard_map/ppermute | solution.py:50
  168.1 10.0 %shard_map.256 = (bf16[1280,2560]{1,0:T(8,128)(2,1)}, bf16[1280,2560]{1,0:T(8,128)(2,1)}) custom-call(s32[16]{0:T(128)S(1)} %stack.173.at_ref, bf16[160,2560]{1,0:T(8,128)(2,1)S(1)} %constant_dynamic-update-slice_fusion.refs_0_, bf16[160,2560]{1,0:T(8,128)(2,1)S(1)} %copy-done.24, bf16[160,2560]{1,0:T(8,128)(2,1)} %collective-permute-done.20.refs_2_, ...), custom_call_target="tpu_custom_call" | custom-call | tf_op jit(solution)/shard_map/pallas_call | solution.py:650
  179.1 4.9 fusion.131.pre_ref
  194.7 8.7 %collective-permute-done.42 = bf16[128,2560]{1,0:T(8,128)(2,1)S(1)} collective-permute-done((bf16[128,2560]{1,0:T(8,128)(2,1)}, bf16[128,2560]{1,0:T(8,128)(2,1)S(1)}, u32[]{:S(2)}, u32[]{:S(2)}) %collective-permute-start.42) | collective-permute-done | bytes 655392 | tf_op jit(solution)/shard_map/ppermute | solution.py:47
  210.9 11.9 %shard_map.257 = (bf16[128,960]{1,0:T(8,128)(2,1)S(1)}, bf16[128,960]{1,0:T(8,128)(2,1)S(1)}, bf16[128,960]{1,0:T(8,128)(2,1)S(1)}, bf16[128,2560]{1,0:T(8,128)(2,1)S(1)}) custom-call(bf16[128,2560]{1,0:T(8,128)(2,1)S(1)} %multiply_convert_fusion.refs_0_.refs_5_, bf16[128,2560]{1,0:T(8,128)(2,1)S(1)} %copy-done.2, ...), custom_call_target="tpu_custom_call" | custom-call | tf_op jit(solution)/shard_map/pallas_call | solution.py:884
  224.1 11.5 %collective-permute-done.46 = bf16[128,2560]{1,0:T(8,128)(2,1)S(1)} collective-permute-done((bf16[128,2560]{1,0:T(8,128)(2,1)}, bf16[128,2560]{1,0:T(8,128)(2,1)S(1)}, u32[]{:S(2)}, u32[]{:S(2)}) %collective-permute-start.46) | collective-permute-done | bytes 655392 | tf_op jit(solution)/shard_map/ppermute | solution.py:47
  245.8 3.4 multiply_convert_fusion.5
  250.7 2.6 fusion
  253.3 6.1 %collective-permute-done.48 = bf16[128,2560]{1,0:T(8,128)(2,1)S(1)} collective-permute-done((bf16[128,2560]{1,0:T(8,128)(2,1)S(1)}, bf16[128,2560]{1,0:T(8,128)(2,1)S(1)}, u32[]{:S(2)}, u32[]{:S(2)}) %collective-permute-start.48) | collective-permute-done | bytes 655392 | tf_op jit(solution)/shard_map/ppermute | solution.py:47
  270.1 3.0 collective-permute-done.52
  295.0 7.8 %collective-permute-done.56 = bf16[64,2560]{1,0:T(8,128)(2,1)S(1)} collective-permute-done((bf16[64,2560]{1,0:T(8,128)(2,1)S(1)}, bf16[64,2560]{1,0:T(8,128)(2,1)S(1)}, u32[]{:S(2)}, u32[]{:S(2)}) %collective-permute-start.56) | collective-permute-done | bytes 327712 | tf_op jit(solution)/shard_map/ppermute | solution.py:50
  307.2 9.7 %shard_map.258 = (bf16[128,2560]{1,0:T(8,128)(2,1)S(1)}, bf16[256,2560]{1,0:T(8,128)(2,1)S(1)}, bf16[256,2560]{1,0:T(8,128)(2,1)S(1)}, bf16[256,2560]{1,0:T(8,128)(2,1)}, bf16[128,2560]{1,0:T(8,128)(2,1)S(1)}) custom-call(bf16[128,960]{1,0:T(8,128)(2,1)S(1)} %get-tuple-element.613.refs_0_, bf16[256,960]{1,0:T(8,128)(2,1)S(1)} %get-tuple-element.614.refs_1_, ...), custom_call_target="tpu_custom_call" | custom-call | tf_op jit(solution)/shard_map/pallas_call | solution.py:949
  325.3 9.7 %shard_map.259.refs_10_ = bf16[4,3,240,2560]{3,2,1,0:T(8,128)(2,1)} custom-call(bf16[128,960]{1,0:T(8,128)(2,1)S(1)} %copy-done.48, bf16[256,960]{1,0:T(8,128)(2,1)S(1)} %copy-done.42, bf16[256,960]{1,0:T(8,128)(2,1)S(1)} %copy-done.44, bf16[256,960]{1,0:T(8,128)(2,1)S(1)} %copy-done.46, bf16[128,960]{1,0:T(8,128)(2,1)S(1)} %get-tuple-element.583.refs_4_, ...), custom_call_target="tpu_custom_call" | custom-call | tf_op jit(solution)/shard_map/pallas_call | solution.py:813
  335.1 3.8 collective-permute-done.60
  343.7 9.7 %shard_map.260.refs_10_ = bf16[4,3,240,2560]{3,2,1,0:T(8,128)(2,1)} custom-call(bf16[128,960]{1,0:T(8,128)(2,1)S(1)} %get-tuple-element.595.refs_0_, bf16[256,960]{1,0:T(8,128)(2,1)S(1)} %copy-done.36, bf16[256,960]{1,0:T(8,128)(2,1)S(1)} %copy-done.38, bf16[256,960]{1,0:T(8,128)(2,1)S(1)} %copy-done.40, ...), custom_call_target="tpu_custom_call", output_to_operand_aliasing={{}: (10, {})} | custom-call | tf_op jit(solution)/shard_map/pallas_call | solution.py:813
  359.6 3.2 collective-permute-start.64
  363.4 9.8 %shard_map.261 = bf16[4,3,240,2560]{3,2,1,0:T(8,128)(2,1)} custom-call(bf16[128,960]{1,0:T(8,128)(2,1)S(1)} %get-tuple-element.613.refs_0_, bf16[256,960]{1,0:T(8,128)(2,1)S(1)} %get-tuple-element.614.refs_1_, bf16[256,960]{1,0:T(8,128)(2,1)S(1)} %get-tuple-element.615.refs_2_, ...), custom_call_target="tpu_custom_call", output_to_operand_aliasing={{}: (10, {})} | custom-call | tf_op jit(solution)/shard_map/pallas_call | solution.py:813
  377.4 8.1 %shard_map.262 = (bf16[256,1280]{1,0:T(8,128)(2,1)S(1)}, f32[256,1280]{1,0:T(8,128)S(1)}, f32[256,1280]{1,0:T(8,128)S(1)}, f32[2,1280]{1,0:T(2,128)S(1)}) custom-call(bf16[256,2560]{1,0:T(8,128)(2,1)S(1)} %pad_maximum_fusion.1.dz_ref.refs_3_, bf16[1280,2560]{1,0:T(8,128)(2,1)} %get-tuple-element.633.wide_ref, f32[256,1280]{1,0:T(8,128)S(1)} %copy-done.8, ...), custom_call_target="tpu_custom_call" | custom-call | tf_op jit(solution)/shard_map/pallas_call | solution.py:515
  390.6 2.9 collective-permute-start.69
  396.2 10.8 %shard_map.263 = (bf16[8,160,2560]{2,1,0:T(8,128)(2,1)}, bf16[8,160,2560]{2,1,0:T(8,128)(2,1)}) custom-call(s32[9]{0:T(128)S(1)} %stack.193.at_ref, bf16[256,1280]{1,0:T(8,128)(2,1)S(1)} %copy-done.12, bf16[256,1280]{1,0:T(8,128)(2,1)S(1)} %fusion.26.refs_1_, bf16[256,2560]{1,0:T(8,128)(2,1)S(1)} %slice.554.refs_2_.refs_1_, ...), custom_call_target="tpu_custom_call" | custom-call | tf_op jit(solution)/shard_map/pallas_call | solution.py:731
  416.3 2.6 collective-permute-start.71
  421.6 8.3 %shard_map.264 = (bf16[256,1280]{1,0:T(8,128)(2,1)S(1)}, f32[8,1280]{1,0:T(8,128)S(1)}, f32[8,1280]{1,0:T(8,128)S(1)}, f32[8,1280]{1,0:T(8,128)S(1)}, bf16[256,2560]{1,0:T(8,128)(2,1)S(1)}) custom-call(f32[256,1280]{1,0:T(8,128)S(1)} %copy-done.54, f32[256,1280]{1,0:T(8,128)} %copy-done.55, f32[1,1280]{1,0:T(1,128)S(1)} %slice_add_fusion.refs_2_, ...), custom_call_target="tpu_custom_call" | custom-call | flops 499999997952 | tf_op jit(solution)/shard_map/pallas_call | solution.py:552
  437.1 3.0 add_convert_fusion.1
  442.2 4.2 fusion.94
  458.4 7.1 %shard_map.265 = (bf16[8,96,2560]{2,1,0:T(8,128)(2,1)}, bf16[8,96,2560]{2,1,0:T(8,128)(2,1)}) custom-call(s32[9]{0:T(128)S(1)} %copy-done.52, bf16[256,1280]{1,0:T(8,128)(2,1)S(1)} %fusion.107.refs_0_, bf16[256,2560]{1,0:T(8,128)(2,1)S(1)} %slice.554.refs_2_.refs_1_, bf16[256,2560]{1,0:T(8,128)(2,1)S(1)} %get-tuple-element.704.refs_2_), custom_call_target="tpu_custom_call" | custom-call | tf_op jit(solution)/shard_map/pallas_call | solution.py:731
  465.7 3.9 fusion.91
  473.8 2.6 collective-permute-start.81
  476.4 2.9 fusion.11
  479.3 2.8 fusion.10
  487.7 2.9 shard_map.266
  494.1 12.7 %collective-permute-done.85 = bf16[160,2560]{1,0:T(8,128)(2,1)} collective-permute-done((bf16[160,2560]{1,0:T(8,128)(2,1)}, bf16[160,2560]{1,0:T(8,128)(2,1)}, u32[]{:S(2)}, u32[]{:S(2)}) %collective-permute-start.85) | collective-permute-done | bytes 819232 | tf_op jit(solution)/shard_map/ppermute | solution.py:50
  508.7 2.6 collective-permute-done.88
  528.0 21.0 %collective-permute-done.92 = bf16[97,2560]{1,0:T(8,128)(2,1)} collective-permute-done((bf16[97,2560]{1,0:T(8,128)(2,1)}, bf16[97,2560]{1,0:T(8,128)(2,1)}, u32[]{:S(2)}, u32[]{:S(2)}) %collective-permute-start.92) | collective-permute-done | bytes 496672 | tf_op jit(solution)/shard_map/ppermute | solution.py:50
  558.9 8.2 %collective-permute-done.94 = bf16[97,2560]{1,0:T(8,128)(2,1)S(1)} collective-permute-done((bf16[97,2560]{1,0:T(8,128)(2,1)S(1)}, bf16[97,2560]{1,0:T(8,128)(2,1)S(1)}, u32[]{:S(2)}, u32[]{:S(2)}) %collective-permute-start.94) | collective-permute-done | bytes 496672 | tf_op jit(solution)/shard_map/ppermute | solution.py:50
  575.6 3.6 shard_map.267
  (603 shorter events, 259.3 us)
Async XLA Ops:
  7.2 144.1 %all-gather.4.cloned.1.call-start = ((), (), s32[]{:S(2)}) async-start(), calls=%async_computation.1 | async-start | bytes 6144000 | tf_op jit(solution)/shard_map/all_gather | solution.py:217
  7.9 198.8 %all-gather.6.cloned.1.call-start = ((), (), s32[]{:S(2)}) async-start(), calls=%async_computation.2 | async-start | bytes 6144000 | tf_op jit(solution)/shard_map/all_gather | solution.py:217
  8.7 198.1 %all-gather.8.cloned.1.call-start = ((), (), s32[]{:S(2)}) async-start(), calls=%async_computation.3 | async-start | bytes 6144000 | tf_op jit(solution)/shard_map/all_gather | solution.py:217
  9.3 18.3 %collective-permute-start.1 = (bf16[112,2560]{1,0:T(8,128)(2,1)S(1)}, bf16[112,2560]{1,0:T(8,128)(2,1)S(1)}, u32[]{:S(2)}, u32[]{:S(2)}) collective-permute-start(bf16[112,2560]{1,0:T(8,128)(2,1)S(1)} %pad_maximum_fusion.9.refs_0_), channel_id=1, source_target_pairs={{0,2},{2,0},{4,6},{6,4},{8,10},{10,8},{12,14},{14,12},{16,18},{18,... | collective-permute-start | bytes 1720328 | tf_op jit(solution)/shard_map/ppermute | solution.py:206
  9.9 16.2 %collective-permute-start.2 = (bf16[112,2560]{1,0:T(8,128)(2,1)S(1)}, bf16[112,2560]{1,0:T(8,128)(2,1)S(1)}, u32[]{:S(2)}, u32[]{:S(2)}) collective-permute-start(bf16[112,2560]{1,0:T(8,128)(2,1)S(1)} %pad_maximum_fusion.9.refs_0_), channel_id=1, source_target_pairs={{0,8},{2,10},{8,16},{10,18},{16,24},{18,26},{24,28},{26,30},{28,20... | collective-permute-start | bytes 1720328 | tf_op jit(solution)/shard_map/ppermute | solution.py:47
  12.5 24.6 %collective-permute-start = (bf16[128,2560]{1,0:T(8,128)(2,1)S(1)}, bf16[128,2560]{1,0:T(8,128)(2,1)}, u32[]{:S(2)}, u32[]{:S(2)}) collective-permute-start(bf16[128,2560]{1,0:T(8,128)(2,1)S(1)} %copy-done), channel_id=1, source_target_pairs={{0,1},{1,0},{2,3},{3,2},{4,5},{5,4},{6,7},{7,6},{8,9},{9,8},{10,11... | collective-permute-start | bytes 1966088 | tf_op jit(solution)/shard_map/ppermute | solution.py:233
  43.5 17.1 %collective-permute-start.9 = (bf16[112,2560]{1,0:T(8,128)(2,1)}, bf16[112,2560]{1,0:T(8,128)(2,1)S(1)}, u32[]{:S(2)}, u32[]{:S(2)}) collective-permute-start(bf16[112,2560]{1,0:T(8,128)(2,1)} %collective-permute-done.7.refs_6_), channel_id=1, source_target_pairs={{0,2},{2,0},{4,6},{6,4},{8,10},{10,8},{12,14},{14,12},{16,18},{18,... | collective-permute-start | bytes 1720328 | tf_op jit(solution)/shard_map/ppermute | solution.py:206
  43.5 17.9 %collective-permute-start.10 = (bf16[112,2560]{1,0:T(8,128)(2,1)}, bf16[112,2560]{1,0:T(8,128)(2,1)S(1)}, u32[]{:S(2)}, u32[]{:S(2)}) collective-permute-start(bf16[112,2560]{1,0:T(8,128)(2,1)} %collective-permute-done.8.refs_8_), channel_id=1, source_target_pairs={{0,2},{2,0},{4,6},{6,4},{8,10},{10,8},{12,14},{14,12},{16,18},{18,... | collective-permute-start | bytes 1720328 | tf_op jit(solution)/shard_map/ppermute | solution.py:206
  70.9 22.2 %collective-permute-start.19 = (bf16[160,2560]{1,0:T(8,128)(2,1)S(1)}, bf16[160,2560]{1,0:T(8,128)(2,1)S(1)}, u32[]{:S(2)}, u32[]{:S(2)}) collective-permute-start(bf16[160,2560]{1,0:T(8,128)(2,1)S(1)} %constant_dynamic-update-slice_fusion.refs_0_), channel_id=1, source_target_pairs={{0,2},{2,0},{4,6},{6,4},{8,10},{10,8},{12,14},{14,12},{16,18},{18,... | collective-permute-start | bytes 2457608 | tf_op jit(solution)/shard_map/ppermute | solution.py:206
  79.0 20.3 %collective-permute-start.20 = (bf16[160,2560]{1,0:T(8,128)(2,1)S(1)}, bf16[160,2560]{1,0:T(8,128)(2,1)}, u32[]{:S(2)}, u32[]{:S(2)}) collective-permute-start(bf16[160,2560]{1,0:T(8,128)(2,1)S(1)} %constant_dynamic-update-slice_fusion.refs_0_), channel_id=1, source_target_pairs={{0,8},{2,10},{8,16},{10,18},{16,24},{18,26},{24,28},{26,30},{28,20... | collective-permute-start | bytes 2457608 | tf_op jit(solution)/shard_map/ppermute | solution.py:47
  79.6 20.0 %collective-permute-start.21 = (bf16[160,2560]{1,0:T(8,128)(2,1)S(1)}, bf16[160,2560]{1,0:T(8,128)(2,1)}, u32[]{:S(2)}, u32[]{:S(2)}) collective-permute-start(bf16[160,2560]{1,0:T(8,128)(2,1)S(1)} %constant_dynamic-update-slice_fusion.refs_0_), channel_id=1, source_target_pairs={{8,0},{10,2},{16,8},{18,10},{24,16},{26,18},{28,24},{30,26},{20,28... | collective-permute-start | bytes 2457608 | tf_op jit(solution)/shard_map/ppermute | solution.py:50
  99.7 21.8 %collective-permute-start.22 = (bf16[160,2560]{1,0:T(8,128)(2,1)}, bf16[160,2560]{1,0:T(8,128)(2,1)}, u32[]{:S(2)}, u32[]{:S(2)}) collective-permute-start(bf16[160,2560]{1,0:T(8,128)(2,1)} %collective-permute-done.20.refs_2_), channel_id=1, source_target_pairs={{0,2},{2,0},{4,6},{6,4},{8,10},{10,8},{12,14},{14,12},{16,18},{18,... | collective-permute-start | bytes 2457608 | tf_op jit(solution)/shard_map/ppermute | solution.py:206
  99.7 21.8 %collective-permute-start.23 = (bf16[160,2560]{1,0:T(8,128)(2,1)}, bf16[160,2560]{1,0:T(8,128)(2,1)}, u32[]{:S(2)}, u32[]{:S(2)}) collective-permute-start(bf16[160,2560]{1,0:T(8,128)(2,1)} %collective-permute-done.21.refs_4_), channel_id=1, source_target_pairs={{0,2},{2,0},{4,6},{6,4},{8,10},{10,8},{12,14},{14,12},{16,18},{18,... | collective-permute-start | bytes 2457608 | tf_op jit(solution)/shard_map/ppermute | solution.py:206
  100.8 20.5 %collective-permute-start.24 = (bf16[160,2560]{1,0:T(8,128)(2,1)}, bf16[160,2560]{1,0:T(8,128)(2,1)}, u32[]{:S(2)}, u32[]{:S(2)}) collective-permute-start(bf16[160,2560]{1,0:T(8,128)(2,1)} %collective-permute-done.20.refs_2_), channel_id=1, source_target_pairs={{0,8},{2,10},{8,16},{10,18},{16,24},{18,26},{24,28},{26,30},{28,20... | collective-permute-start | bytes 2457608 | tf_op jit(solution)/shard_map/ppermute | solution.py:47
  101.3 20.2 %collective-permute-start.25 = (bf16[160,2560]{1,0:T(8,128)(2,1)}, bf16[160,2560]{1,0:T(8,128)(2,1)}, u32[]{:S(2)}, u32[]{:S(2)}) collective-permute-start(bf16[160,2560]{1,0:T(8,128)(2,1)} %collective-permute-done.21.refs_4_), channel_id=1, source_target_pairs={{8,0},{10,2},{16,8},{18,10},{24,16},{26,18},{28,24},{30,26},{20,28... | collective-permute-start | bytes 2457608 | tf_op jit(solution)/shard_map/ppermute | solution.py:50
  122.1 451.5 %reduce-scatter.2.cloned.1.call-start = ((), (), s32[]{:S(2)}) async-start(), calls=%async_computation.4 | async-start | bytes 18432000 | tf_op jit(solution)/shard_map/reduce_scatter | solution.py:223
  124.1 20.9 %collective-permute-start.28 = (bf16[160,2560]{1,0:T(8,128)(2,1)}, bf16[160,2560]{1,0:T(8,128)(2,1)S(1)}, u32[]{:S(2)}, u32[]{:S(2)}) collective-permute-start(bf16[160,2560]{1,0:T(8,128)(2,1)} %collective-permute-done.24.refs_6_), channel_id=1, source_target_pairs={{0,8},{2,10},{8,16},{10,18},{16,24},{18,26},{24,28},{26,30},{28,20... | collective-permute-start | bytes 2457608 | tf_op jit(solution)/shard_map/ppermute | solution.py:47
  125.5 21.1 %collective-permute-start.29 = (bf16[160,2560]{1,0:T(8,128)(2,1)}, bf16[160,2560]{1,0:T(8,128)(2,1)}, u32[]{:S(2)}, u32[]{:S(2)}) collective-permute-start(bf16[160,2560]{1,0:T(8,128)(2,1)} %collective-permute-done.25.refs_8_), channel_id=1, source_target_pairs={{8,0},{10,2},{16,8},{18,10},{24,16},{26,18},{28,24},{30,26},{20,28... | collective-permute-start | bytes 2457608 | tf_op jit(solution)/shard_map/ppermute | solution.py:50
  126.3 18.7 %collective-permute-start.32 = (f32[2,1280]{1,0:T(2,128)S(1)}, f32[2,1280]{1,0:T(2,128)S(1)}, u32[]{:S(2)}, u32[]{:S(2)}) collective-permute-start(f32[2,1280]{1,0:T(2,128)S(1)} %pad_maximum_fusion.14), channel_id=1, source_target_pairs={{0,6},{2,8},{4,10},{6,12},{8,14},{10,16},{12,18},{14,20},{16,22},{... | collective-permute-start | bytes 30728 | tf_op jit(solution)/shard_map/ppermute | solution.py:239
  161.5 16.6 %collective-permute-start.39 = (bf16[128,2560]{1,0:T(8,128)(2,1)S(1)}, bf16[128,2560]{1,0:T(8,128)(2,1)}, u32[]{:S(2)}, u32[]{:S(2)}) collective-permute-start(bf16[128,2560]{1,0:T(8,128)(2,1)S(1)} %copy-done.2), channel_id=1, source_target_pairs={{0,8},{2,10},{8,16},{10,18},{16,24},{18,26},{24,28},{26,30},{28,20... | collective-permute-start | bytes 1966088 | tf_op jit(solution)/shard_map/ppermute | solution.py:47
  163.2 15.9 %collective-permute-start.40 = (bf16[128,2560]{1,0:T(8,128)(2,1)S(1)}, bf16[128,2560]{1,0:T(8,128)(2,1)}, u32[]{:S(2)}, u32[]{:S(2)}) collective-permute-start(bf16[128,2560]{1,0:T(8,128)(2,1)S(1)} %copy-done.2), channel_id=1, source_target_pairs={{8,0},{10,2},{16,8},{18,10},{24,16},{26,18},{28,24},{30,26},{20,28... | collective-permute-start | bytes 1966088 | tf_op jit(solution)/shard_map/ppermute | solution.py:50
  186.1 18.6 %collective-permute-start.41 = (bf16[128,2560]{1,0:T(8,128)(2,1)S(1)}, bf16[128,2560]{1,0:T(8,128)(2,1)S(1)}, u32[]{:S(2)}, u32[]{:S(2)}) collective-permute-start(bf16[128,2560]{1,0:T(8,128)(2,1)S(1)} %convolution_convert_fusion), channel_id=1, source_target_pairs={{0,1},{1,0},{2,3},{3,2},{4,5},{5,4},{6,7},{7,6},{8,9},{9,8},{10,11... | collective-permute-start | bytes 1966088 | tf_op jit(solution)/shard_map/ppermute | solution.py:233
  206.8 30.5 %collective-permute-start.44 = (bf16[128,2560]{1,0:T(8,128)(2,1)S(1)}, bf16[128,2560]{1,0:T(8,128)(2,1)S(1)}, u32[]{:S(2)}, u32[]{:S(2)}) collective-permute-start(bf16[128,2560]{1,0:T(8,128)(2,1)S(1)} %multiply_convert_fusion.refs_0_.refs_5_), channel_id=1, source_target_pairs={{0,8},{2,10},{8,16},{10,18},{16,24},{18,26},{24,28},{26,30},{28,20... | collective-permute-start | bytes 1966088 | tf_op jit(solution)/shard_map/ppermute | solution.py:47
  208.4 29.0 %collective-permute-start.45 = (bf16[128,2560]{1,0:T(8,128)(2,1)S(1)}, bf16[128,2560]{1,0:T(8,128)(2,1)S(1)}, u32[]{:S(2)}, u32[]{:S(2)}) collective-permute-start(bf16[128,2560]{1,0:T(8,128)(2,1)S(1)} %multiply_convert_fusion.refs_0_.refs_5_), channel_id=1, source_target_pairs={{8,0},{10,2},{16,8},{18,10},{24,16},{26,18},{28,24},{30,26},{20,28... | collective-permute-start | bytes 1966088 | tf_op jit(solution)/shard_map/ppermute | solution.py:50
  208.9 26.7 %collective-permute-start.46 = (bf16[128,2560]{1,0:T(8,128)(2,1)}, bf16[128,2560]{1,0:T(8,128)(2,1)S(1)}, u32[]{:S(2)}, u32[]{:S(2)}) collective-permute-start(bf16[128,2560]{1,0:T(8,128)(2,1)} %copy-done.71), channel_id=1, source_target_pairs={{0,8},{2,10},{8,16},{10,18},{16,24},{18,26},{24,28},{26,30},{28,20... | collective-permute-start | bytes 1966088 | tf_op jit(solution)/shard_map/ppermute | solution.py:47
  210.5 26.9 %collective-permute-start.47 = (bf16[128,2560]{1,0:T(8,128)(2,1)}, bf16[128,2560]{1,0:T(8,128)(2,1)S(1)}, u32[]{:S(2)}, u32[]{:S(2)}) collective-permute-start(bf16[128,2560]{1,0:T(8,128)(2,1)} %copy-done.73), channel_id=1, source_target_pairs={{8,0},{10,2},{16,8},{18,10},{24,16},{26,18},{28,24},{30,26},{20,28... | collective-permute-start | bytes 1966088 | tf_op jit(solution)/shard_map/ppermute | solution.py:50
  237.5 22.0 %collective-permute-start.51 = (bf16[64,2560]{1,0:T(8,128)(2,1)S(1)}, bf16[64,2560]{1,0:T(8,128)(2,1)S(1)}, u32[]{:S(2)}, u32[]{:S(2)}) collective-permute-start(bf16[64,2560]{1,0:T(8,128)(2,1)S(1)} %slice.453), channel_id=1, source_target_pairs={{8,0},{10,2},{16,8},{18,10},{24,16},{26,18},{28,24},{30,26},{20,28... | collective-permute-start | bytes 983048 | tf_op jit(solution)/shard_map/ppermute | solution.py:50
  237.8 21.7 %collective-permute-start.50 = (bf16[64,2560]{1,0:T(8,128)(2,1)S(1)}, bf16[64,2560]{1,0:T(8,128)(2,1)S(1)}, u32[]{:S(2)}, u32[]{:S(2)}) collective-permute-start(bf16[64,2560]{1,0:T(8,128)(2,1)S(1)} %slice.452), channel_id=1, source_target_pairs={{0,8},{2,10},{8,16},{10,18},{16,24},{18,26},{24,28},{26,30},{28,20... | collective-permute-start | bytes 983048 | tf_op jit(solution)/shard_map/ppermute | solution.py:47
  239.6 19.9 %collective-permute-start.48 = (bf16[128,2560]{1,0:T(8,128)(2,1)S(1)}, bf16[128,2560]{1,0:T(8,128)(2,1)S(1)}, u32[]{:S(2)}, u32[]{:S(2)}) collective-permute-start(bf16[128,2560]{1,0:T(8,128)(2,1)S(1)} %collective-permute-done.44), channel_id=1, source_target_pairs={{0,8},{2,10},{8,16},{10,18},{16,24},{18,26},{24,28},{26,30},{28,20... | collective-permute-start | bytes 1966088 | tf_op jit(solution)/shard_map/ppermute | solution.py:47
  240.4 19.1 %collective-permute-start.49 = (bf16[128,2560]{1,0:T(8,128)(2,1)S(1)}, bf16[128,2560]{1,0:T(8,128)(2,1)S(1)}, u32[]{:S(2)}, u32[]{:S(2)}) collective-permute-start(bf16[128,2560]{1,0:T(8,128)(2,1)S(1)} %collective-permute-done.45), channel_id=1, source_target_pairs={{8,0},{10,2},{16,8},{18,10},{24,16},{26,18},{28,24},{30,26},{20,28... | collective-permute-start | bytes 1966088 | tf_op jit(solution)/shard_map/ppermute | solution.py:50
  323.2 15.9 %collective-permute-start.61 = (bf16[128,2560]{1,0:T(8,128)(2,1)}, bf16[128,2560]{1,0:T(8,128)(2,1)S(1)}, u32[]{:S(2)}, u32[]{:S(2)}) collective-permute-start(bf16[128,2560]{1,0:T(8,128)(2,1)} %add_convert_fusion.8), channel_id=1, source_target_pairs={{0,8},{2,10},{8,16},{10,18},{16,24},{18,26},{24,28},{26,30},{28,20... | collective-permute-start | bytes 1966088 | tf_op jit(solution)/shard_map/ppermute | solution.py:47
  390.6 16.4 %collective-permute-start.69 = (bf16[128,2560]{1,0:T(8,128)(2,1)}, bf16[128,2560]{1,0:T(8,128)(2,1)}, u32[]{:S(2)}, u32[]{:S(2)}) collective-permute-start(bf16[128,2560]{1,0:T(8,128)(2,1)} %add_convert_fusion.5), channel_id=1, source_target_pairs={{8,0},{10,2},{16,8},{18,10},{24,16},{26,18},{28,24},{30,26},{20,28... | collective-permute-start | bytes 1966088 | tf_op jit(solution)/shard_map/ppermute | solution.py:50
  393.6 17.6 %collective-permute-start.74 = (f32[2,1280]{1,0:T(2,128)S(1)}, f32[2,1280]{1,0:T(2,128)S(1)}, u32[]{:S(2)}, u32[]{:S(2)}) collective-permute-start(f32[2,1280]{1,0:T(2,128)S(1)} %get-tuple-element.662), channel_id=1, source_target_pairs={{2,0},{4,2},{6,4},{8,6},{10,8},{12,10},{14,12},{16,14},{18,16},{20... | collective-permute-start | bytes 30728 | tf_op jit(solution)/shard_map/ppermute | solution.py:239
  414.4 16.8 %collective-permute-start.73 = (bf16[8,160,2560]{2,1,0:T(8,128)(2,1)}, bf16[8,160,2560]{2,1,0:T(8,128)(2,1)}, u32[]{:S(2)}, u32[]{:S(2)}) collective-permute-start(bf16[8,160,2560]{2,1,0:T(8,128)(2,1)} %get-tuple-element.654), channel_id=1, source_target_pairs={{0,2},{2,0},{4,6},{6,4},{8,10},{10,8},{12,14},{14,12},{16,18},{18,... | collective-permute-start | bytes 19660808 | tf_op jit(solution)/shard_map/ppermute | solution.py:206
  416.3 19.4 %collective-permute-start.71 = (bf16[128,2560]{1,0:T(8,128)(2,1)}, bf16[128,2560]{1,0:T(8,128)(2,1)}, u32[]{:S(2)}, u32[]{:S(2)}) collective-permute-start(bf16[128,2560]{1,0:T(8,128)(2,1)} %add_convert_fusion.3), channel_id=1, source_target_pairs={{8,0},{10,2},{16,8},{18,10},{24,16},{26,18},{28,24},{30,26},{20,28... | collective-permute-start | bytes 1966088 | tf_op jit(solution)/shard_map/ppermute | solution.py:50
  418.9 18.1 %collective-permute-start.72 = (bf16[128,2560]{1,0:T(8,128)(2,1)}, bf16[128,2560]{1,0:T(8,128)(2,1)}, u32[]{:S(2)}, u32[]{:S(2)}) collective-permute-start(bf16[128,2560]{1,0:T(8,128)(2,1)} %add_convert_fusion.2), channel_id=1, source_target_pairs={{0,8},{2,10},{8,16},{10,18},{16,24},{18,26},{24,28},{26,30},{28,20... | collective-permute-start | bytes 1966088 | tf_op jit(solution)/shard_map/ppermute | solution.py:47
  448.3 39.4 %collective-permute-start.80 = (bf16[128,2560]{1,0:T(8,128)(2,1)}, bf16[128,2560]{1,0:T(8,128)(2,1)}, u32[]{:S(2)}, u32[]{:S(2)}) collective-permute-start(bf16[128,2560]{1,0:T(8,128)(2,1)} %get-tuple-element.897), channel_id=1, source_target_pairs={{0,1},{1,0},{2,3},{3,2},{4,5},{5,4},{6,7},{7,6},{8,9},{9,8},{10,11... | collective-permute-start | bytes 1966088 | tf_op jit(solution)/shard_map/ppermute | solution.py:233
  456.4 20.0 %collective-permute-start.82 = (bf16[160,2560]{1,0:T(8,128)(2,1)S(1)}, bf16[160,2560]{1,0:T(8,128)(2,1)}, u32[]{:S(2)}, u32[]{:S(2)}) collective-permute-start(bf16[160,2560]{1,0:T(8,128)(2,1)S(1)} %pad_maximum_fusion.2), channel_id=1, source_target_pairs={{8,0},{10,2},{16,8},{18,10},{24,16},{26,18},{28,24},{30,26},{20,28... | collective-permute-start | bytes 2457608 | tf_op jit(solution)/shard_map/ppermute | solution.py:50
  458.1 18.3 %collective-permute-start.83 = (bf16[160,2560]{1,0:T(8,128)(2,1)S(1)}, bf16[160,2560]{1,0:T(8,128)(2,1)}, u32[]{:S(2)}, u32[]{:S(2)}) collective-permute-start(bf16[160,2560]{1,0:T(8,128)(2,1)S(1)} %pad_maximum_fusion.3), channel_id=1, source_target_pairs={{0,8},{2,10},{8,16},{10,18},{16,24},{18,26},{24,28},{26,30},{28,20... | collective-permute-start | bytes 2457608 | tf_op jit(solution)/shard_map/ppermute | solution.py:47
  465.6 25.1 %collective-permute-start.87 = (bf16[8,96,2560]{2,1,0:T(8,128)(2,1)}, bf16[8,96,2560]{2,1,0:T(8,128)(2,1)}, u32[]{:S(2)}, u32[]{:S(2)}) collective-permute-start(bf16[8,96,2560]{2,1,0:T(8,128)(2,1)} %get-tuple-element.706), channel_id=1, source_target_pairs={{0,2},{2,0},{4,6},{6,4},{8,10},{10,8},{12,14},{14,12},{16,18},{18,... | collective-permute-start | bytes 11796488 | tf_op jit(solution)/shard_map/ppermute | solution.py:206
  485.4 21.4 %collective-permute-start.85 = (bf16[160,2560]{1,0:T(8,128)(2,1)}, bf16[160,2560]{1,0:T(8,128)(2,1)}, u32[]{:S(2)}, u32[]{:S(2)}) collective-permute-start(bf16[160,2560]{1,0:T(8,128)(2,1)} %fusion.11), channel_id=1, source_target_pairs={{8,0},{10,2},{16,8},{18,10},{24,16},{26,18},{28,24},{30,26},{20,28... | collective-permute-start | bytes 2457608 | tf_op jit(solution)/shard_map/ppermute | solution.py:50
  487.1 21.7 %collective-permute-start.86 = (bf16[160,2560]{1,0:T(8,128)(2,1)}, bf16[160,2560]{1,0:T(8,128)(2,1)}, u32[]{:S(2)}, u32[]{:S(2)}) collective-permute-start(bf16[160,2560]{1,0:T(8,128)(2,1)} %fusion.10), channel_id=1, source_target_pairs={{0,8},{2,10},{8,16},{10,18},{16,24},{18,26},{24,28},{26,30},{28,20... | collective-permute-start | bytes 2457608 | tf_op jit(solution)/shard_map/ppermute | solution.py:47
  492.0 21.8 %collective-permute-start.89 = (bf16[49,2560]{1,0:T(8,128)(2,1)S(1)}, bf16[49,2560]{1,0:T(8,128)(2,1)S(1)}, u32[]{:S(2)}, u32[]{:S(2)}) collective-permute-start(bf16[49,2560]{1,0:T(8,128)(2,1)S(1)} %pad_maximum_fusion.11), channel_id=1, source_target_pairs={{0,8},{2,10},{8,16},{10,18},{16,24},{18,26},{24,28},{26,30},{28,20... | collective-permute-start | bytes 752648 | tf_op jit(solution)/shard_map/ppermute | solution.py:47
  492.9 18.5 %collective-permute-start.88 = (bf16[48,2560]{1,0:T(8,128)(2,1)S(1)}, bf16[48,2560]{1,0:T(8,128)(2,1)S(1)}, u32[]{:S(2)}, u32[]{:S(2)}) collective-permute-start(bf16[48,2560]{1,0:T(8,128)(2,1)S(1)} %slice_bitcast_fusion.7), channel_id=1, source_target_pairs={{8,0},{10,2},{16,8},{18,10},{24,16},{26,18},{28,24},{30,26},{20,28... | collective-permute-start | bytes 737288 | tf_op jit(solution)/shard_map/ppermute | solution.py:50
  518.0 32.1 %collective-permute-start.90 = (bf16[160,2560]{1,0:T(8,128)(2,1)S(1)}, bf16[160,2560]{1,0:T(8,128)(2,1)S(1)}, u32[]{:S(2)}, u32[]{:S(2)}) collective-permute-start(bf16[160,2560]{1,0:T(8,128)(2,1)S(1)} %fusion.9), channel_id=1, source_target_pairs={{8,0},{10,2},{16,8},{18,10},{24,16},{26,18},{28,24},{30,26},{20,28... | collective-permute-start | bytes 2457608 | tf_op jit(solution)/shard_map/ppermute | solution.py:50
  519.5 30.6 %collective-permute-start.91 = (bf16[160,2560]{1,0:T(8,128)(2,1)S(1)}, bf16[160,2560]{1,0:T(8,128)(2,1)S(1)}, u32[]{:S(2)}, u32[]{:S(2)}) collective-permute-start(bf16[160,2560]{1,0:T(8,128)(2,1)S(1)} %fusion.8), channel_id=1, source_target_pairs={{0,8},{2,10},{8,16},{10,18},{16,24},{18,26},{24,28},{26,30},{28,20... | collective-permute-start | bytes 2457608 | tf_op jit(solution)/shard_map/ppermute | solution.py:47
  525.9 23.0 %collective-permute-start.92 = (bf16[97,2560]{1,0:T(8,128)(2,1)}, bf16[97,2560]{1,0:T(8,128)(2,1)}, u32[]{:S(2)}, u32[]{:S(2)}) collective-permute-start(bf16[97,2560]{1,0:T(8,128)(2,1)} %fusion.74), channel_id=1, source_target_pairs={{8,0},{10,2},{16,8},{18,10},{24,16},{26,18},{28,24},{30,26},{20,28... | collective-permute-start | bytes 1489928 | tf_op jit(solution)/shard_map/ppermute | solution.py:50
  527.4 22.7 %collective-permute-start.93 = (bf16[97,2560]{1,0:T(8,128)(2,1)}, bf16[97,2560]{1,0:T(8,128)(2,1)}, u32[]{:S(2)}, u32[]{:S(2)}) collective-permute-start(bf16[97,2560]{1,0:T(8,128)(2,1)} %pad_maximum_fusion.10), channel_id=1, source_target_pairs={{0,8},{2,10},{8,16},{10,18},{16,24},{18,26},{24,28},{26,30},{28,20... | collective-permute-start | bytes 1489928 | tf_op jit(solution)/shard_map/ppermute | solution.py:47
  (159 other events, 1215.6 us)
Sparse Core Ops, SparseCore 0:
  9.6 47.6 all-gather.3
  58.8 39.9 all-gather.5
  122.2 38.4 all-gather.7
  414.6 131.7 reduce-scatter.1

commit v4 on v3

--- a/solution.py
+++ b/solution.py
@@ -152,21 +152,26 @@
         ahead, behind = self.parts.pop(), self.parts.pop()
         half, first = self.half, self.steps == 1
 
-        def add(to_down, to_up, *values):
-            u_values, d_values = values[: len(behind.values)], values[len(behind.values) :]
+        self.steps += 1
+        to_down, to_up = self.flight
+
+        def add_up(got, *values):
             if first:
-                return (
-                    jnp.concatenate(
-                        [behind(u_values, 0, half, to_down), behind(u_values, half, None)]
-                    ),
-                    jnp.concatenate(
-                        [ahead(d_values, 0, half), ahead(d_values, half, None, to_up)]
-                    ),
+                return jnp.concatenate(
+                    [ahead(values, 0, half), ahead(values, half, None, got)]
                 )
-            return behind(u_values, 0, None, to_down), ahead(d_values, 0, None, to_up)
-
-        self.flight = self.order.run(add, *self.flight, *behind.values, *ahead.values)
-        self.send()
+            return ahead(values, 0, None, got)
+
+        def add_down(got, *values):
+            if first:
+                return jnp.concatenate(
+                    [behind(values, 0, half, got), behind(values, half, None)]
+                )
+            return behind(values, 0, None, got)
+
+        up = self.ring.up(self.order.run(add_up, to_up, *ahead.values))
+        down = self.ring.down(self.order.run(add_down, to_down, *behind.values))
+        self.flight = (down, up)
 
     def finish(self, function=None, *more):
         own = self.parts.pop()
@@ -585,10 +590,8 @@
 
 
 def assemble_body(sizes, runs, places, at_ref, *refs):
-    count = len(runs)
-    chunks = refs[:count]
-    outs = refs[count : count + len(sizes)]
-    scratch, in_sems, out_sems = refs[count + len(sizes) :]
+    chunks = refs[: len(runs)]
+    outs, (scratch, in_sems, out_sems) = refs[-3 - len(sizes) : -3], refs[-3:]
     loads = [
         pltpu.make_async_copy(
             chunk, scratch.at[slot, pl.ds(first, rows)], in_sems.at[i]
@@ -618,27 +621,34 @@
         store.wait()
 
 
-def assemble(ring, sizes, gathered):
-    near = [(0, (gathered.own,))]
-    for k, (u, d) in enumerate(gathered.pairs, 1):
-        near += [(k, (u,)), (-k, (d,))]
-    near.append((ring.reach, gathered.far))
+def assemble_whole(ring, sizes, gathered):
+    return assemble(ring, sizes, gathered, None, 0, 2 * ring.chips)
+
+
+def assemble(ring, sizes, gathered, into, low, high):
+    near = [(gathered.own,)] + [(v,) for pair in gathered.pairs for v in pair]
     their = [gathered.theirs[0]]
-    for pair in gathered.theirs[1:-1]:
+    for pair in gathered.theirs[1 : ring.reach]:
         their += [(v,) for v in pair]
-    their.append(gathered.theirs[-1])
+    if gathered.far is not None:
+        near.append(gathered.far)
+        their.append(gathered.theirs[-1])
     rows, width = gathered.own.shape
     slots = []
-    for (distance, mine), theirs in zip(near, their):
+    for distance, mine, theirs in zip(ring_distances(ring), near, their):
         chip = ring.chip_at(distance)
         slots += [(2 * chip + ring.core, mine), (2 * chip + 1 - ring.core, theirs)]
-    at = jnp.stack([place for place, _ in slots]).astype(jnp.int32)
-    places = len(slots)
     if any(size % 16 for size in sizes):
+        if high < 2 * ring.chips:
+            return list(slots[0][1])
+        at = jnp.stack([place for place, _ in slots]).astype(jnp.int32)
         every = jnp.stack([jnp.concatenate(v) if len(v) > 1 else v[0] for _, v in slots])
         every = jnp.zeros_like(every).at[at].set(every)
         cuts = [sum(sizes[:i]) for i in range(len(sizes) + 1)]
         return [every[:, a:b].reshape(-1, width) for a, b in zip(cuts, cuts[1:])]
+    slots = slots[low:high]
+    at = jnp.stack([place for place, _ in slots]).astype(jnp.int32)
+    places = len(slots)
     chunks, runs = [], []
     for slot, (_, values) in enumerate(slots):
         first = 0
@@ -647,11 +657,14 @@
             runs.append((slot, first, value.shape[0]))
             first += value.shape[0]
     anywhere = pl.BlockSpec(memory_space=pl.ANY)
+    more = [] if into is None else list(into)
     return pl.pallas_call(
         functools.partial(assemble_body, sizes, runs, places),
-        out_shape=[shaped(places * size, width, BF16) for size in sizes],
-        in_specs=[pl.BlockSpec(memory_space=pltpu.SMEM)] + [anywhere] * len(chunks),
+        out_shape=[shaped(2 * ring.chips * size, width, BF16) for size in sizes],
+        in_specs=[pl.BlockSpec(memory_space=pltpu.SMEM)]
+        + [anywhere] * (len(chunks) + len(more)),
         out_specs=[anywhere] * len(sizes),
+        input_output_aliases={1 + len(chunks) + i: i for i in range(len(more))},
         scratch_shapes=[
             pltpu.VMEM((places, rows, width), BF16),
             pltpu.SemaphoreType.DMA((len(chunks),)),
@@ -659,7 +672,7 @@
         ],
         cost_estimate=LIGHT,
         compiler_params=BIG,
-    )(at, *chunks)
+    )(at, *chunks, *more)
 
 
 def ring_distances(ring):
@@ -1054,7 +1067,7 @@
     two.start()
     one.finish()
     wide_s, wide_gates, wide_small = order.run(
-        lambda *_: assemble(ring, (shard, n_gate, 16), one), one.theirs[-1][0]
+        lambda *_: assemble_whole(ring, (shard, n_gate, 16), one), one.theirs[-1][0]
     )
     wide_small = wide_small.reshape(count, 16, width)[:, 0]
     n_gain = gain_mixer.shape[0]
@@ -1081,15 +1094,20 @@
     enter.next()
     incoming = enter.finish()
     two.next()
+    two.settle()
     hid_g = order.arrive(hid_g)
+    near_slots = 2 * (ring.chips - 1)
+    wide_two = order.run(
+        lambda *_: assemble(ring, (shard, shard), two, None, 0, near_slots), two.theirs[-1][0]
+    )
     two.finish()
     dy = Gather(ring, order, cotangent)
     dy.start()
     wide_b, wide_o = order.run(
-        lambda *_: assemble(ring, (shard, shard), two), two.theirs[-1][0]
-    )
-    dy.next()
-
+        lambda _, *near: assemble(ring, (shard, shard), two, near, near_slots, near_slots + 2),
+        two.theirs[-1][0],
+        *wide_two,
+    )
     def merge(h, w, local, p, inc):
         pre = cols_inner(h, w)
         return pre, ((local + p * inc) * gelu_tanh(pre)).astype(BF16)
@@ -1103,6 +1121,7 @@
 
     mix_theirs = order.run(lambda m, w: mix_out(m, w, theirs_at).astype(BF16), merged, wide_o)
     mix_got = tensor_swap(mix_theirs)
+    dy.next()
     mix_mine = order.run(lambda m, w: mix_out(m, w, mine_at), merged, wide_o)
     dy.next()
     x_val = block_input.astype(F32)

time: 603 us -> 601 us (level)
  local copies, waits for them, and re-layouts: 42.5 us -> 55.8 us
  waiting for transfers between devices: 186 us -> 175 us
    ppermute x32, waiting for transfers between devices: 93.3 us -> 43.1 us  [down(): return lax.ppermute(value, 'dp', self.down_route)]
    ppermute x32, waiting for transfers between devices: 75.4 us -> 115 us  [up(): return lax.ppermute(value, 'dp', self.up_route)]
    ppermute x32, starting transfers between devices: 38.7 us -> 30.3 us  [up(): return lax.ppermute(value, 'dp', self.up_route)]
    ppermute x32, starting transfers between devices: 33.6 us -> 40.3 us  [down(): return lax.ppermute(value, 'dp', self.down_route)]
    unnamed x224 -> x210, local copies, waits for them, and re-layouts: 22.4 us -> 26.2 us
    pallas_call x2 -> x3, Pallas kernels: 17.5 us -> 19.7 us  [assemble(): pl.pallas_call(functools.partial(assemble_body, sizes, runs, places), out...]
  transfers between devices with their start and end apart: 102 -> 102, of which waited for: 48 -> 44; matrix products, arithmetic and copies ran while one was open for 22% -> 24% of each run, Pallas kernels for 19% -> 20%
where the time goes in v4:
time: 601 us; the launch traced here: 592 us
  waiting for transfers between devices  175 us (29%)
  Pallas kernels  119 us (20%)
  starting transfers between devices  98.9 us (16%)
  other arithmetic  68 us (11%)
  matrix products  58.3 us (10%)
  local copies, waits for them, and re-layouts  55.8 us (9%)
  between operations  16.5 us (3%)
    ppermute x32, waiting for transfers between devices, up(): return lax.ppermute(value, 'dp', self.up_route)  115 us
    ppermute x32, waiting for transfers between devices, down(): return lax.ppermute(value, 'dp', self.down_route)  43.1 us
    ppermute x32, starting transfers between devices, down(): return lax.ppermute(value, 'dp', self.down_route)  40.3 us
    dot_general x14, matrix products, cols_inner(): lax.dot_general(left, right, (((1,), (1,)), ((), ())), preferred_element_...  34.2 us
    ppermute x32, starting transfers between devices, up(): return lax.ppermute(value, 'dp', self.up_route)  30.3 us
    pallas_call x3, Pallas kernels, hidden_grad(): pl.pallas_call(functools.partial(hidden_grad_body, heights, right_heights...  29.6 us
    unnamed x210, local copies, waits for them, and re-layouts  26.2 us
    convert_element_type x24, other arithmetic, __call__(): return total.astype(dtype)  22.4 us
  transfers between devices with their start and end apart: 102, of which 44 were waited for; matrix products, arithmetic and copies ran while one was open for 24% of the time, Pallas kernels for 20%

profile of v4, /device:TPU:0, one launch (start us, length us, event | category | flops | bytes accessed | tf_op | source)
XLA Modules:
  0.0 591.5 jit_solution(5691661569763389866)
XLA Ops:
  9.9 2.6 collective-permute-start.2
  16.5 9.5 %collective-permute-done.2.refs_2_ = bf16[112,2560]{1,0:T(8,128)(2,1)S(1)} collective-permute-done((bf16[112,2560]{1,0:T(8,128)(2,1)S(1)}, bf16[112,2560]{1,0:T(8,128)(2,1)S(1)}, u32[]{:S(2)}, u32[]{:S(2)}) %collective-permute-start.2) | collective-permute-done | bytes 573472 | tf_op jit(solution)/shard_map/ppermute | solution.py:47
  32.6 4.5 collective-permute-done
  37.1 4.8 collective-permute-done.7.refs_6_
  48.1 11.2 %collective-permute-done.11.refs_10_ = bf16[112,2560]{1,0:T(8,128)(2,1)} collective-permute-done((bf16[112,2560]{1,0:T(8,128)(2,1)}, bf16[112,2560]{1,0:T(8,128)(2,1)}, u32[]{:S(2)}, u32[]{:S(2)}) %collective-permute-start.11) | collective-permute-done | bytes 573472 | tf_op jit(solution)/shard_map/ppermute | solution.py:47
  71.0 4.9 collective-permute-done.16.refs_15_
  76.4 2.6 pad_maximum_fusion
  81.0 7.4 %shard_map.254 = (bf16[1280,2560]{1,0:T(8,128)(2,1)}, bf16[256,2560]{1,0:T(8,128)(2,1)}, bf16[256,2560]{1,0:T(8,128)(2,1)}) custom-call(s32[16]{0:T(128)S(1)} %stack.178.at_ref, bf16[112,2560]{1,0:T(8,128)(2,1)S(1)} %pad_maximum_fusion.9.refs_0_, bf16[112,2560]{1,0:T(8,128)(2,1)S(1)} %collective-permute-done.1.refs_1_, bf16[112,2560]{1,0:T(8,128)(2,1)S(1)} %copy-done.33, ...), custom_call_target="tpu_custom_call" | custom-call | tf_op jit(solution)/shard_map/pallas_call | solution.py:661
  93.2 6.1 %collective-permute-done.20.refs_2_ = bf16[160,2560]{1,0:T(8,128)(2,1)} collective-permute-done((bf16[160,2560]{1,0:T(8,128)(2,1)S(1)}, bf16[160,2560]{1,0:T(8,128)(2,1)}, u32[]{:S(2)}, u32[]{:S(2)}) %collective-permute-start.20) | collective-permute-done | bytes 819232 | tf_op jit(solution)/shard_map/ppermute | solution.py:47
  103.0 6.1 %convolution_convert_fusion.1.pad_ref.refs_7_ = bf16[272,1280]{1,0:T(8,128)(2,1)} fusion(bf16[272,2560]{1,0:T(8,128)(2,1)} %fusion.6, bf16[1280,2560]{1,0:T(8,128)(2,1)} %get-tuple-element.682), kind=kOutput, calls=%fused_computation.16 | convolution fusion | flops 1782927360 | bytes 8642560 | tf_op jit(solution)/shard_map/dot_general | solution.py:303
  110.3 6.6 %shard_map.255 = (bf16[256,1280]{1,0:T(8,128)(2,1)S(1)}, f32[256,1280]{1,0:T(8,128)S(1)}, f32[256,1280]{1,0:T(8,128)S(1)}, f32[256,1280]{1,0:T(8,128)S(1)}, f32[2,1280]{1,0:T(2,128)S(1)}) custom-call(bf16[272,1280]{1,0:T(8,128)(2,1)S(1)} %copy-done.28, f32[256,8]{1,0:T(8,128)S(1)} %copy.141.marks_ref, ...), custom_call_target="tpu_custom_call" | custom-call | tf_op jit(solution)/shard_map/pallas_call | solution.py:488
  126.2 3.8 collective-permute-start.32
  130.0 3.3 collective-permute-start.31
  133.3 11.6 %collective-permute-done.32 = f32[2,1280]{1,0:T(2,128)S(1)} collective-permute-done((f32[2,1280]{1,0:T(2,128)S(1)}, f32[2,1280]{1,0:T(2,128)S(1)}, u32[]{:S(2)}, u32[]{:S(2)}) %collective-permute-start.32) | collective-permute-done | bytes 10272 | tf_op jit(solution)/shard_map/ppermute | solution.py:244
  151.7 9.3 %shard_map.256 = (bf16[1280,2560]{1,0:T(8,128)(2,1)}, bf16[1280,2560]{1,0:T(8,128)(2,1)}) custom-call(s32[14]{0:T(128)S(1)} %stack.190.at_ref, bf16[160,2560]{1,0:T(8,128)(2,1)S(1)} %constant_dynamic-update-slice_fusion.refs_0_, bf16[160,2560]{1,0:T(8,128)(2,1)S(1)} %collective-permute-done.19.refs_1_, bf16[160,2560]{1,0:T(8,128)(2,1)} %collective-permute-done.20.refs_2_, ...), custom_call_target="tpu_custom_call" | custom-call | tf_op jit(solution)/shard_map/pallas_call | solution.py:661
  167.3 2.9 shard_map.257
  170.3 4.9 fusion.131.pre_ref
  178.8 3.0 collective-permute-done.39
  190.2 8.8 %collective-permute-done.42 = bf16[128,2560]{1,0:T(8,128)(2,1)} collective-permute-done((bf16[128,2560]{1,0:T(8,128)(2,1)}, bf16[128,2560]{1,0:T(8,128)(2,1)}, u32[]{:S(2)}, u32[]{:S(2)}) %collective-permute-start.42) | collective-permute-done | bytes 655392 | tf_op jit(solution)/shard_map/ppermute | solution.py:47
  209.1 11.9 %shard_map.258 = (bf16[128,960]{1,0:T(8,128)(2,1)S(1)}, bf16[128,960]{1,0:T(8,128)(2,1)S(1)}, bf16[128,960]{1,0:T(8,128)(2,1)S(1)}, bf16[128,2560]{1,0:T(8,128)(2,1)S(1)}) custom-call(bf16[128,2560]{1,0:T(8,128)(2,1)S(1)} %multiply_convert_fusion.refs_0_.refs_5_, bf16[128,2560]{1,0:T(8,128)(2,1)S(1)} %copy-done.2, ...), custom_call_target="tpu_custom_call" | custom-call | tf_op jit(solution)/shard_map/pallas_call | solution.py:897
  221.0 8.4 %collective-permute-done.46 = bf16[128,2560]{1,0:T(8,128)(2,1)} collective-permute-done((bf16[128,2560]{1,0:T(8,128)(2,1)}, bf16[128,2560]{1,0:T(8,128)(2,1)}, u32[]{:S(2)}, u32[]{:S(2)}) %collective-permute-start.46) | collective-permute-done | bytes 655392 | tf_op jit(solution)/shard_map/ppermute | solution.py:47
  243.3 3.4 multiply_convert_fusion.5
  250.9 6.8 %collective-permute-done.48 = bf16[128,2560]{1,0:T(8,128)(2,1)S(1)} collective-permute-done((bf16[128,2560]{1,0:T(8,128)(2,1)}, bf16[128,2560]{1,0:T(8,128)(2,1)S(1)}, u32[]{:S(2)}, u32[]{:S(2)}) %collective-permute-start.48) | collective-permute-done | bytes 655392 | tf_op jit(solution)/shard_map/ppermute | solution.py:47
  263.1 3.4 multiply_convert_fusion.3
  293.3 8.5 %collective-permute-done.57 = bf16[64,2560]{1,0:T(8,128)(2,1)S(1)} collective-permute-done((bf16[64,2560]{1,0:T(8,128)(2,1)S(1)}, bf16[64,2560]{1,0:T(8,128)(2,1)S(1)}, u32[]{:S(2)}, u32[]{:S(2)}) %collective-permute-start.57) | collective-permute-done | bytes 327712 | tf_op jit(solution)/shard_map/ppermute | solution.py:47
  305.8 9.7 %shard_map.259 = (bf16[128,2560]{1,0:T(8,128)(2,1)S(1)}, bf16[256,2560]{1,0:T(8,128)(2,1)S(1)}, bf16[256,2560]{1,0:T(8,128)(2,1)S(1)}, bf16[256,2560]{1,0:T(8,128)(2,1)}, bf16[128,2560]{1,0:T(8,128)(2,1)S(1)}) custom-call(bf16[128,960]{1,0:T(8,128)(2,1)S(1)} %get-tuple-element.591.refs_0_, bf16[256,960]{1,0:T(8,128)(2,1)S(1)} %get-tuple-element.592.refs_1_, ...), custom_call_target="tpu_custom_call" | custom-call | tf_op jit(solution)/shard_map/pallas_call | solution.py:962
  315.5 3.3 collective-permute-done.59
  326.0 9.8 %shard_map.260.refs_10_ = bf16[4,3,240,2560]{3,2,1,0:T(8,128)(2,1)} custom-call(bf16[128,960]{1,0:T(8,128)(2,1)S(1)} %get-tuple-element.559.refs_0_, bf16[256,960]{1,0:T(8,128)(2,1)S(1)} %copy-done.37, bf16[256,960]{1,0:T(8,128)(2,1)S(1)} %copy-done.39, bf16[256,960]{1,0:T(8,128)(2,1)S(1)} %copy-done.41, bf16[128,960]{1,0:T(8,128)(2,1)S(1)} %get-tuple-element.563.refs_4_, ...), custom_call_target="tpu_custom_call" | custom-call | tf_op jit(solution)/shard_map/pallas_call | solution.py:826
  343.5 9.7 %shard_map.261.refs_10_ = bf16[4,3,240,2560]{3,2,1,0:T(8,128)(2,1)} custom-call(bf16[128,960]{1,0:T(8,128)(2,1)S(1)} %get-tuple-element.573.refs_0_, bf16[256,960]{1,0:T(8,128)(2,1)S(1)} %get-tuple-element.574.refs_1_, bf16[256,960]{1,0:T(8,128)(2,1)S(1)} %get-tuple-element.575.refs_2_, ...), custom_call_target="tpu_custom_call", output_to_operand_aliasing={{}: (10, {})} | custom-call | tf_op jit(solution)/shard_map/pallas_call | solution.py:826
  368.7 10.2 %shard_map.262 = bf16[4,3,240,2560]{3,2,1,0:T(8,128)(2,1)} custom-call(bf16[128,960]{1,0:T(8,128)(2,1)S(1)} %get-tuple-element.591.refs_0_, bf16[256,960]{1,0:T(8,128)(2,1)S(1)} %copy-done.14, bf16[256,960]{1,0:T(8,128)(2,1)S(1)} %copy-done.16, bf16[256,960]{1,0:T(8,128)(2,1)S(1)} %copy-done.18, ...), custom_call_target="tpu_custom_call", output_to_operand_aliasing={{}: (10, {})} | custom-call | tf_op jit(solution)/shard_map/pallas_call | solution.py:826
  383.8 8.1 %shard_map.263 = (bf16[256,1280]{1,0:T(8,128)(2,1)S(1)}, f32[256,1280]{1,0:T(8,128)S(1)}, f32[256,1280]{1,0:T(8,128)S(1)}, f32[2,1280]{1,0:T(2,128)S(1)}) custom-call(bf16[256,2560]{1,0:T(8,128)(2,1)S(1)} %pad_maximum_fusion.1.dz_ref.refs_3_, bf16[1280,2560]{1,0:T(8,128)(2,1)} %get-tuple-element.609.wide_ref, f32[256,1280]{1,0:T(8,128)S(1)} %copy-done.8, ...), custom_call_target="tpu_custom_call" | custom-call | tf_op jit(solution)/shard_map/pallas_call | solution.py:520
  395.8 10.7 %shard_map.264 = (bf16[8,160,2560]{2,1,0:T(8,128)(2,1)}, bf16[8,160,2560]{2,1,0:T(8,128)(2,1)}) custom-call(s32[9]{0:T(128)S(1)} %stack.200.at_ref, bf16[256,1280]{1,0:T(8,128)(2,1)S(1)} %get-tuple-element.679.refs_0_, bf16[256,1280]{1,0:T(8,128)(2,1)S(1)} %fusion.26.refs_1_, bf16[256,2560]{1,0:T(8,128)(2,1)S(1)} %slice.554.refs_2_.refs_1_, ...), custom_call_target="tpu_custom_call" | custom-call | tf_op jit(solution)/shard_map/pallas_call | solution.py:744
  406.6 4.5 collective-permute-done.70
  422.7 8.6 %shard_map.265 = (bf16[256,1280]{1,0:T(8,128)(2,1)S(1)}, f32[8,1280]{1,0:T(8,128)S(1)}, f32[8,1280]{1,0:T(8,128)S(1)}, f32[8,1280]{1,0:T(8,128)S(1)}, bf16[256,2560]{1,0:T(8,128)(2,1)S(1)}) custom-call(f32[256,1280]{1,0:T(8,128)S(1)} %copy-done.47, f32[256,1280]{1,0:T(8,128)} %copy-done.48, f32[1,1280]{1,0:T(1,128)S(1)} %slice_add_fusion.refs_2_, ...), custom_call_target="tpu_custom_call" | custom-call | flops 499999997952 | tf_op jit(solution)/shard_map/pallas_call | solution.py:557
  438.1 3.0 add_convert_fusion.1
  443.2 4.2 fusion.94
  449.8 3.5 collective-permute-done.79
  459.3 7.1 %shard_map.266 = (bf16[8,96,2560]{2,1,0:T(8,128)(2,1)}, bf16[8,96,2560]{2,1,0:T(8,128)(2,1)}) custom-call(s32[9]{0:T(128)S(1)} %copy-done.45, bf16[256,1280]{1,0:T(8,128)(2,1)S(1)} %fusion.107.refs_0_, bf16[256,2560]{1,0:T(8,128)(2,1)S(1)} %slice.554.refs_2_.refs_1_, bf16[256,2560]{1,0:T(8,128)(2,1)S(1)} %get-tuple-element.676.refs_2_), custom_call_target="tpu_custom_call" | custom-call | tf_op jit(solution)/shard_map/pallas_call | solution.py:744
  467.5 4.0 convolution_add_fusion.4.mine_ref
  475.6 2.6 fusion.11
  478.2 2.6 fusion.10
  486.2 3.0 shard_map.267
  492.6 12.8 %collective-permute-done.85 = bf16[160,2560]{1,0:T(8,128)(2,1)} collective-permute-done((bf16[160,2560]{1,0:T(8,128)(2,1)}, bf16[160,2560]{1,0:T(8,128)(2,1)}, u32[]{:S(2)}, u32[]{:S(2)}) %collective-permute-start.85) | collective-permute-done | bytes 819232 | tf_op jit(solution)/shard_map/ppermute | solution.py:50
  506.8 3.3 collective-permute-done.88
  526.8 19.0 %collective-permute-done.93 = bf16[97,2560]{1,0:T(8,128)(2,1)} collective-permute-done((bf16[97,2560]{1,0:T(8,128)(2,1)}, bf16[97,2560]{1,0:T(8,128)(2,1)}, u32[]{:S(2)}, u32[]{:S(2)}) %collective-permute-start.93) | collective-permute-done | bytes 496672 | tf_op jit(solution)/shard_map/ppermute | solution.py:47
  557.1 5.7 collective-permute-done.95
  571.9 3.6 shard_map.268
  575.5 3.2 collective-permute-done.96
  (593 shorter events, 266.4 us)
Async XLA Ops:
  7.2 201.8 %all-gather.4.cloned.1.call-start = ((), (), s32[]{:S(2)}) async-start(), calls=%async_computation.1 | async-start | bytes 6144000 | tf_op jit(solution)/shard_map/all_gather | solution.py:222
  7.9 201.1 %all-gather.6.cloned.1.call-start = ((), (), s32[]{:S(2)}) async-start(), calls=%async_computation.2 | async-start | bytes 6144000 | tf_op jit(solution)/shard_map/all_gather | solution.py:222
  8.7 200.4 %all-gather.8.cloned.1.call-start = ((), (), s32[]{:S(2)}) async-start(), calls=%async_computation.3 | async-start | bytes 6144000 | tf_op jit(solution)/shard_map/all_gather | solution.py:222
  9.3 18.3 %collective-permute-start.1 = (bf16[112,2560]{1,0:T(8,128)(2,1)S(1)}, bf16[112,2560]{1,0:T(8,128)(2,1)S(1)}, u32[]{:S(2)}, u32[]{:S(2)}) collective-permute-start(bf16[112,2560]{1,0:T(8,128)(2,1)S(1)} %pad_maximum_fusion.9.refs_0_), channel_id=1, source_target_pairs={{0,2},{2,0},{4,6},{6,4},{8,10},{10,8},{12,14},{14,12},{16,18},{18,... | collective-permute-start | bytes 1720328 | tf_op jit(solution)/shard_map/ppermute | solution.py:211
  12.5 24.6 %collective-permute-start = (bf16[128,2560]{1,0:T(8,128)(2,1)S(1)}, bf16[128,2560]{1,0:T(8,128)(2,1)}, u32[]{:S(2)}, u32[]{:S(2)}) collective-permute-start(bf16[128,2560]{1,0:T(8,128)(2,1)S(1)} %copy-done), channel_id=1, source_target_pairs={{0,1},{1,0},{2,3},{3,2},{4,5},{5,4},{6,7},{7,6},{8,9},{9,8},{10,11... | collective-permute-start | bytes 1966088 | tf_op jit(solution)/shard_map/ppermute | solution.py:238
  43.5 17.1 %collective-permute-start.9 = (bf16[112,2560]{1,0:T(8,128)(2,1)}, bf16[112,2560]{1,0:T(8,128)(2,1)S(1)}, u32[]{:S(2)}, u32[]{:S(2)}) collective-permute-start(bf16[112,2560]{1,0:T(8,128)(2,1)} %collective-permute-done.7.refs_6_), channel_id=1, source_target_pairs={{0,2},{2,0},{4,6},{6,4},{8,10},{10,8},{12,14},{14,12},{16,18},{18,... | collective-permute-start | bytes 1720328 | tf_op jit(solution)/shard_map/ppermute | solution.py:211
  43.5 17.9 %collective-permute-start.10 = (bf16[112,2560]{1,0:T(8,128)(2,1)}, bf16[112,2560]{1,0:T(8,128)(2,1)S(1)}, u32[]{:S(2)}, u32[]{:S(2)}) collective-permute-start(bf16[112,2560]{1,0:T(8,128)(2,1)} %collective-permute-done.8.refs_8_), channel_id=1, source_target_pairs={{0,2},{2,0},{4,6},{6,4},{8,10},{10,8},{12,14},{14,12},{16,18},{18,... | collective-permute-start | bytes 1720328 | tf_op jit(solution)/shard_map/ppermute | solution.py:211
  70.9 22.2 %collective-permute-start.19 = (bf16[160,2560]{1,0:T(8,128)(2,1)S(1)}, bf16[160,2560]{1,0:T(8,128)(2,1)S(1)}, u32[]{:S(2)}, u32[]{:S(2)}) collective-permute-start(bf16[160,2560]{1,0:T(8,128)(2,1)S(1)} %constant_dynamic-update-slice_fusion.refs_0_), channel_id=1, source_target_pairs={{0,2},{2,0},{4,6},{6,4},{8,10},{10,8},{12,14},{14,12},{16,18},{18,... | collective-permute-start | bytes 2457608 | tf_op jit(solution)/shard_map/ppermute | solution.py:211
  79.0 20.3 %collective-permute-start.20 = (bf16[160,2560]{1,0:T(8,128)(2,1)S(1)}, bf16[160,2560]{1,0:T(8,128)(2,1)}, u32[]{:S(2)}, u32[]{:S(2)}) collective-permute-start(bf16[160,2560]{1,0:T(8,128)(2,1)S(1)} %constant_dynamic-update-slice_fusion.refs_0_), channel_id=1, source_target_pairs={{0,8},{2,10},{8,16},{10,18},{16,24},{18,26},{24,28},{26,30},{28,20... | collective-permute-start | bytes 2457608 | tf_op jit(solution)/shard_map/ppermute | solution.py:47
  79.6 20.0 %collective-permute-start.21 = (bf16[160,2560]{1,0:T(8,128)(2,1)S(1)}, bf16[160,2560]{1,0:T(8,128)(2,1)}, u32[]{:S(2)}, u32[]{:S(2)}) collective-permute-start(bf16[160,2560]{1,0:T(8,128)(2,1)S(1)} %constant_dynamic-update-slice_fusion.refs_0_), channel_id=1, source_target_pairs={{8,0},{10,2},{16,8},{18,10},{24,16},{26,18},{28,24},{30,26},{20,28... | collective-permute-start | bytes 2457608 | tf_op jit(solution)/shard_map/ppermute | solution.py:50
  99.7 21.8 %collective-permute-start.22 = (bf16[160,2560]{1,0:T(8,128)(2,1)}, bf16[160,2560]{1,0:T(8,128)(2,1)}, u32[]{:S(2)}, u32[]{:S(2)}) collective-permute-start(bf16[160,2560]{1,0:T(8,128)(2,1)} %collective-permute-done.20.refs_2_), channel_id=1, source_target_pairs={{0,2},{2,0},{4,6},{6,4},{8,10},{10,8},{12,14},{14,12},{16,18},{18,... | collective-permute-start | bytes 2457608 | tf_op jit(solution)/shard_map/ppermute | solution.py:211
  99.7 21.8 %collective-permute-start.23 = (bf16[160,2560]{1,0:T(8,128)(2,1)}, bf16[160,2560]{1,0:T(8,128)(2,1)}, u32[]{:S(2)}, u32[]{:S(2)}) collective-permute-start(bf16[160,2560]{1,0:T(8,128)(2,1)} %collective-permute-done.21.refs_4_), channel_id=1, source_target_pairs={{0,2},{2,0},{4,6},{6,4},{8,10},{10,8},{12,14},{14,12},{16,18},{18,... | collective-permute-start | bytes 2457608 | tf_op jit(solution)/shard_map/ppermute | solution.py:211
  100.8 20.5 %collective-permute-start.24 = (bf16[160,2560]{1,0:T(8,128)(2,1)}, bf16[160,2560]{1,0:T(8,128)(2,1)}, u32[]{:S(2)}, u32[]{:S(2)}) collective-permute-start(bf16[160,2560]{1,0:T(8,128)(2,1)} %collective-permute-done.20.refs_2_), channel_id=1, source_target_pairs={{0,8},{2,10},{8,16},{10,18},{16,24},{18,26},{24,28},{26,30},{28,20... | collective-permute-start | bytes 2457608 | tf_op jit(solution)/shard_map/ppermute | solution.py:47
  101.3 20.2 %collective-permute-start.25 = (bf16[160,2560]{1,0:T(8,128)(2,1)}, bf16[160,2560]{1,0:T(8,128)(2,1)}, u32[]{:S(2)}, u32[]{:S(2)}) collective-permute-start(bf16[160,2560]{1,0:T(8,128)(2,1)} %collective-permute-done.21.refs_4_), channel_id=1, source_target_pairs={{8,0},{10,2},{16,8},{18,10},{24,16},{26,18},{28,24},{30,26},{20,28... | collective-permute-start | bytes 2457608 | tf_op jit(solution)/shard_map/ppermute | solution.py:50
  122.0 447.8 %reduce-scatter.2.cloned.1.call-start = ((), (), s32[]{:S(2)}) async-start(), calls=%async_computation.4 | async-start | bytes 18432000 | tf_op jit(solution)/shard_map/reduce_scatter | solution.py:228
  124.1 20.9 %collective-permute-start.26 = (bf16[160,2560]{1,0:T(8,128)(2,1)}, bf16[160,2560]{1,0:T(8,128)(2,1)}, u32[]{:S(2)}, u32[]{:S(2)}) collective-permute-start(bf16[160,2560]{1,0:T(8,128)(2,1)} %collective-permute-done.24.refs_6_), channel_id=1, source_target_pairs={{0,8},{2,10},{8,16},{10,18},{16,24},{18,26},{24,28},{26,30},{28,20... | collective-permute-start | bytes 2457608 | tf_op jit(solution)/shard_map/ppermute | solution.py:47
  125.5 21.1 %collective-permute-start.27 = (bf16[160,2560]{1,0:T(8,128)(2,1)}, bf16[160,2560]{1,0:T(8,128)(2,1)}, u32[]{:S(2)}, u32[]{:S(2)}) collective-permute-start(bf16[160,2560]{1,0:T(8,128)(2,1)} %collective-permute-done.25.refs_8_), channel_id=1, source_target_pairs={{8,0},{10,2},{16,8},{18,10},{24,16},{26,18},{28,24},{30,26},{20,28... | collective-permute-start | bytes 2457608 | tf_op jit(solution)/shard_map/ppermute | solution.py:50
  126.2 18.7 %collective-permute-start.32 = (f32[2,1280]{1,0:T(2,128)S(1)}, f32[2,1280]{1,0:T(2,128)S(1)}, u32[]{:S(2)}, u32[]{:S(2)}) collective-permute-start(f32[2,1280]{1,0:T(2,128)S(1)} %pad_maximum_fusion.14), channel_id=1, source_target_pairs={{0,6},{2,8},{4,10},{6,12},{8,14},{10,16},{12,18},{14,20},{16,22},{... | collective-permute-start | bytes 30728 | tf_op jit(solution)/shard_map/ppermute | solution.py:244
  177.3 23.1 %collective-permute-start.41 = (bf16[128,2560]{1,0:T(8,128)(2,1)S(1)}, bf16[128,2560]{1,0:T(8,128)(2,1)S(1)}, u32[]{:S(2)}, u32[]{:S(2)}) collective-permute-start(bf16[128,2560]{1,0:T(8,128)(2,1)S(1)} %convolution_convert_fusion), channel_id=1, source_target_pairs={{0,1},{1,0},{2,3},{3,2},{4,5},{5,4},{6,7},{7,6},{8,9},{9,8},{10,11... | collective-permute-start | bytes 1966088 | tf_op jit(solution)/shard_map/ppermute | solution.py:238
  200.9 30.0 %collective-permute-start.44 = (bf16[128,2560]{1,0:T(8,128)(2,1)S(1)}, bf16[128,2560]{1,0:T(8,128)(2,1)}, u32[]{:S(2)}, u32[]{:S(2)}) collective-permute-start(bf16[128,2560]{1,0:T(8,128)(2,1)S(1)} %multiply_convert_fusion.refs_0_.refs_5_), channel_id=1, source_target_pairs={{0,8},{2,10},{8,16},{10,18},{16,24},{18,26},{24,28},{26,30},{28,20... | collective-permute-start | bytes 1966088 | tf_op jit(solution)/shard_map/ppermute | solution.py:47
  201.5 29.5 %collective-permute-start.45 = (bf16[128,2560]{1,0:T(8,128)(2,1)S(1)}, bf16[128,2560]{1,0:T(8,128)(2,1)}, u32[]{:S(2)}, u32[]{:S(2)}) collective-permute-start(bf16[128,2560]{1,0:T(8,128)(2,1)S(1)} %multiply_convert_fusion.refs_0_.refs_5_), channel_id=1, source_target_pairs={{8,0},{10,2},{16,8},{18,10},{24,16},{26,18},{28,24},{30,26},{20,28... | collective-permute-start | bytes 1966088 | tf_op jit(solution)/shard_map/ppermute | solution.py:50
  203.0 26.4 %collective-permute-start.46 = (bf16[128,2560]{1,0:T(8,128)(2,1)}, bf16[128,2560]{1,0:T(8,128)(2,1)}, u32[]{:S(2)}, u32[]{:S(2)}) collective-permute-start(bf16[128,2560]{1,0:T(8,128)(2,1)} %collective-permute-done.42), channel_id=1, source_target_pairs={{0,8},{2,10},{8,16},{10,18},{16,24},{18,26},{24,28},{26,30},{28,20... | collective-permute-start | bytes 1966088 | tf_op jit(solution)/shard_map/ppermute | solution.py:47
  203.5 26.2 %collective-permute-start.47 = (bf16[128,2560]{1,0:T(8,128)(2,1)}, bf16[128,2560]{1,0:T(8,128)(2,1)}, u32[]{:S(2)}, u32[]{:S(2)}) collective-permute-start(bf16[128,2560]{1,0:T(8,128)(2,1)} %collective-permute-done.43), channel_id=1, source_target_pairs={{8,0},{10,2},{16,8},{18,10},{24,16},{26,18},{28,24},{30,26},{20,28... | collective-permute-start | bytes 1966088 | tf_op jit(solution)/shard_map/ppermute | solution.py:50
  234.5 23.3 %collective-permute-start.51 = (bf16[64,2560]{1,0:T(8,128)(2,1)S(1)}, bf16[64,2560]{1,0:T(8,128)(2,1)S(1)}, u32[]{:S(2)}, u32[]{:S(2)}) collective-permute-start(bf16[64,2560]{1,0:T(8,128)(2,1)S(1)} %slice.453), channel_id=1, source_target_pairs={{8,0},{10,2},{16,8},{18,10},{24,16},{26,18},{28,24},{30,26},{20,28... | collective-permute-start | bytes 983048 | tf_op jit(solution)/shard_map/ppermute | solution.py:50
  236.0 21.8 %collective-permute-start.50 = (bf16[64,2560]{1,0:T(8,128)(2,1)S(1)}, bf16[64,2560]{1,0:T(8,128)(2,1)S(1)}, u32[]{:S(2)}, u32[]{:S(2)}) collective-permute-start(bf16[64,2560]{1,0:T(8,128)(2,1)S(1)} %slice.452), channel_id=1, source_target_pairs={{0,8},{2,10},{8,16},{10,18},{16,24},{18,26},{24,28},{26,30},{28,20... | collective-permute-start | bytes 983048 | tf_op jit(solution)/shard_map/ppermute | solution.py:47
  236.5 21.2 %collective-permute-start.48 = (bf16[128,2560]{1,0:T(8,128)(2,1)}, bf16[128,2560]{1,0:T(8,128)(2,1)S(1)}, u32[]{:S(2)}, u32[]{:S(2)}) collective-permute-start(bf16[128,2560]{1,0:T(8,128)(2,1)} %collective-permute-done.44), channel_id=1, source_target_pairs={{0,8},{2,10},{8,16},{10,18},{16,24},{18,26},{24,28},{26,30},{28,20... | collective-permute-start | bytes 1966088 | tf_op jit(solution)/shard_map/ppermute | solution.py:47
  237.7 20.1 %collective-permute-start.49 = (bf16[128,2560]{1,0:T(8,128)(2,1)}, bf16[128,2560]{1,0:T(8,128)(2,1)S(1)}, u32[]{:S(2)}, u32[]{:S(2)}) collective-permute-start(bf16[128,2560]{1,0:T(8,128)(2,1)} %collective-permute-done.45), channel_id=1, source_target_pairs={{8,0},{10,2},{16,8},{18,10},{24,16},{26,18},{28,24},{30,26},{20,28... | collective-permute-start | bytes 1966088 | tf_op jit(solution)/shard_map/ppermute | solution.py:50
  304.4 17.2 %collective-permute-start.58 = (bf16[128,2560]{1,0:T(8,128)(2,1)}, bf16[128,2560]{1,0:T(8,128)(2,1)}, u32[]{:S(2)}, u32[]{:S(2)}) collective-permute-start(bf16[128,2560]{1,0:T(8,128)(2,1)} %pad_maximum_fusion.5), channel_id=1, source_target_pairs={{8,0},{10,2},{16,8},{18,10},{24,16},{26,18},{28,24},{30,26},{20,28... | collective-permute-start | bytes 1966088 | tf_op jit(solution)/shard_map/ppermute | solution.py:50
  360.9 18.0 %collective-permute-start.65 = (bf16[64,2560]{1,0:T(8,128)(2,1)}, bf16[64,2560]{1,0:T(8,128)(2,1)}, u32[]{:S(2)}, u32[]{:S(2)}) collective-permute-start(bf16[64,2560]{1,0:T(8,128)(2,1)} %get-tuple-element.590), channel_id=1, source_target_pairs={{0,8},{2,10},{8,16},{10,18},{16,24},{18,26},{24,28},{26,30},{28,20... | collective-permute-start | bytes 983048 | tf_op jit(solution)/shard_map/ppermute | solution.py:47
  361.0 21.4 %collective-permute-start.68 = (bf16[128,2560]{1,0:T(8,128)(2,1)}, bf16[128,2560]{1,0:T(8,128)(2,1)S(1)}, u32[]{:S(2)}, u32[]{:S(2)}) collective-permute-start(bf16[128,2560]{1,0:T(8,128)(2,1)} %get-tuple-element.606), channel_id=1, source_target_pairs={{0,1},{1,0},{2,3},{3,2},{4,5},{5,4},{6,7},{7,6},{8,9},{9,8},{10,11... | collective-permute-start | bytes 1966088 | tf_op jit(solution)/shard_map/ppermute | solution.py:238
  362.6 17.6 %collective-permute-start.64 = (bf16[64,2560]{1,0:T(8,128)(2,1)}, bf16[64,2560]{1,0:T(8,128)(2,1)S(1)}, u32[]{:S(2)}, u32[]{:S(2)}) collective-permute-start(bf16[64,2560]{1,0:T(8,128)(2,1)} %get-tuple-element.589), channel_id=1, source_target_pairs={{8,0},{10,2},{16,8},{18,10},{24,16},{26,18},{28,24},{30,26},{20,28... | collective-permute-start | bytes 983048 | tf_op jit(solution)/shard_map/ppermute | solution.py:50
  391.9 21.1 %collective-permute-start.74 = (f32[2,1280]{1,0:T(2,128)S(1)}, f32[2,1280]{1,0:T(2,128)S(1)}, u32[]{:S(2)}, u32[]{:S(2)}) collective-permute-start(f32[2,1280]{1,0:T(2,128)S(1)} %get-tuple-element.634), channel_id=1, source_target_pairs={{2,0},{4,2},{6,4},{8,6},{10,8},{12,10},{14,12},{16,14},{18,16},{20... | collective-permute-start | bytes 30728 | tf_op jit(solution)/shard_map/ppermute | solution.py:244
  393.4 17.6 %collective-permute-start.70 = (bf16[128,2560]{1,0:T(8,128)(2,1)S(1)}, bf16[128,2560]{1,0:T(8,128)(2,1)S(1)}, u32[]{:S(2)}, u32[]{:S(2)}) collective-permute-start(bf16[128,2560]{1,0:T(8,128)(2,1)S(1)} %add_convert_fusion.5), channel_id=1, source_target_pairs={{0,8},{2,10},{8,16},{10,18},{16,24},{18,26},{24,28},{26,30},{28,20... | collective-permute-start | bytes 1966088 | tf_op jit(solution)/shard_map/ppermute | solution.py:47
  394.3 17.7 %collective-permute-start.69 = (bf16[128,2560]{1,0:T(8,128)(2,1)S(1)}, bf16[128,2560]{1,0:T(8,128)(2,1)S(1)}, u32[]{:S(2)}, u32[]{:S(2)}) collective-permute-start(bf16[128,2560]{1,0:T(8,128)(2,1)S(1)} %add_convert_fusion.4), channel_id=1, source_target_pairs={{8,0},{10,2},{16,8},{18,10},{24,16},{26,18},{28,24},{30,26},{20,28... | collective-permute-start | bytes 1966088 | tf_op jit(solution)/shard_map/ppermute | solution.py:50
  417.5 19.0 %collective-permute-start.71 = (bf16[128,2560]{1,0:T(8,128)(2,1)}, bf16[128,2560]{1,0:T(8,128)(2,1)}, u32[]{:S(2)}, u32[]{:S(2)}) collective-permute-start(bf16[128,2560]{1,0:T(8,128)(2,1)} %add_convert_fusion.2), channel_id=1, source_target_pairs={{8,0},{10,2},{16,8},{18,10},{24,16},{26,18},{28,24},{30,26},{20,28... | collective-permute-start | bytes 1966088 | tf_op jit(solution)/shard_map/ppermute | solution.py:50
  419.7 18.3 %collective-permute-start.72 = (bf16[128,2560]{1,0:T(8,128)(2,1)}, bf16[128,2560]{1,0:T(8,128)(2,1)}, u32[]{:S(2)}, u32[]{:S(2)}) collective-permute-start(bf16[128,2560]{1,0:T(8,128)(2,1)} %add_convert_fusion.3), channel_id=1, source_target_pairs={{0,8},{2,10},{8,16},{10,18},{16,24},{18,26},{24,28},{26,30},{28,20... | collective-permute-start | bytes 1966088 | tf_op jit(solution)/shard_map/ppermute | solution.py:47
  449.3 36.9 %collective-permute-start.80 = (bf16[128,2560]{1,0:T(8,128)(2,1)}, bf16[128,2560]{1,0:T(8,128)(2,1)}, u32[]{:S(2)}, u32[]{:S(2)}) collective-permute-start(bf16[128,2560]{1,0:T(8,128)(2,1)} %get-tuple-element.857), channel_id=1, source_target_pairs={{0,1},{1,0},{2,3},{3,2},{4,5},{5,4},{6,7},{7,6},{8,9},{9,8},{10,11... | collective-permute-start | bytes 1966088 | tf_op jit(solution)/shard_map/ppermute | solution.py:238
  455.3 20.2 %collective-permute-start.83 = (bf16[160,2560]{1,0:T(8,128)(2,1)S(1)}, bf16[160,2560]{1,0:T(8,128)(2,1)S(1)}, u32[]{:S(2)}, u32[]{:S(2)}) collective-permute-start(bf16[160,2560]{1,0:T(8,128)(2,1)S(1)} %pad_maximum_fusion.2), channel_id=1, source_target_pairs={{0,8},{2,10},{8,16},{10,18},{16,24},{18,26},{24,28},{26,30},{28,20... | collective-permute-start | bytes 2457608 | tf_op jit(solution)/shard_map/ppermute | solution.py:47
  458.1 20.1 %collective-permute-start.82 = (bf16[160,2560]{1,0:T(8,128)(2,1)S(1)}, bf16[160,2560]{1,0:T(8,128)(2,1)S(1)}, u32[]{:S(2)}, u32[]{:S(2)}) collective-permute-start(bf16[160,2560]{1,0:T(8,128)(2,1)S(1)} %pad_maximum_fusion.3), channel_id=1, source_target_pairs={{8,0},{10,2},{16,8},{18,10},{24,16},{26,18},{28,24},{30,26},{20,28... | collective-permute-start | bytes 2457608 | tf_op jit(solution)/shard_map/ppermute | solution.py:50
  466.4 22.8 %collective-permute-start.87 = (bf16[8,96,2560]{2,1,0:T(8,128)(2,1)}, bf16[8,96,2560]{2,1,0:T(8,128)(2,1)}, u32[]{:S(2)}, u32[]{:S(2)}) collective-permute-start(bf16[8,96,2560]{2,1,0:T(8,128)(2,1)} %get-tuple-element.678), channel_id=1, source_target_pairs={{0,2},{2,0},{4,6},{6,4},{8,10},{10,8},{12,14},{14,12},{16,18},{18,... | collective-permute-start | bytes 11796488 | tf_op jit(solution)/shard_map/ppermute | solution.py:211
  484.0 21.4 %collective-permute-start.85 = (bf16[160,2560]{1,0:T(8,128)(2,1)}, bf16[160,2560]{1,0:T(8,128)(2,1)}, u32[]{:S(2)}, u32[]{:S(2)}) collective-permute-start(bf16[160,2560]{1,0:T(8,128)(2,1)} %fusion.10), channel_id=1, source_target_pairs={{8,0},{10,2},{16,8},{18,10},{24,16},{26,18},{28,24},{30,26},{20,28... | collective-permute-start | bytes 2457608 | tf_op jit(solution)/shard_map/ppermute | solution.py:50
  485.4 21.4 %collective-permute-start.86 = (bf16[160,2560]{1,0:T(8,128)(2,1)}, bf16[160,2560]{1,0:T(8,128)(2,1)}, u32[]{:S(2)}, u32[]{:S(2)}) collective-permute-start(bf16[160,2560]{1,0:T(8,128)(2,1)} %fusion.11), channel_id=1, source_target_pairs={{0,8},{2,10},{8,16},{10,18},{16,24},{18,26},{24,28},{26,30},{28,20... | collective-permute-start | bytes 2457608 | tf_op jit(solution)/shard_map/ppermute | solution.py:47
  490.6 21.4 %collective-permute-start.89 = (bf16[49,2560]{1,0:T(8,128)(2,1)S(1)}, bf16[49,2560]{1,0:T(8,128)(2,1)S(1)}, u32[]{:S(2)}, u32[]{:S(2)}) collective-permute-start(bf16[49,2560]{1,0:T(8,128)(2,1)S(1)} %pad_maximum_fusion.11), channel_id=1, source_target_pairs={{0,8},{2,10},{8,16},{10,18},{16,24},{18,26},{24,28},{26,30},{28,20... | collective-permute-start | bytes 752648 | tf_op jit(solution)/shard_map/ppermute | solution.py:47
  491.5 18.6 %collective-permute-start.88 = (bf16[48,2560]{1,0:T(8,128)(2,1)S(1)}, bf16[48,2560]{1,0:T(8,128)(2,1)S(1)}, u32[]{:S(2)}, u32[]{:S(2)}) collective-permute-start(bf16[48,2560]{1,0:T(8,128)(2,1)S(1)} %slice_bitcast_fusion.7), channel_id=1, source_target_pairs={{8,0},{10,2},{16,8},{18,10},{24,16},{26,18},{28,24},{30,26},{20,28... | collective-permute-start | bytes 737288 | tf_op jit(solution)/shard_map/ppermute | solution.py:50
  514.6 33.7 %collective-permute-start.91 = (bf16[160,2560]{1,0:T(8,128)(2,1)S(1)}, bf16[160,2560]{1,0:T(8,128)(2,1)S(1)}, u32[]{:S(2)}, u32[]{:S(2)}) collective-permute-start(bf16[160,2560]{1,0:T(8,128)(2,1)S(1)} %fusion.9), channel_id=1, source_target_pairs={{0,8},{2,10},{8,16},{10,18},{16,24},{18,26},{24,28},{26,30},{28,20... | collective-permute-start | bytes 2457608 | tf_op jit(solution)/shard_map/ppermute | solution.py:47
  517.7 30.6 %collective-permute-start.90 = (bf16[160,2560]{1,0:T(8,128)(2,1)S(1)}, bf16[160,2560]{1,0:T(8,128)(2,1)S(1)}, u32[]{:S(2)}, u32[]{:S(2)}) collective-permute-start(bf16[160,2560]{1,0:T(8,128)(2,1)S(1)} %fusion.8), channel_id=1, source_target_pairs={{8,0},{10,2},{16,8},{18,10},{24,16},{26,18},{28,24},{30,26},{20,28... | collective-permute-start | bytes 2457608 | tf_op jit(solution)/shard_map/ppermute | solution.py:50
  522.5 23.3 %collective-permute-start.93 = (bf16[97,2560]{1,0:T(8,128)(2,1)}, bf16[97,2560]{1,0:T(8,128)(2,1)}, u32[]{:S(2)}, u32[]{:S(2)}) collective-permute-start(bf16[97,2560]{1,0:T(8,128)(2,1)} %pad_maximum_fusion.10), channel_id=1, source_target_pairs={{0,8},{2,10},{8,16},{10,18},{16,24},{18,26},{24,28},{26,30},{28,20... | collective-permute-start | bytes 1489928 | tf_op jit(solution)/shard_map/ppermute | solution.py:47
  525.6 22.7 %collective-permute-start.92 = (bf16[97,2560]{1,0:T(8,128)(2,1)}, bf16[97,2560]{1,0:T(8,128)(2,1)}, u32[]{:S(2)}, u32[]{:S(2)}) collective-permute-start(bf16[97,2560]{1,0:T(8,128)(2,1)} %fusion.74), channel_id=1, source_target_pairs={{8,0},{10,2},{16,8},{18,10},{24,16},{26,18},{28,24},{30,26},{20,28... | collective-permute-start | bytes 1489928 | tf_op jit(solution)/shard_map/ppermute | solution.py:50
  (152 other events, 1332.3 us)
Sparse Core Ops, SparseCore 0:
  9.6 47.6 all-gather.3
  58.8 39.9 all-gather.5
  122.2 38.4 all-gather.7
  416.4 130.1 reduce-scatter.1

commit v5 on v4

--- a/solution.py
+++ b/solution.py
@@ -111,11 +111,22 @@
             self.theirs.append(landed[: len(swapped)])
 
     def next(self):
-        self.land()
-        landed = self.flight
-        self.pairs.append(landed)
-        self.send()
-        self.swap(*landed)
+        u, d = self.flight
+        swapped = self.theirs.pop() if self.theirs and not self.settled else ()
+        self.settled = False
+        if swapped:
+            *swapped, u = self.order.arrive(*swapped, u)
+            self.theirs.append(tuple(swapped))
+        else:
+            u = self.order.arrive(u)
+        self.steps += 1
+        final = self.steps == self.ring.reach
+        up = self.ring.up(u[: self.half] if final else u)
+        d = self.order.arrive(d)
+        down = self.ring.down(d[self.half :] if final else d)
+        self.pairs.append((u, d))
+        self.flight = (up, down)
+        self.swap(u, d)
 
     def settle(self):
         swapped = self.order.arrive(*self.theirs.pop())

time: 601 us -> 597 us (level)
  transfers between devices with their start and end apart: 102 -> 102, of which waited for: 44 -> 38; matrix products, arithmetic and copies ran while one was open for 24% -> 25% of each run, Pallas kernels for 20% -> 20%
where the time goes in v5:
time: 597 us; the launch traced here: 587 us
  waiting for transfers between devices  174 us (29%)
  Pallas kernels  118 us (20%)
  starting transfers between devices  95.9 us (16%)
  other arithmetic  68.6 us (11%)
  matrix products  58.4 us (10%)
  local copies, waits for them, and re-layouts  55.9 us (9%)
  between operations  16.6 us (3%)
    ppermute x32, waiting for transfers between devices, up(): return lax.ppermute(value, 'dp', self.up_route)  114 us
    ppermute x32, waiting for transfers between devices, down(): return lax.ppermute(value, 'dp', self.down_route)  41.7 us
    ppermute x32, starting transfers between devices, down(): return lax.ppermute(value, 'dp', self.down_route)  38.5 us
    dot_general x14, matrix products, cols_inner(): lax.dot_general(left, right, (((1,), (1,)), ((), ())), preferred_element_...  34.2 us
    ppermute x32, starting transfers between devices, up(): return lax.ppermute(value, 'dp', self.up_route)  30.7 us
    pallas_call x3, Pallas kernels, hidden_grad(): pl.pallas_call(functools.partial(hidden_grad_body, heights, right_heights...  29.6 us
    unnamed x210, local copies, waits for them, and re-layouts  26.2 us
    convert_element_type x24, other arithmetic, __call__(): return total.astype(dtype)  22.6 us
  transfers between devices with their start and end apart: 102, of which 38 were waited for; matrix products, arithmetic and copies ran while one was open for 25% of the time, Pallas kernels for 20%

profile of v5, /device:TPU:0, one launch (start us, length us, event | category | flops | bytes accessed | tf_op | source)
XLA Modules:
  0.0 587.4 jit_solution(210955410352855876)
XLA Ops:
  9.9 2.6 collective-permute-start.1
  16.5 11.1 %collective-permute-done.3.refs_2_ = bf16[112,2560]{1,0:T(8,128)(2,1)} collective-permute-done((bf16[112,2560]{1,0:T(8,128)(2,1)S(1)}, bf16[112,2560]{1,0:T(8,128)(2,1)}, u32[]{:S(2)}, u32[]{:S(2)}) %collective-permute-start.3) | collective-permute-done | bytes 573472 | tf_op jit(solution)/shard_map/ppermute | solution.py:47
  32.4 4.8 collective-permute-done
  37.2 6.2 %collective-permute-done.7.refs_6_ = bf16[112,2560]{1,0:T(8,128)(2,1)} collective-permute-done((bf16[112,2560]{1,0:T(8,128)(2,1)}, bf16[112,2560]{1,0:T(8,128)(2,1)}, u32[]{:S(2)}, u32[]{:S(2)}) %collective-permute-start.7) | collective-permute-done | bytes 573472 | tf_op jit(solution)/shard_map/ppermute | solution.py:47
  47.9 13.1 %collective-permute-done.11.refs_10_ = bf16[112,2560]{1,0:T(8,128)(2,1)} collective-permute-done((bf16[112,2560]{1,0:T(8,128)(2,1)}, bf16[112,2560]{1,0:T(8,128)(2,1)}, u32[]{:S(2)}, u32[]{:S(2)}) %collective-permute-start.11) | collective-permute-done | bytes 573472 | tf_op jit(solution)/shard_map/ppermute | solution.py:47
  69.5 3.5 collective-permute-done.15.refs_14_
  75.6 2.6 pad_maximum_fusion
  80.6 7.4 %shard_map.254 = (bf16[1280,2560]{1,0:T(8,128)(2,1)}, bf16[256,2560]{1,0:T(8,128)(2,1)}, bf16[256,2560]{1,0:T(8,128)(2,1)}) custom-call(s32[16]{0:T(128)S(1)} %stack.178.at_ref, bf16[112,2560]{1,0:T(8,128)(2,1)S(1)} %pad_maximum_fusion.9.refs_0_, bf16[112,2560]{1,0:T(8,128)(2,1)S(1)} %collective-permute-done.2.refs_1_, ...), custom_call_target="tpu_custom_call" | custom-call | tf_op jit(solution)/shard_map/pallas_call | solution.py:672
  92.8 6.4 %collective-permute-done.20.refs_2_ = bf16[160,2560]{1,0:T(8,128)(2,1)} collective-permute-done((bf16[160,2560]{1,0:T(8,128)(2,1)S(1)}, bf16[160,2560]{1,0:T(8,128)(2,1)}, u32[]{:S(2)}, u32[]{:S(2)}) %collective-permute-start.20) | collective-permute-done | bytes 819232 | tf_op jit(solution)/shard_map/ppermute | solution.py:47
  102.8 6.2 %convolution_convert_fusion.1.pad_ref.refs_7_ = bf16[272,1280]{1,0:T(8,128)(2,1)} fusion(bf16[272,2560]{1,0:T(8,128)(2,1)} %fusion.6, bf16[1280,2560]{1,0:T(8,128)(2,1)} %get-tuple-element.634), kind=kOutput, calls=%fused_computation.16 | convolution fusion | flops 1782927360 | bytes 8642560 | tf_op jit(solution)/shard_map/dot_general | solution.py:314
  110.2 6.6 %shard_map.255 = (bf16[256,1280]{1,0:T(8,128)(2,1)S(1)}, f32[256,1280]{1,0:T(8,128)S(1)}, f32[256,1280]{1,0:T(8,128)S(1)}, f32[256,1280]{1,0:T(8,128)S(1)}, f32[2,1280]{1,0:T(2,128)S(1)}) custom-call(bf16[272,1280]{1,0:T(8,128)(2,1)S(1)} %copy-done.28, f32[256,8]{1,0:T(8,128)S(1)} %copy.141.marks_ref, ...), custom_call_target="tpu_custom_call" | custom-call | tf_op jit(solution)/shard_map/pallas_call | solution.py:499
  126.6 3.5 collective-permute-start.31
  130.2 3.1 collective-permute-start.30
  133.3 11.8 %collective-permute-done.31 = f32[2,1280]{1,0:T(2,128)S(1)} collective-permute-done((f32[2,1280]{1,0:T(2,128)S(1)}, f32[2,1280]{1,0:T(2,128)S(1)}, u32[]{:S(2)}, u32[]{:S(2)}) %collective-permute-start.31) | collective-permute-done | bytes 10272 | tf_op jit(solution)/shard_map/ppermute | solution.py:255
  152.1 9.3 %shard_map.256 = (bf16[1280,2560]{1,0:T(8,128)(2,1)}, bf16[1280,2560]{1,0:T(8,128)(2,1)}) custom-call(s32[14]{0:T(128)S(1)} %stack.190.at_ref, bf16[160,2560]{1,0:T(8,128)(2,1)S(1)} %constant_dynamic-update-slice_fusion.refs_0_, bf16[160,2560]{1,0:T(8,128)(2,1)S(1)} %collective-permute-done.19.refs_1_, bf16[160,2560]{1,0:T(8,128)(2,1)} %collective-permute-done.20.refs_2_, ...), custom_call_target="tpu_custom_call" | custom-call | tf_op jit(solution)/shard_map/pallas_call | solution.py:672
  168.6 2.9 shard_map.257
  171.6 4.9 fusion.131.pre_ref
  180.1 3.3 collective-permute-done.40
  190.5 10.2 %collective-permute-done.43 = bf16[128,2560]{1,0:T(8,128)(2,1)} collective-permute-done((bf16[128,2560]{1,0:T(8,128)(2,1)}, bf16[128,2560]{1,0:T(8,128)(2,1)}, u32[]{:S(2)}, u32[]{:S(2)}) %collective-permute-start.43) | collective-permute-done | bytes 655392 | tf_op jit(solution)/shard_map/ppermute | solution.py:47
  209.4 11.9 %shard_map.258 = (bf16[128,960]{1,0:T(8,128)(2,1)S(1)}, bf16[128,960]{1,0:T(8,128)(2,1)S(1)}, bf16[128,960]{1,0:T(8,128)(2,1)S(1)}, bf16[128,2560]{1,0:T(8,128)(2,1)S(1)}) custom-call(bf16[128,2560]{1,0:T(8,128)(2,1)S(1)} %multiply_convert_fusion.refs_0_.refs_5_, bf16[128,2560]{1,0:T(8,128)(2,1)S(1)} %copy-done.2, ...), custom_call_target="tpu_custom_call" | custom-call | tf_op jit(solution)/shard_map/pallas_call | solution.py:908
  223.3 6.3 %collective-permute-done.44 = bf16[128,2560]{1,0:T(8,128)(2,1)} collective-permute-done((bf16[128,2560]{1,0:T(8,128)(2,1)S(1)}, bf16[128,2560]{1,0:T(8,128)(2,1)}, u32[]{:S(2)}, u32[]{:S(2)}) %collective-permute-start.44) | collective-permute-done | bytes 655392 | tf_op jit(solution)/shard_map/ppermute | solution.py:47
  242.4 3.4 multiply_convert_fusion.5
  250.4 5.8 collective-permute-done.49
  259.9 3.4 multiply_convert_fusion.3
  289.5 8.5 %collective-permute-done.57 = bf16[64,2560]{1,0:T(8,128)(2,1)S(1)} collective-permute-done((bf16[64,2560]{1,0:T(8,128)(2,1)S(1)}, bf16[64,2560]{1,0:T(8,128)(2,1)S(1)}, u32[]{:S(2)}, u32[]{:S(2)}) %collective-permute-start.57) | collective-permute-done | bytes 327712 | tf_op jit(solution)/shard_map/ppermute | solution.py:47
  302.0 9.7 %shard_map.259 = (bf16[128,2560]{1,0:T(8,128)(2,1)S(1)}, bf16[256,2560]{1,0:T(8,128)(2,1)S(1)}, bf16[256,2560]{1,0:T(8,128)(2,1)S(1)}, bf16[256,2560]{1,0:T(8,128)(2,1)}, bf16[128,2560]{1,0:T(8,128)(2,1)S(1)}) custom-call(bf16[128,960]{1,0:T(8,128)(2,1)S(1)} %get-tuple-element.543.refs_0_, bf16[256,960]{1,0:T(8,128)(2,1)S(1)} %get-tuple-element.544.refs_1_, ...), custom_call_target="tpu_custom_call" | custom-call | tf_op jit(solution)/shard_map/pallas_call | solution.py:973
  311.7 3.1 collective-permute-done.59
  321.7 9.8 %shard_map.260.refs_10_ = bf16[4,3,240,2560]{3,2,1,0:T(8,128)(2,1)} custom-call(bf16[128,960]{1,0:T(8,128)(2,1)S(1)} %get-tuple-element.511.refs_0_, bf16[256,960]{1,0:T(8,128)(2,1)S(1)} %copy-done.37, bf16[256,960]{1,0:T(8,128)(2,1)S(1)} %copy-done.39, bf16[256,960]{1,0:T(8,128)(2,1)S(1)} %copy-done.41, bf16[128,960]{1,0:T(8,128)(2,1)S(1)} %get-tuple-element.515.refs_4_, ...), custom_call_target="tpu_custom_call" | custom-call | tf_op jit(solution)/shard_map/pallas_call | solution.py:837
  333.8 3.9 collective-permute-done.60
  341.1 9.7 %shard_map.261.refs_10_ = bf16[4,3,240,2560]{3,2,1,0:T(8,128)(2,1)} custom-call(bf16[128,960]{1,0:T(8,128)(2,1)S(1)} %get-tuple-element.525.refs_0_, bf16[256,960]{1,0:T(8,128)(2,1)S(1)} %get-tuple-element.526.refs_1_, bf16[256,960]{1,0:T(8,128)(2,1)S(1)} %get-tuple-element.527.refs_2_, ...), custom_call_target="tpu_custom_call", output_to_operand_aliasing={{}: (10, {})} | custom-call | tf_op jit(solution)/shard_map/pallas_call | solution.py:837
  364.8 10.2 %shard_map.262 = bf16[4,3,240,2560]{3,2,1,0:T(8,128)(2,1)} custom-call(bf16[128,960]{1,0:T(8,128)(2,1)S(1)} %get-tuple-element.543.refs_0_, bf16[256,960]{1,0:T(8,128)(2,1)S(1)} %copy-done.14, bf16[256,960]{1,0:T(8,128)(2,1)S(1)} %copy-done.16, bf16[256,960]{1,0:T(8,128)(2,1)S(1)} %copy-done.18, ...), custom_call_target="tpu_custom_call", output_to_operand_aliasing={{}: (10, {})} | custom-call | tf_op jit(solution)/shard_map/pallas_call | solution.py:837
  379.9 8.1 %shard_map.263 = (bf16[256,1280]{1,0:T(8,128)(2,1)S(1)}, f32[256,1280]{1,0:T(8,128)S(1)}, f32[256,1280]{1,0:T(8,128)S(1)}, f32[2,1280]{1,0:T(2,128)S(1)}) custom-call(bf16[256,2560]{1,0:T(8,128)(2,1)S(1)} %pad_maximum_fusion.1.dz_ref.refs_3_, bf16[1280,2560]{1,0:T(8,128)(2,1)} %get-tuple-element.561.wide_ref, f32[256,1280]{1,0:T(8,128)S(1)} %copy-done.8, ...), custom_call_target="tpu_custom_call" | custom-call | tf_op jit(solution)/shard_map/pallas_call | solution.py:531
  392.0 10.7 %shard_map.264 = (bf16[8,160,2560]{2,1,0:T(8,128)(2,1)}, bf16[8,160,2560]{2,1,0:T(8,128)(2,1)}) custom-call(s32[9]{0:T(128)S(1)} %stack.200.at_ref, bf16[256,1280]{1,0:T(8,128)(2,1)S(1)} %get-tuple-element.631.refs_0_, bf16[256,1280]{1,0:T(8,128)(2,1)S(1)} %fusion.26.refs_1_, bf16[256,2560]{1,0:T(8,128)(2,1)S(1)} %slice.554.refs_2_.refs_1_, ...), custom_call_target="tpu_custom_call" | custom-call | tf_op jit(solution)/shard_map/pallas_call | solution.py:755
  402.7 4.4 collective-permute-done.70
  419.4 8.3 %shard_map.265 = (bf16[256,1280]{1,0:T(8,128)(2,1)S(1)}, f32[8,1280]{1,0:T(8,128)S(1)}, f32[8,1280]{1,0:T(8,128)S(1)}, f32[8,1280]{1,0:T(8,128)S(1)}, bf16[256,2560]{1,0:T(8,128)(2,1)S(1)}) custom-call(f32[256,1280]{1,0:T(8,128)S(1)} %copy-done.47, f32[256,1280]{1,0:T(8,128)} %copy-done.48, f32[1,1280]{1,0:T(1,128)S(1)} %slice_add_fusion.refs_2_, ...), custom_call_target="tpu_custom_call" | custom-call | flops 499999997952 | tf_op jit(solution)/shard_map/pallas_call | solution.py:568
  434.4 2.8 add_convert_fusion.1
  439.4 4.3 fusion.94
  446.2 3.5 collective-permute-done.79
  456.1 7.1 %shard_map.266 = (bf16[8,96,2560]{2,1,0:T(8,128)(2,1)}, bf16[8,96,2560]{2,1,0:T(8,128)(2,1)}) custom-call(s32[9]{0:T(128)S(1)} %copy-done.45, bf16[256,1280]{1,0:T(8,128)(2,1)S(1)} %fusion.107.refs_0_, bf16[256,2560]{1,0:T(8,128)(2,1)S(1)} %slice.554.refs_2_.refs_1_, bf16[256,2560]{1,0:T(8,128)(2,1)S(1)} %get-tuple-element.628.refs_2_), custom_call_target="tpu_custom_call" | custom-call | tf_op jit(solution)/shard_map/pallas_call | solution.py:755
  464.4 4.0 convolution_add_fusion.4.mine_ref
  471.9 2.8 fusion.11
  474.8 2.6 fusion.10
  482.8 3.0 shard_map.267
  489.3 12.8 %collective-permute-done.85 = bf16[160,2560]{1,0:T(8,128)(2,1)} collective-permute-done((bf16[160,2560]{1,0:T(8,128)(2,1)}, bf16[160,2560]{1,0:T(8,128)(2,1)}, u32[]{:S(2)}, u32[]{:S(2)}) %collective-permute-start.85) | collective-permute-done | bytes 819232 | tf_op jit(solution)/shard_map/ppermute | solution.py:50
  503.8 2.9 collective-permute-done.88
  523.9 19.0 %collective-permute-done.93 = bf16[97,2560]{1,0:T(8,128)(2,1)} collective-permute-done((bf16[97,2560]{1,0:T(8,128)(2,1)}, bf16[97,2560]{1,0:T(8,128)(2,1)}, u32[]{:S(2)}, u32[]{:S(2)}) %collective-permute-start.93) | collective-permute-done | bytes 496672 | tf_op jit(solution)/shard_map/ppermute | solution.py:47
  553.8 5.7 collective-permute-done.95
  568.5 3.6 shard_map.268
  (593 shorter events, 260.0 us)
Async XLA Ops:
  7.2 202.2 %all-gather.4.cloned.1.call-start = ((), (), s32[]{:S(2)}) async-start(), calls=%async_computation.1 | async-start | bytes 6144000 | tf_op jit(solution)/shard_map/all_gather | solution.py:233
  7.9 201.4 %all-gather.6.cloned.1.call-start = ((), (), s32[]{:S(2)}) async-start(), calls=%async_computation.2 | async-start | bytes 6144000 | tf_op jit(solution)/shard_map/all_gather | solution.py:233
  8.7 200.7 %all-gather.8.cloned.1.call-start = ((), (), s32[]{:S(2)}) async-start(), calls=%async_computation.3 | async-start | bytes 6144000 | tf_op jit(solution)/shard_map/all_gather | solution.py:233
  9.3 18.3 %collective-permute-start.2 = (bf16[112,2560]{1,0:T(8,128)(2,1)S(1)}, bf16[112,2560]{1,0:T(8,128)(2,1)S(1)}, u32[]{:S(2)}, u32[]{:S(2)}) collective-permute-start(bf16[112,2560]{1,0:T(8,128)(2,1)S(1)} %pad_maximum_fusion.9.refs_0_), channel_id=1, source_target_pairs={{0,2},{2,0},{4,6},{6,4},{8,10},{10,8},{12,14},{14,12},{16,18},{18,... | collective-permute-start | bytes 1720328 | tf_op jit(solution)/shard_map/ppermute | solution.py:222
  9.9 17.7 %collective-permute-start.1 = (bf16[112,2560]{1,0:T(8,128)(2,1)S(1)}, bf16[112,2560]{1,0:T(8,128)(2,1)S(1)}, u32[]{:S(2)}, u32[]{:S(2)}) collective-permute-start(bf16[112,2560]{1,0:T(8,128)(2,1)S(1)} %pad_maximum_fusion.9.refs_0_), channel_id=1, source_target_pairs={{8,0},{10,2},{16,8},{18,10},{24,16},{26,18},{28,24},{30,26},{20,28... | collective-permute-start | bytes 1720328 | tf_op jit(solution)/shard_map/ppermute | solution.py:50
  12.6 24.6 %collective-permute-start = (bf16[128,2560]{1,0:T(8,128)(2,1)S(1)}, bf16[128,2560]{1,0:T(8,128)(2,1)}, u32[]{:S(2)}, u32[]{:S(2)}) collective-permute-start(bf16[128,2560]{1,0:T(8,128)(2,1)S(1)} %copy-done), channel_id=1, source_target_pairs={{0,1},{1,0},{2,3},{3,2},{4,5},{5,4},{6,7},{7,6},{8,9},{9,8},{10,11... | collective-permute-start | bytes 1966088 | tf_op jit(solution)/shard_map/ppermute | solution.py:249
  43.6 19.2 %collective-permute-start.13 = (bf16[112,2560]{1,0:T(8,128)(2,1)}, bf16[112,2560]{1,0:T(8,128)(2,1)}, u32[]{:S(2)}, u32[]{:S(2)}) collective-permute-start(bf16[112,2560]{1,0:T(8,128)(2,1)} %collective-permute-done.9.refs_8_), channel_id=1, source_target_pairs={{8,0},{10,2},{16,8},{18,10},{24,16},{26,18},{28,24},{30,26},{20,28... | collective-permute-start | bytes 1720328 | tf_op jit(solution)/shard_map/ppermute | solution.py:50
  73.0 19.9 %collective-permute-start.19 = (bf16[160,2560]{1,0:T(8,128)(2,1)S(1)}, bf16[160,2560]{1,0:T(8,128)(2,1)S(1)}, u32[]{:S(2)}, u32[]{:S(2)}) collective-permute-start(bf16[160,2560]{1,0:T(8,128)(2,1)S(1)} %constant_dynamic-update-slice_fusion.refs_0_), channel_id=1, source_target_pairs={{0,2},{2,0},{4,6},{6,4},{8,10},{10,8},{12,14},{14,12},{16,18},{18,... | collective-permute-start | bytes 2457608 | tf_op jit(solution)/shard_map/ppermute | solution.py:222
  78.1 21.1 %collective-permute-start.20 = (bf16[160,2560]{1,0:T(8,128)(2,1)S(1)}, bf16[160,2560]{1,0:T(8,128)(2,1)}, u32[]{:S(2)}, u32[]{:S(2)}) collective-permute-start(bf16[160,2560]{1,0:T(8,128)(2,1)S(1)} %constant_dynamic-update-slice_fusion.refs_0_), channel_id=1, source_target_pairs={{0,8},{2,10},{8,16},{10,18},{16,24},{18,26},{24,28},{26,30},{28,20... | collective-permute-start | bytes 2457608 | tf_op jit(solution)/shard_map/ppermute | solution.py:47
  80.6 19.2 %collective-permute-start.22 = (bf16[160,2560]{1,0:T(8,128)(2,1)S(1)}, bf16[160,2560]{1,0:T(8,128)(2,1)}, u32[]{:S(2)}, u32[]{:S(2)}) collective-permute-start(bf16[160,2560]{1,0:T(8,128)(2,1)S(1)} %constant_dynamic-update-slice_fusion.refs_0_), channel_id=1, source_target_pairs={{8,0},{10,2},{16,8},{18,10},{24,16},{26,18},{28,24},{30,26},{20,28... | collective-permute-start | bytes 2457608 | tf_op jit(solution)/shard_map/ppermute | solution.py:50
  99.8 22.1 %collective-permute-start.28 = (bf16[160,2560]{1,0:T(8,128)(2,1)}, bf16[160,2560]{1,0:T(8,128)(2,1)}, u32[]{:S(2)}, u32[]{:S(2)}) collective-permute-start(bf16[160,2560]{1,0:T(8,128)(2,1)} %collective-permute-done.22.refs_4_), channel_id=1, source_target_pairs={{8,0},{10,2},{16,8},{18,10},{24,16},{26,18},{28,24},{30,26},{20,28... | collective-permute-start | bytes 2457608 | tf_op jit(solution)/shard_map/ppermute | solution.py:50
  101.0 19.9 %collective-permute-start.23 = (bf16[160,2560]{1,0:T(8,128)(2,1)}, bf16[160,2560]{1,0:T(8,128)(2,1)}, u32[]{:S(2)}, u32[]{:S(2)}) collective-permute-start(bf16[160,2560]{1,0:T(8,128)(2,1)} %collective-permute-done.22.refs_4_), channel_id=1, source_target_pairs={{0,2},{2,0},{4,6},{6,4},{8,10},{10,8},{12,14},{14,12},{16,18},{18,... | collective-permute-start | bytes 2457608 | tf_op jit(solution)/shard_map/ppermute | solution.py:222
  101.0 21.0 %collective-permute-start.24 = (bf16[160,2560]{1,0:T(8,128)(2,1)}, bf16[160,2560]{1,0:T(8,128)(2,1)}, u32[]{:S(2)}, u32[]{:S(2)}) collective-permute-start(bf16[160,2560]{1,0:T(8,128)(2,1)} %collective-permute-done.20.refs_2_), channel_id=1, source_target_pairs={{0,8},{2,10},{8,16},{10,18},{16,24},{18,26},{24,28},{26,30},{28,20... | collective-permute-start | bytes 2457608 | tf_op jit(solution)/shard_map/ppermute | solution.py:47
  101.9 20.1 %collective-permute-start.21 = (bf16[160,2560]{1,0:T(8,128)(2,1)}, bf16[160,2560]{1,0:T(8,128)(2,1)}, u32[]{:S(2)}, u32[]{:S(2)}) collective-permute-start(bf16[160,2560]{1,0:T(8,128)(2,1)} %collective-permute-done.20.refs_2_), channel_id=1, source_target_pairs={{0,2},{2,0},{4,6},{6,4},{8,10},{10,8},{12,14},{14,12},{16,18},{18,... | collective-permute-start | bytes 2457608 | tf_op jit(solution)/shard_map/ppermute | solution.py:222
  122.5 444.0 %reduce-scatter.2.cloned.1.call-start = ((), (), s32[]{:S(2)}) async-start(), calls=%async_computation.4 | async-start | bytes 18432000 | tf_op jit(solution)/shard_map/reduce_scatter | solution.py:239
  124.5 22.8 %collective-permute-start.33 = (bf16[160,2560]{1,0:T(8,128)(2,1)}, bf16[160,2560]{1,0:T(8,128)(2,1)}, u32[]{:S(2)}, u32[]{:S(2)}) collective-permute-start(bf16[160,2560]{1,0:T(8,128)(2,1)} %collective-permute-done.28.refs_8_), channel_id=1, source_target_pairs={{8,0},{10,2},{16,8},{18,10},{24,16},{26,18},{28,24},{30,26},{20,28... | collective-permute-start | bytes 2457608 | tf_op jit(solution)/shard_map/ppermute | solution.py:50
  126.3 21.0 %collective-permute-start.25 = (bf16[160,2560]{1,0:T(8,128)(2,1)}, bf16[160,2560]{1,0:T(8,128)(2,1)}, u32[]{:S(2)}, u32[]{:S(2)}) collective-permute-start(bf16[160,2560]{1,0:T(8,128)(2,1)} %collective-permute-done.24.refs_6_), channel_id=1, source_target_pairs={{0,8},{2,10},{8,16},{10,18},{16,24},{18,26},{24,28},{26,30},{28,20... | collective-permute-start | bytes 2457608 | tf_op jit(solution)/shard_map/ppermute | solution.py:47
  126.6 18.4 %collective-permute-start.31 = (f32[2,1280]{1,0:T(2,128)S(1)}, f32[2,1280]{1,0:T(2,128)S(1)}, u32[]{:S(2)}, u32[]{:S(2)}) collective-permute-start(f32[2,1280]{1,0:T(2,128)S(1)} %pad_maximum_fusion.14), channel_id=1, source_target_pairs={{0,6},{2,8},{4,10},{6,12},{8,14},{10,16},{12,18},{14,20},{16,22},{... | collective-permute-start | bytes 30728 | tf_op jit(solution)/shard_map/ppermute | solution.py:255
  178.6 24.2 %collective-permute-start.41 = (bf16[128,2560]{1,0:T(8,128)(2,1)S(1)}, bf16[128,2560]{1,0:T(8,128)(2,1)S(1)}, u32[]{:S(2)}, u32[]{:S(2)}) collective-permute-start(bf16[128,2560]{1,0:T(8,128)(2,1)S(1)} %convolution_convert_fusion), channel_id=1, source_target_pairs={{0,1},{1,0},{2,3},{3,2},{4,5},{5,4},{6,7},{7,6},{8,9},{9,8},{10,11... | collective-permute-start | bytes 1966088 | tf_op jit(solution)/shard_map/ppermute | solution.py:249
  183.5 17.6 %collective-permute-start.42 = (bf16[128,2560]{1,0:T(8,128)(2,1)}, bf16[128,2560]{1,0:T(8,128)(2,1)}, u32[]{:S(2)}, u32[]{:S(2)}) collective-permute-start(bf16[128,2560]{1,0:T(8,128)(2,1)} %collective-permute-done.39), channel_id=1, source_target_pairs={{8,0},{10,2},{16,8},{18,10},{24,16},{26,18},{28,24},{30,26},{20,28... | collective-permute-start | bytes 1966088 | tf_op jit(solution)/shard_map/ppermute | solution.py:50
  200.7 20.6 %collective-permute-start.46 = (bf16[128,2560]{1,0:T(8,128)(2,1)}, bf16[128,2560]{1,0:T(8,128)(2,1)}, u32[]{:S(2)}, u32[]{:S(2)}) collective-permute-start(bf16[128,2560]{1,0:T(8,128)(2,1)} %collective-permute-done.43), channel_id=1, source_target_pairs={{0,8},{2,10},{8,16},{10,18},{16,24},{18,26},{24,28},{26,30},{28,20... | collective-permute-start | bytes 1966088 | tf_op jit(solution)/shard_map/ppermute | solution.py:47
  201.0 21.3 %collective-permute-start.45 = (bf16[128,2560]{1,0:T(8,128)(2,1)}, bf16[128,2560]{1,0:T(8,128)(2,1)}, u32[]{:S(2)}, u32[]{:S(2)}) collective-permute-start(bf16[128,2560]{1,0:T(8,128)(2,1)} %collective-permute-done.42), channel_id=1, source_target_pairs={{8,0},{10,2},{16,8},{18,10},{24,16},{26,18},{28,24},{30,26},{20,28... | collective-permute-start | bytes 1966088 | tf_op jit(solution)/shard_map/ppermute | solution.py:50
  203.3 26.3 %collective-permute-start.44 = (bf16[128,2560]{1,0:T(8,128)(2,1)S(1)}, bf16[128,2560]{1,0:T(8,128)(2,1)}, u32[]{:S(2)}, u32[]{:S(2)}) collective-permute-start(bf16[128,2560]{1,0:T(8,128)(2,1)S(1)} %multiply_convert_fusion.refs_0_.refs_5_), channel_id=1, source_target_pairs={{0,8},{2,10},{8,16},{10,18},{16,24},{18,26},{24,28},{26,30},{28,20... | collective-permute-start | bytes 1966088 | tf_op jit(solution)/shard_map/ppermute | solution.py:47
  203.7 29.0 %collective-permute-start.47 = (bf16[128,2560]{1,0:T(8,128)(2,1)S(1)}, bf16[128,2560]{1,0:T(8,128)(2,1)}, u32[]{:S(2)}, u32[]{:S(2)}) collective-permute-start(bf16[128,2560]{1,0:T(8,128)(2,1)S(1)} %multiply_convert_fusion.refs_0_.refs_5_), channel_id=1, source_target_pairs={{8,0},{10,2},{16,8},{18,10},{24,16},{26,18},{28,24},{30,26},{20,28... | collective-permute-start | bytes 1966088 | tf_op jit(solution)/shard_map/ppermute | solution.py:50
  229.6 20.4 %collective-permute-start.48 = (bf16[128,2560]{1,0:T(8,128)(2,1)}, bf16[128,2560]{1,0:T(8,128)(2,1)S(1)}, u32[]{:S(2)}, u32[]{:S(2)}) collective-permute-start(bf16[128,2560]{1,0:T(8,128)(2,1)} %collective-permute-done.44), channel_id=1, source_target_pairs={{0,8},{2,10},{8,16},{10,18},{16,24},{18,26},{24,28},{26,30},{28,20... | collective-permute-start | bytes 1966088 | tf_op jit(solution)/shard_map/ppermute | solution.py:47
  232.7 24.0 %collective-permute-start.50 = (bf16[64,2560]{1,0:T(8,128)(2,1)S(1)}, bf16[64,2560]{1,0:T(8,128)(2,1)S(1)}, u32[]{:S(2)}, u32[]{:S(2)}) collective-permute-start(bf16[64,2560]{1,0:T(8,128)(2,1)S(1)} %slice.452), channel_id=1, source_target_pairs={{0,8},{2,10},{8,16},{10,18},{16,24},{18,26},{24,28},{26,30},{28,20... | collective-permute-start | bytes 983048 | tf_op jit(solution)/shard_map/ppermute | solution.py:47
  234.3 22.4 %collective-permute-start.51 = (bf16[64,2560]{1,0:T(8,128)(2,1)S(1)}, bf16[64,2560]{1,0:T(8,128)(2,1)S(1)}, u32[]{:S(2)}, u32[]{:S(2)}) collective-permute-start(bf16[64,2560]{1,0:T(8,128)(2,1)S(1)} %slice.453), channel_id=1, source_target_pairs={{8,0},{10,2},{16,8},{18,10},{24,16},{26,18},{28,24},{30,26},{20,28... | collective-permute-start | bytes 983048 | tf_op jit(solution)/shard_map/ppermute | solution.py:50
  235.9 20.3 %collective-permute-start.49 = (bf16[128,2560]{1,0:T(8,128)(2,1)}, bf16[128,2560]{1,0:T(8,128)(2,1)S(1)}, u32[]{:S(2)}, u32[]{:S(2)}) collective-permute-start(bf16[128,2560]{1,0:T(8,128)(2,1)} %collective-permute-done.47), channel_id=1, source_target_pairs={{8,0},{10,2},{16,8},{18,10},{24,16},{26,18},{28,24},{30,26},{20,28... | collective-permute-start | bytes 1966088 | tf_op jit(solution)/shard_map/ppermute | solution.py:50
  250.1 17.6 %collective-permute-start.52 = (bf16[128,2560]{1,0:T(8,128)(2,1)S(1)}, bf16[128,2560]{1,0:T(8,128)(2,1)S(1)}, u32[]{:S(2)}, u32[]{:S(2)}) collective-permute-start(bf16[128,2560]{1,0:T(8,128)(2,1)S(1)} %collective-permute-done.48), channel_id=1, source_target_pairs={{0,8},{2,10},{8,16},{10,18},{16,24},{18,26},{24,28},{26,30},{28,20... | collective-permute-start | bytes 1966088 | tf_op jit(solution)/shard_map/ppermute | solution.py:47
  357.0 18.0 %collective-permute-start.65 = (bf16[64,2560]{1,0:T(8,128)(2,1)}, bf16[64,2560]{1,0:T(8,128)(2,1)}, u32[]{:S(2)}, u32[]{:S(2)}) collective-permute-start(bf16[64,2560]{1,0:T(8,128)(2,1)} %get-tuple-element.542), channel_id=1, source_target_pairs={{0,8},{2,10},{8,16},{10,18},{16,24},{18,26},{24,28},{26,30},{28,20... | collective-permute-start | bytes 983048 | tf_op jit(solution)/shard_map/ppermute | solution.py:47
  358.5 20.0 %collective-permute-start.68 = (bf16[128,2560]{1,0:T(8,128)(2,1)}, bf16[128,2560]{1,0:T(8,128)(2,1)S(1)}, u32[]{:S(2)}, u32[]{:S(2)}) collective-permute-start(bf16[128,2560]{1,0:T(8,128)(2,1)} %get-tuple-element.558), channel_id=1, source_target_pairs={{0,1},{1,0},{2,3},{3,2},{4,5},{5,4},{6,7},{7,6},{8,9},{9,8},{10,11... | collective-permute-start | bytes 1966088 | tf_op jit(solution)/shard_map/ppermute | solution.py:249
  360.1 17.6 %collective-permute-start.64 = (bf16[64,2560]{1,0:T(8,128)(2,1)}, bf16[64,2560]{1,0:T(8,128)(2,1)S(1)}, u32[]{:S(2)}, u32[]{:S(2)}) collective-permute-start(bf16[64,2560]{1,0:T(8,128)(2,1)} %get-tuple-element.541), channel_id=1, source_target_pairs={{8,0},{10,2},{16,8},{18,10},{24,16},{26,18},{28,24},{30,26},{20,28... | collective-permute-start | bytes 983048 | tf_op jit(solution)/shard_map/ppermute | solution.py:50
  388.1 21.7 %collective-permute-start.74 = (f32[2,1280]{1,0:T(2,128)S(1)}, f32[2,1280]{1,0:T(2,128)S(1)}, u32[]{:S(2)}, u32[]{:S(2)}) collective-permute-start(f32[2,1280]{1,0:T(2,128)S(1)} %get-tuple-element.586), channel_id=1, source_target_pairs={{2,0},{4,2},{6,4},{8,6},{10,8},{12,10},{14,12},{16,14},{18,16},{20... | collective-permute-start | bytes 30728 | tf_op jit(solution)/shard_map/ppermute | solution.py:255
  389.6 17.6 %collective-permute-start.70 = (bf16[128,2560]{1,0:T(8,128)(2,1)S(1)}, bf16[128,2560]{1,0:T(8,128)(2,1)S(1)}, u32[]{:S(2)}, u32[]{:S(2)}) collective-permute-start(bf16[128,2560]{1,0:T(8,128)(2,1)S(1)} %add_convert_fusion.5), channel_id=1, source_target_pairs={{0,8},{2,10},{8,16},{10,18},{16,24},{18,26},{24,28},{26,30},{28,20... | collective-permute-start | bytes 1966088 | tf_op jit(solution)/shard_map/ppermute | solution.py:47
  414.2 19.0 %collective-permute-start.71 = (bf16[128,2560]{1,0:T(8,128)(2,1)}, bf16[128,2560]{1,0:T(8,128)(2,1)}, u32[]{:S(2)}, u32[]{:S(2)}) collective-permute-start(bf16[128,2560]{1,0:T(8,128)(2,1)} %add_convert_fusion.2), channel_id=1, source_target_pairs={{8,0},{10,2},{16,8},{18,10},{24,16},{26,18},{28,24},{30,26},{20,28... | collective-permute-start | bytes 1966088 | tf_op jit(solution)/shard_map/ppermute | solution.py:50
  416.5 17.9 %collective-permute-start.72 = (bf16[128,2560]{1,0:T(8,128)(2,1)}, bf16[128,2560]{1,0:T(8,128)(2,1)}, u32[]{:S(2)}, u32[]{:S(2)}) collective-permute-start(bf16[128,2560]{1,0:T(8,128)(2,1)} %add_convert_fusion.3), channel_id=1, source_target_pairs={{0,8},{2,10},{8,16},{10,18},{16,24},{18,26},{24,28},{26,30},{28,20... | collective-permute-start | bytes 1966088 | tf_op jit(solution)/shard_map/ppermute | solution.py:47
  445.6 37.2 %collective-permute-start.80 = (bf16[128,2560]{1,0:T(8,128)(2,1)}, bf16[128,2560]{1,0:T(8,128)(2,1)}, u32[]{:S(2)}, u32[]{:S(2)}) collective-permute-start(bf16[128,2560]{1,0:T(8,128)(2,1)} %get-tuple-element.809), channel_id=1, source_target_pairs={{0,1},{1,0},{2,3},{3,2},{4,5},{5,4},{6,7},{7,6},{8,9},{9,8},{10,11... | collective-permute-start | bytes 1966088 | tf_op jit(solution)/shard_map/ppermute | solution.py:249
  452.2 19.8 %collective-permute-start.83 = (bf16[160,2560]{1,0:T(8,128)(2,1)S(1)}, bf16[160,2560]{1,0:T(8,128)(2,1)S(1)}, u32[]{:S(2)}, u32[]{:S(2)}) collective-permute-start(bf16[160,2560]{1,0:T(8,128)(2,1)S(1)} %pad_maximum_fusion.2), channel_id=1, source_target_pairs={{0,8},{2,10},{8,16},{10,18},{16,24},{18,26},{24,28},{26,30},{28,20... | collective-permute-start | bytes 2457608 | tf_op jit(solution)/shard_map/ppermute | solution.py:47
  454.0 20.7 %collective-permute-start.82 = (bf16[160,2560]{1,0:T(8,128)(2,1)S(1)}, bf16[160,2560]{1,0:T(8,128)(2,1)S(1)}, u32[]{:S(2)}, u32[]{:S(2)}) collective-permute-start(bf16[160,2560]{1,0:T(8,128)(2,1)S(1)} %pad_maximum_fusion.3), channel_id=1, source_target_pairs={{8,0},{10,2},{16,8},{18,10},{24,16},{26,18},{28,24},{30,26},{20,28... | collective-permute-start | bytes 2457608 | tf_op jit(solution)/shard_map/ppermute | solution.py:50
  463.2 22.6 %collective-permute-start.87 = (bf16[8,96,2560]{2,1,0:T(8,128)(2,1)}, bf16[8,96,2560]{2,1,0:T(8,128)(2,1)}, u32[]{:S(2)}, u32[]{:S(2)}) collective-permute-start(bf16[8,96,2560]{2,1,0:T(8,128)(2,1)} %get-tuple-element.630), channel_id=1, source_target_pairs={{0,2},{2,0},{4,6},{6,4},{8,10},{10,8},{12,14},{14,12},{16,18},{18,... | collective-permute-start | bytes 11796488 | tf_op jit(solution)/shard_map/ppermute | solution.py:222
  480.6 21.4 %collective-permute-start.85 = (bf16[160,2560]{1,0:T(8,128)(2,1)}, bf16[160,2560]{1,0:T(8,128)(2,1)}, u32[]{:S(2)}, u32[]{:S(2)}) collective-permute-start(bf16[160,2560]{1,0:T(8,128)(2,1)} %fusion.10), channel_id=1, source_target_pairs={{8,0},{10,2},{16,8},{18,10},{24,16},{26,18},{28,24},{30,26},{20,28... | collective-permute-start | bytes 2457608 | tf_op jit(solution)/shard_map/ppermute | solution.py:50
  482.4 21.4 %collective-permute-start.86 = (bf16[160,2560]{1,0:T(8,128)(2,1)}, bf16[160,2560]{1,0:T(8,128)(2,1)}, u32[]{:S(2)}, u32[]{:S(2)}) collective-permute-start(bf16[160,2560]{1,0:T(8,128)(2,1)} %fusion.11), channel_id=1, source_target_pairs={{0,8},{2,10},{8,16},{10,18},{16,24},{18,26},{24,28},{26,30},{28,20... | collective-permute-start | bytes 2457608 | tf_op jit(solution)/shard_map/ppermute | solution.py:47
  487.2 21.8 %collective-permute-start.89 = (bf16[49,2560]{1,0:T(8,128)(2,1)S(1)}, bf16[49,2560]{1,0:T(8,128)(2,1)S(1)}, u32[]{:S(2)}, u32[]{:S(2)}) collective-permute-start(bf16[49,2560]{1,0:T(8,128)(2,1)S(1)} %pad_maximum_fusion.11), channel_id=1, source_target_pairs={{0,8},{2,10},{8,16},{10,18},{16,24},{18,26},{24,28},{26,30},{28,20... | collective-permute-start | bytes 752648 | tf_op jit(solution)/shard_map/ppermute | solution.py:47
  487.5 19.1 %collective-permute-start.88 = (bf16[48,2560]{1,0:T(8,128)(2,1)S(1)}, bf16[48,2560]{1,0:T(8,128)(2,1)S(1)}, u32[]{:S(2)}, u32[]{:S(2)}) collective-permute-start(bf16[48,2560]{1,0:T(8,128)(2,1)S(1)} %slice_bitcast_fusion.7), channel_id=1, source_target_pairs={{8,0},{10,2},{16,8},{18,10},{24,16},{26,18},{28,24},{30,26},{20,28... | collective-permute-start | bytes 737288 | tf_op jit(solution)/shard_map/ppermute | solution.py:50
  511.6 33.4 %collective-permute-start.91 = (bf16[160,2560]{1,0:T(8,128)(2,1)S(1)}, bf16[160,2560]{1,0:T(8,128)(2,1)S(1)}, u32[]{:S(2)}, u32[]{:S(2)}) collective-permute-start(bf16[160,2560]{1,0:T(8,128)(2,1)S(1)} %fusion.9), channel_id=1, source_target_pairs={{0,8},{2,10},{8,16},{10,18},{16,24},{18,26},{24,28},{26,30},{28,20... | collective-permute-start | bytes 2457608 | tf_op jit(solution)/shard_map/ppermute | solution.py:47
  514.3 30.6 %collective-permute-start.90 = (bf16[160,2560]{1,0:T(8,128)(2,1)S(1)}, bf16[160,2560]{1,0:T(8,128)(2,1)S(1)}, u32[]{:S(2)}, u32[]{:S(2)}) collective-permute-start(bf16[160,2560]{1,0:T(8,128)(2,1)S(1)} %fusion.8), channel_id=1, source_target_pairs={{8,0},{10,2},{16,8},{18,10},{24,16},{26,18},{28,24},{30,26},{20,28... | collective-permute-start | bytes 2457608 | tf_op jit(solution)/shard_map/ppermute | solution.py:50
  519.6 23.2 %collective-permute-start.93 = (bf16[97,2560]{1,0:T(8,128)(2,1)}, bf16[97,2560]{1,0:T(8,128)(2,1)}, u32[]{:S(2)}, u32[]{:S(2)}) collective-permute-start(bf16[97,2560]{1,0:T(8,128)(2,1)} %pad_maximum_fusion.10), channel_id=1, source_target_pairs={{0,8},{2,10},{8,16},{10,18},{16,24},{18,26},{24,28},{26,30},{28,20... | collective-permute-start | bytes 1489928 | tf_op jit(solution)/shard_map/ppermute | solution.py:47
  522.2 22.7 %collective-permute-start.92 = (bf16[97,2560]{1,0:T(8,128)(2,1)}, bf16[97,2560]{1,0:T(8,128)(2,1)}, u32[]{:S(2)}, u32[]{:S(2)}) collective-permute-start(bf16[97,2560]{1,0:T(8,128)(2,1)} %fusion.74), channel_id=1, source_target_pairs={{8,0},{10,2},{16,8},{18,10},{24,16},{26,18},{28,24},{30,26},{20,28... | collective-permute-start | bytes 1489928 | tf_op jit(solution)/shard_map/ppermute | solution.py:50
  (152 other events, 1328.7 us)
Sparse Core Ops, SparseCore 0:
  9.6 47.6 all-gather.3
  58.8 39.9 all-gather.5
  122.6 40.0 all-gather.7
  413.2 129.7 reduce-scatter.1
